TPU v7x, 512 devices: a whole 4x4x16 slice. The times are simulated.
512 devices in a mesh: seq: 512 (over y, z, x, core).
Axes of the slice: x: 4, y: 4, z: 16, core: 2. Of those that a mesh axis runs over, the one named last changes fastest.
Arguments:
- query_rows: bfloat16 [65536, 1024], P('seq'), may hold values from -6 to 6
- key_rows: bfloat16 [65536, 1024], P('seq'), may hold values from -6 to 6
- value_rows: bfloat16 [65536, 1024], P('seq'), may hold values from -6 to 6
- attn_out: bfloat16 [65536, 1024], P('seq'), may hold values from -6 to 6
- out_grad: bfloat16 [65536, 1024], P('seq'), may hold values from -6 to 6
- log_norms: float32 [8, 65536], P(None, 'seq'), may hold values from 2.5 to 4.5
Outputs:
- query_grad: bfloat16 [65536, 1024], P('seq')
- key_grad: bfloat16 [65536, 1024], P('seq')
- value_grad: bfloat16 [65536, 1024], P('seq')
All inputs are finite; a program needn't handle non-finite values.
Results may differ from a plain program's by a relative error of at most 0.0049.
Values may be sent and summed in bfloat16 or wider, within the bound.
No kernel may reach another device: no remote copies, remote signals or barrier semaphores. Data moves between devices by JAX's collectives and lax.ppermute only.
A program may use at most 128 MiB of HBM per device.

v0:
```python
import jax
import jax.numpy as jnp
from jax import lax
from jax.sharding import PartitionSpec as P

SPAN_NEAR = 4
SPAN_FAR = 16


def shortened(array):

    def short(part):
        return part.astype(jnp.bfloat16) if part.dtype == jnp.float32 else part

    return jax.tree.map(short, array)


def partner(array, axis, bit):
    return lax.ppermute(array, axis, [(i, i ^ 1 << bit) for i in range(lax.axis_size(axis))])


def head_choice(dilation, heads):
    return jnp.arange(dilation)[:, None] == (jnp.arange(heads) % dilation)[None, :]


def pick_rows(whole, dilation, heads):
    count = whole.shape[0] // dilation
    width = whole.shape[1] // heads
    shaped = whole.reshape(count, dilation, heads, width)
    chosen = head_choice(dilation, heads)
    return jnp.sum(jnp.where(chosen[None, :, :, None], shaped, jnp.zeros((), whole.dtype)), axis=1)


def pick_stats(whole, dilation):
    heads = whole.shape[0]
    count = whole.shape[1] // dilation
    shaped = whole.reshape(heads, count, dilation)
    chosen = head_choice(dilation, heads).T
    picked = jnp.sum(jnp.where(chosen[:, None, :], shaped, jnp.float32(0.0)), axis=-1)
    return picked.T


def spread_rows(values, dilation):
    count, heads, width = values.shape
    chosen = head_choice(dilation, heads)
    placed = jnp.where(chosen[None, :, :, None], values[:, None, :, :], jnp.float32(0.0))
    return placed.reshape(count * dilation, heads * width)


def join_pair(own_part, peer_part, upper_half):
    return jnp.where(upper_half, jnp.stack([peer_part, own_part]), jnp.stack([own_part, peer_part]))


def finish_stack(held, bits):
    return held.reshape((-1,) + held.shape[bits + 2 :])


def collect_group(rows, stats, bits, device_index):
    bit_list = list(range(bits))
    held_rows = [member[None] for member in rows]
    held_stats = [member[None] for member in stats]
    for bit_number in bit_list:
        peer_rows = partner(shortened(tuple(held_rows)), "seq", bit_number)
        peer_stats = partner(tuple(held_stats), "seq", bit_number)
        upper_half = device_index >> bit_number & 1 == 1
        held_rows = [
            join_pair(own_part, peer_part, upper_half)
            for own_part, peer_part in zip(held_rows, peer_rows)
        ]
        held_stats = [
            join_pair(own_part, peer_part, upper_half)
            for own_part, peer_part in zip(held_stats, peer_stats)
        ]
    return (
        [finish_stack(held, bits) for held in held_rows],
        [finish_stack(held, bits) for held in held_stats],
    )


def head_major(rows):
    return jnp.transpose(rows, (1, 0, 2))


def level_terms(query_rows, key_rows, value_rows, out_grad, log_norms, deltas, span, device_index):
    heads = log_norms.shape[0]
    width = query_rows.shape[1] // heads
    dilation = span // 4
    bits = span.bit_length() - 1
    score_scale = width ** (-0.5)
    own_query = pick_rows(query_rows, dilation, heads)
    own_key = pick_rows(key_rows, dilation, heads)
    own_value = pick_rows(value_rows, dilation, heads)
    own_grad = pick_rows(out_grad, dilation, heads)
    own_norms = pick_stats(log_norms, dilation)
    own_deltas = pick_stats(deltas, dilation)
    count = own_query.shape[0]
    gathered_rows, gathered_stats = collect_group(
        (own_key, own_value, own_query, own_grad), (own_norms, own_deltas), bits, device_index
    )
    all_key, all_value, all_query, all_grad = gathered_rows
    selected = all_key.shape[0]
    position = device_index % span
    own_ids = position * count + jnp.arange(count)
    all_ids = jnp.arange(selected)
    causal = own_ids[:, None] >= all_ids[None, :]
    causal_back = all_ids[None, :] >= own_ids[:, None]

    def one_head(pieces):
        (
            query,
            keyown,
            valueown,
            gradown,
            norms,
            dlt,
            keyall,
            valueall,
            queryall,
            gradall,
            normsall,
            dltall,
        ) = pieces
        scores = jnp.dot(query, keyall.T, preferred_element_type=jnp.float32) * score_scale
        probs = jnp.where(causal, jnp.exp(scores - norms[:, None]), jnp.float32(0.0))
        dprobs = jnp.dot(gradown, valueall.T, preferred_element_type=jnp.float32)
        dscores = (probs * (dprobs - dlt[:, None])).astype(jnp.bfloat16)
        grad_query = jnp.dot(dscores, keyall, preferred_element_type=jnp.float32) * score_scale
        scores_back = jnp.dot(keyown, queryall.T, preferred_element_type=jnp.float32) * score_scale
        probs_back = jnp.where(
            causal_back, jnp.exp(scores_back - normsall[None, :]), jnp.float32(0.0)
        )
        dprobs_back = jnp.dot(valueown, gradall.T, preferred_element_type=jnp.float32)
        dscores_back = (probs_back * (dprobs_back - dltall[None, :])).astype(jnp.bfloat16)
        grad_key = jnp.dot(dscores_back, queryall, preferred_element_type=jnp.float32) * score_scale
        grad_value = jnp.dot(
            probs_back.astype(jnp.bfloat16), gradall, preferred_element_type=jnp.float32
        )
        return (grad_query, grad_key, grad_value)

    pieces = (
        head_major(own_query),
        head_major(own_key),
        head_major(own_value),
        head_major(own_grad),
        own_norms.T,
        own_deltas.T,
        head_major(all_key),
        head_major(all_value),
        head_major(all_query),
        head_major(all_grad),
        gathered_stats[0].T,
        gathered_stats[1].T,
    )
    grad_query, grad_key, grad_value = lax.map(one_head, pieces)
    return [
        spread_rows(head_major(grad_query), dilation),
        spread_rows(head_major(grad_key), dilation),
        spread_rows(head_major(grad_value), dilation),
    ]


def body(query_rows, key_rows, value_rows, attn_out, out_grad, log_norms):
    heads = log_norms.shape[0]
    tokens_here = query_rows.shape[0]
    width = query_rows.shape[1] // heads
    device_index = lax.axis_index("seq")
    product = out_grad.astype(jnp.float32) * attn_out.astype(jnp.float32)
    deltas = jnp.sum(product.reshape(tokens_here, heads, width), axis=-1).T
    totals = [jnp.zeros(query_rows.shape, jnp.float32) for _ in range(3)]
    for span in (SPAN_NEAR, SPAN_FAR, lax.axis_size("seq")):
        terms = level_terms(
            query_rows, key_rows, value_rows, out_grad, log_norms, deltas, span, device_index
        )
        totals = [total + term for total, term in zip(totals, terms)]
    return (
        totals[0].astype(jnp.bfloat16),
        totals[1].astype(jnp.bfloat16),
        totals[2].astype(jnp.bfloat16),
    )


def solution(mesh):
    return jax.shard_map(
        body,
        mesh=mesh,
        in_specs=(
            P("seq", None),
            P("seq", None),
            P("seq", None),
            P("seq", None),
            P("seq", None),
            P(None, "seq"),
        ),
        out_specs=(P("seq", None), P("seq", None), P("seq", None)),
        check_vma=False,
    )
```

profile of v0, /device:TPU:26, one launch (start us, length us, event | category | flops | bytes accessed | tf_op | source)
XLA Modules:
  0.0 788.6 jit_solution(16512746668584717970)
XLA Ops:
  41.8 4.0 collective-permute-start.83
  48.8 4.0 collective-permute-start.65
  55.8 3.8 collective-permute-start.84
  61.3 3.8 collective-permute-start.66
  66.8 5.2 collective-permute-start.85
  73.5 4.8 collective-permute-start.67
  86.1 9.1 %collective-permute-start.86 = (f32[2,2,2,2,2,1,1,8]{7,4,3,2,1,0,6,5:T(2,128)S(1)}, f32[2,2,2,2,2,1,1,8]{7,4,3,2,1,0,6,5:T(2,128)S(1)}, u32[]{:S(2)}, u32[]{:S(2)}) collective-permute-start(f32[2,2,2,2,2,1,1,8]{7,4,3,2,1,0,6,5:T(2,128)S(1)} %maximum_select_fusion.109), channel_id=1, source_target_pairs={{0,32},{1,33},{2,34},{3,35},{4,36},{5,37},{6,38},{7,39},{8,40},{9,... | collective-permute-start | bytes 3080 | tf_op jit(solution)/shard_map/ppermute | solution.py:19
  96.9 7.8 collective-permute-start.68
  127.8 14.1 %collective-permute-start.87 = (f32[2,2,2,2,2,2,1,1,8]{8,5,4,3,2,1,0,7,6:T(2,128)S(1)}, f32[2,2,2,2,2,2,1,1,8]{8,5,4,3,2,1,0,7,6:T(2,128)S(1)}, u32[]{:S(2)}, u32[]{:S(2)}) collective-permute-start(f32[2,2,2,2,2,2,1,1,8]{8,5,4,3,2,1,0,7,6:T(2,128)S(1)} %maximum_select_fusion.92), channel_id=1, source_target_pairs={{0,64},{1,65},{2,66},{3,67},{4,68},{5,69},{6,70},{7,71},{8,72},{9,... | collective-permute-start | bytes 6152 | tf_op jit(solution)/shard_map/ppermute | solution.py:19
  143.8 12.6 %collective-permute-start.69 = (f32[2,2,2,2,2,2,1,1,8]{8,5,4,3,2,1,0,7,6:T(2,128)S(1)}, f32[2,2,2,2,2,2,1,1,8]{8,5,4,3,2,1,0,7,6:T(2,128)S(1)}, u32[]{:S(2)}, u32[]{:S(2)}) collective-permute-start(f32[2,2,2,2,2,2,1,1,8]{8,5,4,3,2,1,0,7,6:T(2,128)S(1)} %maximum_select_fusion.88), channel_id=1, source_target_pairs={{0,64},{1,65},{2,66},{3,67},{4,68},{5,69},{6,70},{7,71},{8,72},{9,... | collective-permute-start | bytes 6152 | tf_op jit(solution)/shard_map/ppermute | solution.py:19
  184.9 4.0 collective-permute-start.34
  192.0 4.0 collective-permute-start.26
  222.5 4.0 collective-permute-start.56
  229.5 4.0 collective-permute-start.74
  236.6 4.0 collective-permute-start.38
  243.6 4.0 collective-permute-start.47
  273.9 5.0 collective-permute-done.71
  308.3 3.8 collective-permute-start.76
  315.0 3.8 collective-permute-start.40
  321.7 3.8 collective-permute-start.49
  341.0 7.4 collective-permute-start.59
  348.5 6.8 collective-permute-done.59
  358.7 9.0 %collective-permute-done.77 = bf16[2,2,2,2,2,1,1,8,128]{8,7,4,3,2,1,0,6,5:T(8,128)(2,1)S(1)} collective-permute-done((bf16[2,2,2,2,2,1,1,8,128]{8,7,4,3,2,1,0,6,5:T(8,128)(2,1)S(1)}, bf16[2,2,2,2,2,1,1,8,128]{8,7,4,3,2,1,0,6,5:T(8,128)(2,1)S(1)}, u32[]{:S(2)}, u32[]{:S(2)}) %collective-permute-start.77) | collective-permute-done | bytes 65568 | tf_op jit(solution)/shard_map/ppermute | solution.py:19
  369.7 9.7 %collective-permute-done.41 = bf16[2,2,2,2,2,1,1,8,128]{8,7,4,3,2,1,0,6,5:T(8,128)(2,1)S(1)} collective-permute-done((bf16[2,2,2,2,2,1,1,8,128]{8,7,4,3,2,1,0,6,5:T(8,128)(2,1)S(1)}, bf16[2,2,2,2,2,1,1,8,128]{8,7,4,3,2,1,0,6,5:T(8,128)(2,1)S(1)}, u32[]{:S(2)}, u32[]{:S(2)}) %collective-permute-start.41) | collective-permute-done | bytes 65568 | tf_op jit(solution)/shard_map/ppermute | solution.py:19
  381.3 8.1 %collective-permute-done.50 = bf16[2,2,2,2,2,1,1,8,128]{8,7,4,3,2,1,0,6,5:T(8,128)(2,1)S(1)} collective-permute-done((bf16[2,2,2,2,2,1,1,8,128]{8,7,4,3,2,1,0,6,5:T(8,128)(2,1)S(1)}, bf16[2,2,2,2,2,1,1,8,128]{8,7,4,3,2,1,0,6,5:T(8,128)(2,1)S(1)}, u32[]{:S(2)}, u32[]{:S(2)}) %collective-permute-start.50) | collective-permute-done | bytes 65568 | tf_op jit(solution)/shard_map/ppermute | solution.py:19
  391.9 5.5 collective-permute-done.29
  399.9 4.9 collective-permute-done.21
  407.3 4.3 collective-permute-done.17
  414.2 4.3 collective-permute-done.13
  418.5 12.0 %collective-permute-start.60 = (bf16[2,2,2,2,2,2,1,1,8,128]{9,8,5,4,3,2,1,0,7,6:T(8,128)(2,1)S(1)}, bf16[2,2,2,2,2,2,1,1,8,128]{9,8,5,4,3,2,1,0,7,6:T(8,128)(2,1)S(1)}, u32[]{:S(2)}, u32[]{:S(2)}) collective-permute-start(bf16[2,2,2,2,2,2,1,1,8,128]{9,8,5,4,3,2,1,0,7,6:T(8,128)(2,1)S(1)} %maximum_select_fusion.56), channel_id=1, source_target_pairs={{0,64},{1,65},{2,66},{3,67},{4,68},{5,69},{6,70},{7,71},{8,72},{9,... | collective-permute-start | bytes 393224 | tf_op jit(solution)/shard_map/ppermute | solution.py:19
  430.6 5.4 collective-permute-done.60
  436.0 10.1 %collective-permute-start.78 = (bf16[2,2,2,2,2,2,1,1,8,128]{9,8,5,4,3,2,1,0,7,6:T(8,128)(2,1)S(1)}, bf16[2,2,2,2,2,2,1,1,8,128]{9,8,5,4,3,2,1,0,7,6:T(8,128)(2,1)S(1)}, u32[]{:S(2)}, u32[]{:S(2)}) collective-permute-start(bf16[2,2,2,2,2,2,1,1,8,128]{9,8,5,4,3,2,1,0,7,6:T(8,128)(2,1)S(1)} %maximum_select_fusion.60), channel_id=1, source_target_pairs={{0,64},{1,65},{2,66},{3,67},{4,68},{5,69},{6,70},{7,71},{8,72},{9,... | collective-permute-start | bytes 393224 | tf_op jit(solution)/shard_map/ppermute | solution.py:19
  446.2 5.7 collective-permute-done.78
  451.9 12.1 %collective-permute-start.42 = (bf16[2,2,2,2,2,2,1,1,8,128]{9,8,5,4,3,2,1,0,7,6:T(8,128)(2,1)S(1)}, bf16[2,2,2,2,2,2,1,1,8,128]{9,8,5,4,3,2,1,0,7,6:T(8,128)(2,1)S(1)}, u32[]{:S(2)}, u32[]{:S(2)}) collective-permute-start(bf16[2,2,2,2,2,2,1,1,8,128]{9,8,5,4,3,2,1,0,7,6:T(8,128)(2,1)S(1)} %maximum_select_fusion.52), channel_id=1, source_target_pairs={{0,64},{1,65},{2,66},{3,67},{4,68},{5,69},{6,70},{7,71},{8,72},{9,... | collective-permute-start | bytes 393224 | tf_op jit(solution)/shard_map/ppermute | solution.py:19
  464.0 4.6 collective-permute-done.42
  468.6 11.2 %collective-permute-start.51 = (bf16[2,2,2,2,2,2,1,1,8,128]{9,8,5,4,3,2,1,0,7,6:T(8,128)(2,1)S(1)}, bf16[2,2,2,2,2,2,1,1,8,128]{9,8,5,4,3,2,1,0,7,6:T(8,128)(2,1)S(1)}, u32[]{:S(2)}, u32[]{:S(2)}) collective-permute-start(bf16[2,2,2,2,2,2,1,1,8,128]{9,8,5,4,3,2,1,0,7,6:T(8,128)(2,1)S(1)} %maximum_select_fusion.54), channel_id=1, source_target_pairs={{0,64},{1,65},{2,66},{3,67},{4,68},{5,69},{6,70},{7,71},{8,72},{9,... | collective-permute-start | bytes 393224 | tf_op jit(solution)/shard_map/ppermute | solution.py:19
  479.9 7.2 collective-permute-done.51
  489.4 5.2 collective-permute-start.22
  497.0 5.2 collective-permute-start.14
  523.2 9.8 %collective-permute-start.3 = (bf16[2,1,128,8,128]{4,2,3,0,1:T(8,128)(2,1)S(1)}, bf16[2,1,128,8,128]{4,2,3,0,1:T(8,128)(2,1)S(1)}, u32[]{:S(2)}, u32[]{:S(2)}) collective-permute-start(bf16[2,1,128,8,128]{4,2,3,0,1:T(8,128)(2,1)S(1)} %bitcast_select_fusion.3), channel_id=1, source_target_pairs={{0,2},{1,3},{2,0},{3,1},{4,6},{5,7},{6,4},{7,5},{8,10},{9,11},{10,... | collective-permute-start | bytes 1572872 | tf_op jit(solution)/shard_map/ppermute | solution.py:19
  538.5 3.9 collective-permute-start.5
  551.6 3.9 collective-permute-start.23
  560.2 4.5 collective-permute-done.5
  574.2 64.9 %while.48 = (s32[]{:T(128)}, f32[8,128,128]{2,1,0:T(8,128)}, f32[8,128,128]{2,1,0:T(8,128)}, f32[8,128,128]{2,1,0:T(8,128)}, bf16[8,128,128]{1,2,0:T(8,128)(2,1)...) while((s32[]{:T(128)}, f32[8,128,128]{2,1,0:T(8,128)}, ...), condition=%wide.region_2.3_spmd.clone.clone, body=%wide.region_1.2_spmd.clone.clone.sunk | while | flops 118456320 | bytes 2579629 | solution.py:154
  639.1 4.2 collective-permute-start.80
  649.7 4.2 collective-permute-start.53
  658.7 66.7 %while.49 = (s32[]{:T(128)}, f32[8,32,128]{2,1,0:T(8,128)}, f32[8,32,128]{2,1,0:T(8,128)}, f32[8,32,128]{2,1,0:T(8,128)}, bf16[8,32,128]{2,1,0:T(8,128)(2,1)S(1)...) while((s32[]{:T(128)}, f32[8,32,128]{2,1,0:T(8,128)}, ...), condition=%wide.region_10.11_spmd.clone.clone, body=%wide.region_9.10_spmd.clone.clone.sunk | while | flops 29614080 | bytes 1349841 | solution.py:154
  738.0 47.4 %while.50 = (s32[]{:T(128)}, f32[8,1,128]{2,1,0:T(1,128)S(1)}, f32[8,1,128]{2,1,0:T(1,128)S(1)}, f32[8,1,128]{2,1,0:T(1,128)S(1)}, bf16[8,1,128]{2,0,1:T(8,128)(...) while((s32[]{:T(128)}, f32[8,1,128]{2,1,0:T(1,128)S(1)}, ...), condition=%wide.region_18.19_spmd.clone.clone, body=%wide.region_17.18_spmd.clone.clone.sunk | while | flops 926978 | bytes 961221 | solution.py:154
  (674 shorter events, 506.0 us)
Async XLA Ops:
  2.8 25.7 %collective-permute-start.81 = (f32[1,1,8]{2,1,0:T(1,128)S(1)}, f32[1,1,8]{2,1,0:T(1,128)S(1)}, u32[]{:S(2)}, u32[]{:S(2)}) collective-permute-start(f32[1,1,8]{2,1,0:T(1,128)S(1)} %bitcast.1292), channel_id=1, source_target_pairs={{0,1},{1,0},{2,3},{3,2},{4,5},{5,4},{6,7},{7,6},{8,9},{9,8},{10,11... | collective-permute-start | bytes 104 | tf_op jit(solution)/shard_map/ppermute | solution.py:19
  4.9 26.0 %collective-permute-start.63 = (f32[1,1,8]{2,1,0:T(1,128)S(1)}, f32[1,1,8]{2,1,0:T(1,128)S(1)}, u32[]{:S(2)}, u32[]{:S(2)}) collective-permute-start(f32[1,1,8]{2,1,0:T(1,128)S(1)} %bitcast.1296), channel_id=1, source_target_pairs={{0,1},{1,0},{2,3},{3,2},{4,5},{5,4},{6,7},{7,6},{8,9},{9,8},{10,11... | collective-permute-start | bytes 104 | tf_op jit(solution)/shard_map/ppermute | solution.py:19
  7.9 100.5 %collective-permute-start.54 = (bf16[1,1,8,128]{3,2,1,0:T(8,128)(2,1)S(1)}, bf16[1,1,8,128]{3,2,1,0:T(8,128)(2,1)S(1)}, u32[]{:S(2)}, u32[]{:S(2)}) collective-permute-start(bf16[1,1,8,128]{3,2,1,0:T(8,128)(2,1)S(1)} %bitcast.1288), channel_id=1, source_target_pairs={{0,1},{1,0},{2,3},{3,2},{4,5},{5,4},{6,7},{7,6},{8,9},{9,8},{10,11... | collective-permute-start | bytes 6152 | tf_op jit(solution)/shard_map/ppermute | solution.py:19
  9.8 101.0 %collective-permute-start.72 = (bf16[1,1,8,128]{3,2,1,0:T(8,128)(2,1)S(1)}, bf16[1,1,8,128]{3,2,1,0:T(8,128)(2,1)}, u32[]{:S(2)}, u32[]{:S(2)}) collective-permute-start(bf16[1,1,8,128]{3,2,1,0:T(8,128)(2,1)S(1)} %bitcast.1280), channel_id=1, source_target_pairs={{0,1},{1,0},{2,3},{3,2},{4,5},{5,4},{6,7},{7,6},{8,9},{9,8},{10,11... | collective-permute-start | bytes 6152 | tf_op jit(solution)/shard_map/ppermute | solution.py:19
  12.2 101.3 %collective-permute-start.36 = (bf16[1,1,8,128]{3,2,1,0:T(8,128)(2,1)S(1)}, bf16[1,1,8,128]{3,2,1,0:T(8,128)(2,1)}, u32[]{:S(2)}, u32[]{:S(2)}) collective-permute-start(bf16[1,1,8,128]{3,2,1,0:T(8,128)(2,1)S(1)} %bitcast.1284), channel_id=1, source_target_pairs={{0,1},{1,0},{2,3},{3,2},{4,5},{5,4},{6,7},{7,6},{8,9},{9,8},{10,11... | collective-permute-start | bytes 6152 | tf_op jit(solution)/shard_map/ppermute | solution.py:19
  28.5 88.2 %collective-permute-start.45 = (bf16[1,1,8,128]{3,2,1,0:T(8,128)(2,1)S(1)}, bf16[1,1,8,128]{3,2,1,0:T(8,128)(2,1)S(1)}, u32[]{:S(2)}, u32[]{:S(2)}) collective-permute-start(bf16[1,1,8,128]{3,2,1,0:T(8,128)(2,1)S(1)} %bitcast.1276), channel_id=1, source_target_pairs={{0,1},{1,0},{2,3},{3,2},{4,5},{5,4},{6,7},{7,6},{8,9},{9,8},{10,11... | collective-permute-start | bytes 6152 | tf_op jit(solution)/shard_map/ppermute | solution.py:19
  86.1 10.8 %collective-permute-start.86 = (f32[2,2,2,2,2,1,1,8]{7,4,3,2,1,0,6,5:T(2,128)S(1)}, f32[2,2,2,2,2,1,1,8]{7,4,3,2,1,0,6,5:T(2,128)S(1)}, u32[]{:S(2)}, u32[]{:S(2)}) collective-permute-start(f32[2,2,2,2,2,1,1,8]{7,4,3,2,1,0,6,5:T(2,128)S(1)} %maximum_select_fusion.109), channel_id=1, source_target_pairs={{0,32},{1,33},{2,34},{3,35},{4,36},{5,37},{6,38},{7,39},{8,40},{9,... | collective-permute-start | bytes 3080 | tf_op jit(solution)/shard_map/ppermute | solution.py:19
  96.9 9.5 %collective-permute-start.68 = (f32[2,2,2,2,2,1,1,8]{7,4,3,2,1,6,5,0:T(2,128)S(1)}, f32[2,2,2,2,2,1,1,8]{7,4,3,2,1,6,5,0:T(2,128)S(1)}, u32[]{:S(2)}, u32[]{:S(2)}) collective-permute-start(f32[2,2,2,2,2,1,1,8]{7,4,3,2,1,6,5,0:T(2,128)S(1)} %bitcast_select_fusion.8), channel_id=1, source_target_pairs={{0,32},{1,33},{2,34},{3,35},{4,36},{5,37},{6,38},{7,39},{8,40},{9,... | collective-permute-start | bytes 3080 | tf_op jit(solution)/shard_map/ppermute | solution.py:19
  106.4 53.9 %collective-permute-start.10 = (f32[1,128,8]{2,1,0:T(8,128)S(1)}, f32[1,128,8]{2,1,0:T(8,128)S(1)}, u32[]{:S(2)}, u32[]{:S(2)}) collective-permute-start(f32[1,128,8]{2,1,0:T(8,128)S(1)} %bitcast.1129), channel_id=1, source_target_pairs={{0,1},{1,0},{2,3},{3,2},{4,5},{5,4},{6,7},{7,6},{8,9},{9,8},{10,11... | collective-permute-start | bytes 12296 | tf_op jit(solution)/shard_map/ppermute | solution.py:19
  108.4 54.4 %collective-permute-start.6 = (f32[1,128,8]{1,2,0:T(8,128)S(1)}, f32[1,128,8]{1,2,0:T(8,128)S(1)}, u32[]{:S(2)}, u32[]{:S(2)}) collective-permute-start(f32[1,128,8]{1,2,0:T(8,128)S(1)} %bitcast.1267), channel_id=1, source_target_pairs={{0,1},{1,0},{2,3},{3,2},{4,5},{5,4},{6,7},{7,6},{8,9},{9,8},{10,11... | collective-permute-start | bytes 12296 | tf_op jit(solution)/shard_map/ppermute | solution.py:19
  110.9 378.5 %collective-permute-start.2 = (bf16[1,128,8,128]{3,1,2,0:T(8,128)(2,1)}, bf16[1,128,8,128]{3,1,2,0:T(8,128)(2,1)S(1)}, u32[]{:S(2)}, u32[]{:S(2)}) collective-permute-start(bf16[1,128,8,128]{3,1,2,0:T(8,128)(2,1)} %copy.500), channel_id=1, source_target_pairs={{0,1},{1,0},{2,3},{3,2},{4,5},{5,4},{6,7},{7,6},{8,9},{9,8},{10,11... | collective-permute-start | bytes 786440 | tf_op jit(solution)/shard_map/ppermute | solution.py:19
  113.6 381.2 %collective-permute-start = (bf16[1,128,8,128]{3,1,2,0:T(8,128)(2,1)}, bf16[1,128,8,128]{3,1,2,0:T(8,128)(2,1)S(1)}, u32[]{:S(2)}, u32[]{:S(2)}) collective-permute-start(bf16[1,128,8,128]{3,1,2,0:T(8,128)(2,1)} %copy.493), channel_id=1, source_target_pairs={{0,1},{1,0},{2,3},{3,2},{4,5},{5,4},{6,7},{7,6},{8,9},{9,8},{10,11... | collective-permute-start | bytes 786440 | tf_op jit(solution)/shard_map/ppermute | solution.py:19
  127.8 16.0 %collective-permute-start.87 = (f32[2,2,2,2,2,2,1,1,8]{8,5,4,3,2,1,0,7,6:T(2,128)S(1)}, f32[2,2,2,2,2,2,1,1,8]{8,5,4,3,2,1,0,7,6:T(2,128)S(1)}, u32[]{:S(2)}, u32[]{:S(2)}) collective-permute-start(f32[2,2,2,2,2,2,1,1,8]{8,5,4,3,2,1,0,7,6:T(2,128)S(1)} %maximum_select_fusion.92), channel_id=1, source_target_pairs={{0,64},{1,65},{2,66},{3,67},{4,68},{5,69},{6,70},{7,71},{8,72},{9,... | collective-permute-start | bytes 6152 | tf_op jit(solution)/shard_map/ppermute | solution.py:19
  143.8 14.5 %collective-permute-start.69 = (f32[2,2,2,2,2,2,1,1,8]{8,5,4,3,2,1,0,7,6:T(2,128)S(1)}, f32[2,2,2,2,2,2,1,1,8]{8,5,4,3,2,1,0,7,6:T(2,128)S(1)}, u32[]{:S(2)}, u32[]{:S(2)}) collective-permute-start(f32[2,2,2,2,2,2,1,1,8]{8,5,4,3,2,1,0,7,6:T(2,128)S(1)} %maximum_select_fusion.88), channel_id=1, source_target_pairs={{0,64},{1,65},{2,66},{3,67},{4,68},{5,69},{6,70},{7,71},{8,72},{9,... | collective-permute-start | bytes 6152 | tf_op jit(solution)/shard_map/ppermute | solution.py:19
  158.3 338.7 %collective-permute-start.4 = (bf16[1,128,8,128]{3,1,2,0:T(8,128)(2,1)}, bf16[1,128,8,128]{3,1,2,0:T(8,128)(2,1)}, u32[]{:S(2)}, u32[]{:S(2)}) collective-permute-start(bf16[1,128,8,128]{3,1,2,0:T(8,128)(2,1)} %copy.510), channel_id=1, source_target_pairs={{0,1},{1,0},{2,3},{3,2},{4,5},{5,4},{6,7},{7,6},{8,9},{9,8},{10,11... | collective-permute-start | bytes 786440 | tf_op jit(solution)/shard_map/ppermute | solution.py:19
  160.3 344.1 %collective-permute-start.8 = (bf16[1,128,8,128]{3,1,2,0:T(8,128)(2,1)}, bf16[1,128,8,128]{3,1,2,0:T(8,128)(2,1)}, u32[]{:S(2)}, u32[]{:S(2)}) collective-permute-start(bf16[1,128,8,128]{3,1,2,0:T(8,128)(2,1)} %copy.519), channel_id=1, source_target_pairs={{0,1},{1,0},{2,3},{3,2},{4,5},{5,4},{6,7},{7,6},{8,9},{9,8},{10,11... | collective-permute-start | bytes 786440 | tf_op jit(solution)/shard_map/ppermute | solution.py:19
  262.2 8.4 %collective-permute-start.89 = (f32[2,2,2,2,2,2,2,2,1,1,8]{10,7,6,5,4,3,2,1,0,9,8:T(2,128)S(1)}, f32[2,2,2,2,2,2,2,2,1,1,8]{10,7,6,5,4,3,2,1,0,9,8:T(2,128)S(1)}, u32[]{:S(2)}, u32[]{:S(2)}) collective-permute-start(f32[2,2,2,2,2,2,2,2,1,1,8]{10,7,6,5,4,3,2,1,0,9,8:T(2,128)S(1)} %maximum_select_fusion.62), channel_id=1, source_target_pairs={{0,256},{1,257},{2,258},{3,259},{4,260},{5,261},{6,262},{7,263},{8... | collective-permute-start | bytes 24584 | tf_op jit(solution)/shard_map/ppermute | solution.py:19
  270.6 8.4 %collective-permute-start.71 = (f32[2,2,2,2,2,2,2,2,1,1,8]{10,7,6,5,4,3,2,1,0,9,8:T(2,128)S(1)}, f32[2,2,2,2,2,2,2,2,1,1,8]{10,7,6,5,4,3,2,1,0,9,8:T(2,128)S(1)}, u32[]{:S(2)}, u32[]{:S(2)}) collective-permute-start(f32[2,2,2,2,2,2,2,2,1,1,8]{10,7,6,5,4,3,2,1,0,9,8:T(2,128)S(1)} %maximum_select_fusion.58), channel_id=1, source_target_pairs={{0,256},{1,257},{2,258},{3,259},{4,260},{5,261},{6,262},{7,263},{8... | collective-permute-start | bytes 24584 | tf_op jit(solution)/shard_map/ppermute | solution.py:19
  341.0 14.3 %collective-permute-start.59 = (bf16[2,2,2,2,2,1,1,8,128]{8,7,4,3,2,1,0,6,5:T(8,128)(2,1)S(1)}, bf16[2,2,2,2,2,1,1,8,128]{8,7,4,3,2,1,0,6,5:T(8,128)(2,1)S(1)}, u32[]{:S(2)}, u32[]{:S(2)}) collective-permute-start(bf16[2,2,2,2,2,1,1,8,128]{8,7,4,3,2,1,0,6,5:T(8,128)(2,1)S(1)} %maximum_select_fusion.70), channel_id=1, source_target_pairs={{0,32},{1,33},{2,34},{3,35},{4,36},{5,37},{6,38},{7,39},{8,40},{9,... | collective-permute-start | bytes 196616 | tf_op jit(solution)/shard_map/ppermute | solution.py:19
  355.2 12.5 %collective-permute-start.77 = (bf16[2,2,2,2,2,1,1,8,128]{8,7,4,3,2,1,0,6,5:T(8,128)(2,1)S(1)}, bf16[2,2,2,2,2,1,1,8,128]{8,7,4,3,2,1,0,6,5:T(8,128)(2,1)S(1)}, u32[]{:S(2)}, u32[]{:S(2)}) collective-permute-start(bf16[2,2,2,2,2,1,1,8,128]{8,7,4,3,2,1,0,6,5:T(8,128)(2,1)S(1)} %maximum_select_fusion.74), channel_id=1, source_target_pairs={{0,32},{1,33},{2,34},{3,35},{4,36},{5,37},{6,38},{7,39},{8,40},{9,... | collective-permute-start | bytes 196616 | tf_op jit(solution)/shard_map/ppermute | solution.py:19
  367.7 11.6 %collective-permute-start.41 = (bf16[2,2,2,2,2,1,1,8,128]{8,7,4,3,2,1,0,6,5:T(8,128)(2,1)S(1)}, bf16[2,2,2,2,2,1,1,8,128]{8,7,4,3,2,1,0,6,5:T(8,128)(2,1)S(1)}, u32[]{:S(2)}, u32[]{:S(2)}) collective-permute-start(bf16[2,2,2,2,2,1,1,8,128]{8,7,4,3,2,1,0,6,5:T(8,128)(2,1)S(1)} %maximum_select_fusion.66), channel_id=1, source_target_pairs={{0,32},{1,33},{2,34},{3,35},{4,36},{5,37},{6,38},{7,39},{8,40},{9,... | collective-permute-start | bytes 196616 | tf_op jit(solution)/shard_map/ppermute | solution.py:19
  379.3 10.1 %collective-permute-start.50 = (bf16[2,2,2,2,2,1,1,8,128]{8,7,4,3,2,1,0,6,5:T(8,128)(2,1)S(1)}, bf16[2,2,2,2,2,1,1,8,128]{8,7,4,3,2,1,0,6,5:T(8,128)(2,1)S(1)}, u32[]{:S(2)}, u32[]{:S(2)}) collective-permute-start(bf16[2,2,2,2,2,1,1,8,128]{8,7,4,3,2,1,0,6,5:T(8,128)(2,1)S(1)} %maximum_select_fusion.68), channel_id=1, source_target_pairs={{0,32},{1,33},{2,34},{3,35},{4,36},{5,37},{6,38},{7,39},{8,40},{9,... | collective-permute-start | bytes 196616 | tf_op jit(solution)/shard_map/ppermute | solution.py:19
  389.4 8.0 %collective-permute-start.29 = (bf16[2,1,32,8,128]{4,3,2,0,1:T(8,128)(2,1)S(1)}, bf16[2,1,32,8,128]{4,3,2,0,1:T(8,128)(2,1)S(1)}, u32[]{:S(2)}, u32[]{:S(2)}) collective-permute-start(bf16[2,1,32,8,128]{4,3,2,0,1:T(8,128)(2,1)S(1)} %fusion.200), channel_id=1, source_target_pairs={{0,2},{1,3},{2,0},{3,1},{4,6},{5,7},{6,4},{7,5},{8,10},{9,11},{10,... | collective-permute-start | bytes 393224 | tf_op jit(solution)/shard_map/ppermute | solution.py:19
  397.4 7.4 collective-permute-start.21
  418.5 17.5 %collective-permute-start.60 = (bf16[2,2,2,2,2,2,1,1,8,128]{9,8,5,4,3,2,1,0,7,6:T(8,128)(2,1)S(1)}, bf16[2,2,2,2,2,2,1,1,8,128]{9,8,5,4,3,2,1,0,7,6:T(8,128)(2,1)S(1)}, u32[]{:S(2)}, u32[]{:S(2)}) collective-permute-start(bf16[2,2,2,2,2,2,1,1,8,128]{9,8,5,4,3,2,1,0,7,6:T(8,128)(2,1)S(1)} %maximum_select_fusion.56), channel_id=1, source_target_pairs={{0,64},{1,65},{2,66},{3,67},{4,68},{5,69},{6,70},{7,71},{8,72},{9,... | collective-permute-start | bytes 393224 | tf_op jit(solution)/shard_map/ppermute | solution.py:19
  436.0 15.9 %collective-permute-start.78 = (bf16[2,2,2,2,2,2,1,1,8,128]{9,8,5,4,3,2,1,0,7,6:T(8,128)(2,1)S(1)}, bf16[2,2,2,2,2,2,1,1,8,128]{9,8,5,4,3,2,1,0,7,6:T(8,128)(2,1)S(1)}, u32[]{:S(2)}, u32[]{:S(2)}) collective-permute-start(bf16[2,2,2,2,2,2,1,1,8,128]{9,8,5,4,3,2,1,0,7,6:T(8,128)(2,1)S(1)} %maximum_select_fusion.60), channel_id=1, source_target_pairs={{0,64},{1,65},{2,66},{3,67},{4,68},{5,69},{6,70},{7,71},{8,72},{9,... | collective-permute-start | bytes 393224 | tf_op jit(solution)/shard_map/ppermute | solution.py:19
  451.9 16.8 %collective-permute-start.42 = (bf16[2,2,2,2,2,2,1,1,8,128]{9,8,5,4,3,2,1,0,7,6:T(8,128)(2,1)S(1)}, bf16[2,2,2,2,2,2,1,1,8,128]{9,8,5,4,3,2,1,0,7,6:T(8,128)(2,1)S(1)}, u32[]{:S(2)}, u32[]{:S(2)}) collective-permute-start(bf16[2,2,2,2,2,2,1,1,8,128]{9,8,5,4,3,2,1,0,7,6:T(8,128)(2,1)S(1)} %maximum_select_fusion.52), channel_id=1, source_target_pairs={{0,64},{1,65},{2,66},{3,67},{4,68},{5,69},{6,70},{7,71},{8,72},{9,... | collective-permute-start | bytes 393224 | tf_op jit(solution)/shard_map/ppermute | solution.py:19
  468.6 18.5 %collective-permute-start.51 = (bf16[2,2,2,2,2,2,1,1,8,128]{9,8,5,4,3,2,1,0,7,6:T(8,128)(2,1)S(1)}, bf16[2,2,2,2,2,2,1,1,8,128]{9,8,5,4,3,2,1,0,7,6:T(8,128)(2,1)S(1)}, u32[]{:S(2)}, u32[]{:S(2)}) collective-permute-start(bf16[2,2,2,2,2,2,1,1,8,128]{9,8,5,4,3,2,1,0,7,6:T(8,128)(2,1)S(1)} %maximum_select_fusion.54), channel_id=1, source_target_pairs={{0,64},{1,65},{2,66},{3,67},{4,68},{5,69},{6,70},{7,71},{8,72},{9,... | collective-permute-start | bytes 393224 | tf_op jit(solution)/shard_map/ppermute | solution.py:19
  487.2 22.5 %collective-permute-start.30 = (bf16[2,2,1,32,8,128]{5,4,3,1,0,2:T(8,128)(2,1)S(1)}, bf16[2,2,1,32,8,128]{5,4,3,1,0,2:T(8,128)(2,1)S(1)}, u32[]{:S(2)}, u32[]{:S(2)}) collective-permute-start(bf16[2,2,1,32,8,128]{5,4,3,1,0,2:T(8,128)(2,1)S(1)} %maximum_select_fusion.36), channel_id=1, source_target_pairs={{0,4},{1,5},{2,6},{3,7},{4,0},{5,1},{6,2},{7,3},{8,12},{9,13},{10,... | collective-permute-start | bytes 786440 | tf_op jit(solution)/shard_map/ppermute | solution.py:19
  489.4 24.4 %collective-permute-start.22 = (bf16[2,2,1,32,8,128]{5,4,3,1,0,2:T(8,128)(2,1)S(1)}, bf16[2,2,1,32,8,128]{5,4,3,1,0,2:T(8,128)(2,1)S(1)}, u32[]{:S(2)}, u32[]{:S(2)}) collective-permute-start(bf16[2,2,1,32,8,128]{5,4,3,1,0,2:T(8,128)(2,1)S(1)} %maximum_select_fusion.34), channel_id=1, source_target_pairs={{0,4},{1,5},{2,6},{3,7},{4,0},{5,1},{6,2},{7,3},{8,12},{9,13},{10,... | collective-permute-start | bytes 786440 | tf_op jit(solution)/shard_map/ppermute | solution.py:19
  494.7 23.5 %collective-permute-start.18 = (bf16[2,2,1,32,8,128]{5,4,3,1,0,2:T(8,128)(2,1)S(1)}, bf16[2,2,1,32,8,128]{5,4,3,1,0,2:T(8,128)(2,1)S(1)}, u32[]{:S(2)}, u32[]{:S(2)}) collective-permute-start(bf16[2,2,1,32,8,128]{5,4,3,1,0,2:T(8,128)(2,1)S(1)} %fusion.196), channel_id=1, source_target_pairs={{0,4},{1,5},{2,6},{3,7},{4,0},{5,1},{6,2},{7,3},{8,12},{9,13},{10,... | collective-permute-start | bytes 786440 | tf_op jit(solution)/shard_map/ppermute | solution.py:19
  497.0 26.2 %collective-permute-start.14 = (bf16[2,2,1,32,8,128]{5,4,3,1,0,2:T(8,128)(2,1)S(1)}, bf16[2,2,1,32,8,128]{5,4,3,1,0,2:T(8,128)(2,1)S(1)}, u32[]{:S(2)}, u32[]{:S(2)}) collective-permute-start(bf16[2,2,1,32,8,128]{5,4,3,1,0,2:T(8,128)(2,1)S(1)} %maximum_select_fusion.31), channel_id=1, source_target_pairs={{0,4},{1,5},{2,6},{3,7},{4,0},{5,1},{6,2},{7,3},{8,12},{9,13},{10,... | collective-permute-start | bytes 786440 | tf_op jit(solution)/shard_map/ppermute | solution.py:19
  504.5 30.3 %collective-permute-start.61 = (bf16[2,2,2,2,2,2,2,1,1,8,128]{10,9,6,5,4,3,2,1,0,8,7:T(8,128)(2,1)S(1)}, bf16[2,2,2,2,2,2,2,1,1,8,128]{10,9,6,5,4,3,2,1,0,8,7:T(8,128)(2,1)S(1)}, u32[]{:S(2)}, u32[]{:S(2)}) collective-permute-start(bf16[2,2,2,2,2,2,2,1,1,8,128]{10,9,6,5,4,3,2,1,0,8,7:T(8,128)(2,1)S(1)} %maxim, ...), channel_id=1, source_target_pairs={{0,128},{1,129},{2,130},{3,131},{4,132},{5,133},{6,134},{7,135},{8... | collective-permute-start | bytes 786440 | tf_op jit(solution)/shard_map/ppermute | solution.py:19
  509.7 28.9 %collective-permute-start.79 = (bf16[2,2,2,2,2,2,2,1,1,8,128]{10,9,6,5,4,3,2,1,0,8,7:T(8,128)(2,1)S(1)}, bf16[2,2,2,2,2,2,2,1,1,8,128]{10,9,6,5,4,3,2,1,0,8,7:T(8,128)(2,1)S(1)}, u32[]{:S(2)}, u32[]{:S(2)}) collective-permute-start(bf16[2,2,2,2,2,2,2,1,1,8,128]{10,9,6,5,4,3,2,1,0,8,7:T(8,128)(2,1)S(1)} %maxim, ...), channel_id=1, source_target_pairs={{0,128},{1,129},{2,130},{3,131},{4,132},{5,133},{6,134},{7,135},{8... | collective-permute-start | bytes 786440 | tf_op jit(solution)/shard_map/ppermute | solution.py:19
  513.8 30.4 %collective-permute-start.43 = (bf16[2,2,2,2,2,2,2,1,1,8,128]{10,9,6,5,4,3,2,1,0,8,7:T(8,128)(2,1)S(1)}, bf16[2,2,2,2,2,2,2,1,1,8,128]{10,9,6,5,4,3,2,1,0,8,7:T(8,128)(2,1)S(1)}, u32[]{:S(2)}, u32[]{:S(2)}) collective-permute-start(bf16[2,2,2,2,2,2,2,1,1,8,128]{10,9,6,5,4,3,2,1,0,8,7:T(8,128)(2,1)S(1)} %maxim, ...), channel_id=1, source_target_pairs={{0,128},{1,129},{2,130},{3,131},{4,132},{5,133},{6,134},{7,135},{8... | collective-permute-start | bytes 786440 | tf_op jit(solution)/shard_map/ppermute | solution.py:19
  518.3 29.6 %collective-permute-start.52 = (bf16[2,2,2,2,2,2,2,1,1,8,128]{10,9,6,5,4,3,2,1,0,8,7:T(8,128)(2,1)S(1)}, bf16[2,2,2,2,2,2,2,1,1,8,128]{10,9,6,5,4,3,2,1,0,8,7:T(8,128)(2,1)S(1)}, u32[]{:S(2)}, u32[]{:S(2)}) collective-permute-start(bf16[2,2,2,2,2,2,2,1,1,8,128]{10,9,6,5,4,3,2,1,0,8,7:T(8,128)(2,1)S(1)} %maxim, ...), channel_id=1, source_target_pairs={{0,128},{1,129},{2,130},{3,131},{4,132},{5,133},{6,134},{7,135},{8... | collective-permute-start | bytes 786440 | tf_op jit(solution)/shard_map/ppermute | solution.py:19
  523.2 28.4 %collective-permute-start.3 = (bf16[2,1,128,8,128]{4,2,3,0,1:T(8,128)(2,1)S(1)}, bf16[2,1,128,8,128]{4,2,3,0,1:T(8,128)(2,1)S(1)}, u32[]{:S(2)}, u32[]{:S(2)}) collective-permute-start(bf16[2,1,128,8,128]{4,2,3,0,1:T(8,128)(2,1)S(1)} %bitcast_select_fusion.3), channel_id=1, source_target_pairs={{0,2},{1,3},{2,0},{3,1},{4,6},{5,7},{6,4},{7,5},{8,10},{9,11},{10,... | collective-permute-start | bytes 1572872 | tf_op jit(solution)/shard_map/ppermute | solution.py:19
  534.8 22.3 %collective-permute-start.1 = (bf16[2,1,128,8,128]{4,2,3,1,0:T(8,128)(2,1)S(1)}, bf16[2,1,128,8,128]{4,2,3,1,0:T(8,128)(2,1)S(1)}, u32[]{:S(2)}, u32[]{:S(2)}) collective-permute-start(bf16[2,1,128,8,128]{4,2,3,1,0:T(8,128)(2,1)S(1)} %maximum_select_fusion.11), channel_id=1, source_target_pairs={{0,2},{1,3},{2,0},{3,1},{4,6},{5,7},{6,4},{7,5},{8,10},{9,11},{10,... | collective-permute-start | bytes 1572872 | tf_op jit(solution)/shard_map/ppermute | solution.py:19
  538.5 26.1 %collective-permute-start.5 = (bf16[2,1,128,8,128]{4,2,3,1,0:T(8,128)(2,1)S(1)}, bf16[2,1,128,8,128]{4,2,3,1,0:T(8,128)(2,1)S(1)}, u32[]{:S(2)}, u32[]{:S(2)}) collective-permute-start(bf16[2,1,128,8,128]{4,2,3,1,0:T(8,128)(2,1)S(1)} %maximum_select_fusion.13), channel_id=1, source_target_pairs={{0,2},{1,3},{2,0},{3,1},{4,6},{5,7},{6,4},{7,5},{8,10},{9,11},{10,... | collective-permute-start | bytes 1572872 | tf_op jit(solution)/shard_map/ppermute | solution.py:19
  544.2 26.1 %collective-permute-start.9 = (bf16[2,1,128,8,128]{4,2,3,1,0:T(8,128)(2,1)S(1)}, bf16[2,1,128,8,128]{4,2,3,1,0:T(8,128)(2,1)S(1)}, u32[]{:S(2)}, u32[]{:S(2)}) collective-permute-start(bf16[2,1,128,8,128]{4,2,3,1,0:T(8,128)(2,1)S(1)} %maximum_select_fusion.15), channel_id=1, source_target_pairs={{0,2},{1,3},{2,0},{3,1},{4,6},{5,7},{6,4},{7,5},{8,10},{9,11},{10,... | collective-permute-start | bytes 1572872 | tf_op jit(solution)/shard_map/ppermute | solution.py:19
  547.9 91.2 %collective-permute-start.31 = (bf16[2,2,2,1,32,8,128]{6,5,4,2,1,0,3:T(8,128)(2,1)}, bf16[2,2,2,1,32,8,128]{6,5,4,2,1,0,3:T(8,128)(2,1)}, u32[]{:S(2)}, u32[]{:S(2)}) collective-permute-start(bf16[2,2,2,1,32,8,128]{6,5,4,2,1,0,3:T(8,128)(2,1)} %maximum_select_fusion.21), channel_id=1, source_target_pairs={{0,8},{1,9},{2,10},{3,11},{4,12},{5,13},{6,14},{7,15},{8,0},{9,1},... | collective-permute-start | bytes 1572872 | tf_op jit(solution)/shard_map/ppermute | solution.py:19
  551.6 93.2 %collective-permute-start.23 = (bf16[2,2,2,1,32,8,128]{6,5,4,2,1,0,3:T(8,128)(2,1)}, bf16[2,2,2,1,32,8,128]{6,5,4,2,1,0,3:T(8,128)(2,1)}, u32[]{:S(2)}, u32[]{:S(2)}) collective-permute-start(bf16[2,2,2,1,32,8,128]{6,5,4,2,1,0,3:T(8,128)(2,1)} %maximum_select_fusion.19), channel_id=1, source_target_pairs={{0,8},{1,9},{2,10},{3,11},{4,12},{5,13},{6,14},{7,15},{8,0},{9,1},... | collective-permute-start | bytes 1572872 | tf_op jit(solution)/shard_map/ppermute | solution.py:19
  557.1 92.6 %collective-permute-start.19 = (bf16[2,2,2,1,32,8,128]{6,5,4,2,1,0,3:T(8,128)(2,1)}, bf16[2,2,2,1,32,8,128]{6,5,4,2,1,0,3:T(8,128)(2,1)}, u32[]{:S(2)}, u32[]{:S(2)}) collective-permute-start(bf16[2,2,2,1,32,8,128]{6,5,4,2,1,0,3:T(8,128)(2,1)} %maximum_select_fusion.17), channel_id=1, source_target_pairs={{0,8},{1,9},{2,10},{3,11},{4,12},{5,13},{6,14},{7,15},{8,0},{9,1},... | collective-permute-start | bytes 1572872 | tf_op jit(solution)/shard_map/ppermute | solution.py:19
  564.7 91.8 %collective-permute-start.15 = (bf16[2,2,2,1,32,8,128]{6,5,4,2,1,3,0:T(8,128)(2,1)}, bf16[2,2,2,1,32,8,128]{6,5,4,2,1,3,0:T(8,128)(2,1)}, u32[]{:S(2)}, u32[]{:S(2)}) collective-permute-start(bf16[2,2,2,1,32,8,128]{6,5,4,2,1,3,0:T(8,128)(2,1)} %bitcast_select_fusion.2), channel_id=1, source_target_pairs={{0,8},{1,9},{2,10},{3,11},{4,12},{5,13},{6,14},{7,15},{8,0},{9,1},... | collective-permute-start | bytes 1572872 | tf_op jit(solution)/shard_map/ppermute | solution.py:19
  570.3 158.9 %collective-permute-start.62 = (bf16[2,2,2,2,2,2,2,2,1,1,8,128]{11,10,7,6,5,4,3,2,1,0,9,8:T(8,128)(2,1)}, bf16[2,2,2,2,2,2,2,2,1,1,8,128]{11,10,7,6,5,4,3,2,1,0,9,8:T(8,128)(2,1)}, u32[]{:S(2)}, u32[]{:S(2)}) collective-permute-start(bf16[2,2,2,2,2,2,2,2,1,1,8,128]{11,10,7,6,5,4,3,2,1,0,9,8:T(8,128)(2,1)} %ma, ...), channel_id=1, source_target_pairs={{0,256},{1,257},{2,258},{3,259},{4,260},{5,261},{6,262},{7,263},{8... | collective-permute-start | bytes 1572872 | tf_op jit(solution)/shard_map/ppermute | solution.py:19
  639.1 91.6 %collective-permute-start.80 = (bf16[2,2,2,2,2,2,2,2,1,1,8,128]{11,10,7,6,5,4,3,2,1,0,9,8:T(8,128)(2,1)}, bf16[2,2,2,2,2,2,2,2,1,1,8,128]{11,10,7,6,5,4,3,2,1,0,9,8:T(8,128)(2,1)}, u32[]{:S(2)}, u32[]{:S(2)}) collective-permute-start(bf16[2,2,2,2,2,2,2,2,1,1,8,128]{11,10,7,6,5,4,3,2,1,0,9,8:T(8,128)(2,1)} %ma, ...), channel_id=1, source_target_pairs={{0,256},{1,257},{2,258},{3,259},{4,260},{5,261},{6,262},{7,263},{8... | collective-permute-start | bytes 1572872 | tf_op jit(solution)/shard_map/ppermute | solution.py:19
  644.8 87.3 %collective-permute-start.44 = (bf16[2,2,2,2,2,2,2,2,1,1,8,128]{11,10,7,6,5,4,3,2,1,0,9,8:T(8,128)(2,1)}, bf16[2,2,2,2,2,2,2,2,1,1,8,128]{11,10,7,6,5,4,3,2,1,0,9,8:T(8,128)(2,1)}, u32[]{:S(2)}, u32[]{:S(2)}) collective-permute-start(bf16[2,2,2,2,2,2,2,2,1,1,8,128]{11,10,7,6,5,4,3,2,1,0,9,8:T(8,128)(2,1)} %ma, ...), channel_id=1, source_target_pairs={{0,256},{1,257},{2,258},{3,259},{4,260},{5,261},{6,262},{7,263},{8... | collective-permute-start | bytes 1572872 | tf_op jit(solution)/shard_map/ppermute | solution.py:19
  649.7 84.3 %collective-permute-start.53 = (bf16[2,2,2,2,2,2,2,2,1,1,8,128]{11,10,7,6,5,4,3,2,1,0,9,8:T(8,128)(2,1)}, bf16[2,2,2,2,2,2,2,2,1,1,8,128]{11,10,7,6,5,4,3,2,1,0,9,8:T(8,128)(2,1)}, u32[]{:S(2)}, u32[]{:S(2)}) collective-permute-start(bf16[2,2,2,2,2,2,2,2,1,1,8,128]{11,10,7,6,5,4,3,2,1,0,9,8:T(8,128)(2,1)} %ma, ...), channel_id=1, source_target_pairs={{0,256},{1,257},{2,258},{3,259},{4,260},{5,261},{6,262},{7,263},{8... | collective-permute-start | bytes 1572872 | tf_op jit(solution)/shard_map/ppermute | solution.py:19
  (91 other events, 849.2 us)
where the time goes:
time: 798 us; the launch traced here: 789 us
  starting transfers between devices  341 us (43%)
  waiting for transfers between devices  188 us (24%)
  matrix products  131 us (16%)
  local copies, waits for them, and re-layouts  65.1 us (8%)
  other arithmetic  59.8 us (7%)
    ppermute x90, starting transfers between devices, partner(): lax.ppermute(array, axis, [(i, i ^ 1 << bit) for i in range(lax.axis_size...  341 us
    ppermute x90, waiting for transfers between devices, partner(): lax.ppermute(array, axis, [(i, i ^ 1 << bit) for i in range(lax.axis_size...  188 us
    select_n x106, other arithmetic, join_pair(): jnp.where(upper_half, jnp.stack([peer_part, own_part]), jnp.stack([own_pa...  36.6 us
    dot_general x24, matrix products, one_head(): jnp.dot(dscores_back, queryall, preferred_element_type=jnp.float32)  34.6 us
    dot_general x24, matrix products, one_head(): jnp.dot(dscores, keyall, preferred_element_type=jnp.float32) * score_scale  31.2 us
    dot_general x24, matrix products, one_head(): jnp.dot(query, keyall.T, preferred_element_type=jnp.float32) * score_scale  22 us
    dot_general x24, matrix products, one_head(): jnp.dot(keyown, queryall.T, preferred_element_type=jnp.float32)  21.2 us
    dynamic_slice x24, local copies, waits for them, and re-layouts, level_terms(): grad_query, grad_key, grad_value = lax.map(one_head, pieces)  16.7 us
  transfers between devices with their start and end apart: 90, of which 61 were waited for; matrix products, arithmetic and copies ran while one was open for 24% of the time, Pallas kernels for 0%

commit v1 on v0

v1 whole, which is shorter than its diff:
```python
import functools

import jax
import jax.numpy as jnp
from jax import lax
from jax.experimental import pallas as pl
from jax.experimental.pallas import tpu as pltpu
from jax.sharding import PartitionSpec as P

HEADS = 8
WIDTH = 128
TOK = 128
RING = 8
DEPTH = 16
ROWS = 4
DEVICES = 512
SCALE = WIDTH**-0.5
CHUNK = 4 * TOK + 16
OUT_CHUNK = 3 * TOK
PAIR = 5 * TOK
FAR = 48

BF = jnp.bfloat16
F32 = jnp.float32
VMEM = pl.BlockSpec(memory_space=pltpu.VMEM)
SMEM = pl.BlockSpec(memory_space=pltpu.SMEM)


def iota(shape, dim):
    return lax.broadcasted_iota(jnp.int32, shape, dim)


def dot(a, b):
    return jnp.dot(a, b, preferred_element_type=F32)


def dot_nt(a, b):
    return lax.dot_general(a, b, (((1,), (1,)), ((), ())), preferred_element_type=F32)


def dot_tn(a, b):
    return lax.dot_general(a, b, (((0,), (0,)), ((), ())), preferred_element_type=F32)


def split3(x):
    high = x.astype(BF).astype(F32)
    rest = x - high
    middle = rest.astype(BF).astype(F32)
    low = (rest - middle).astype(BF).astype(F32)
    return high, middle, low


def place3(parts, slot, first):
    high, middle, low = parts
    return jnp.where(
        slot == first,
        high,
        jnp.where(slot == first + 1, middle, jnp.where(slot == first + 2, low, 0.0)),
    )


def position_of(order):
    return 4 * (order % 32) + order // 32


def pre_kernel(q_ref, k_ref, v_ref, o_ref, g_ref, n_ref, near_ref, far_ref):
    perm = (position_of(iota((TOK, TOK), 0)) == iota((TOK, TOK), 1)).astype(BF)
    far_rows = []
    for tensor, ref in enumerate((q_ref, k_ref, v_ref, g_ref)):
        ordered = dot(perm, ref[...]).astype(BF)
        first = ref[0:16, :].astype(F32)
        row = iota((16, WIDTH), 0)
        diagonal = jnp.zeros((16, WIDTH), F32)
        for head in range(HEADS):
            columns = slice(head * WIDTH, (head + 1) * WIDTH)
            near_ref[head, tensor * TOK : (tensor + 1) * TOK, :] = ordered[:, columns]
            diagonal = jnp.where(row == head, first[:, columns], diagonal)
        far_rows.append(diagonal[0:8])
    product = g_ref[...].astype(F32) * o_ref[...].astype(F32)
    lane = iota((TOK, 128), 1)
    spread = jnp.zeros((TOK, 128), F32)
    for head in range(HEADS):
        columns = slice(head * WIDTH, (head + 1) * WIDTH)
        total = jnp.sum(product[:, columns], axis=-1, keepdims=True)
        spread = jnp.where(lane // 16 == head, total, spread)
    deltas = place3(split3(spread), lane % 16, 3)
    norms = jnp.broadcast_to(n_ref[...][:, None, :], (HEADS, 16, TOK)).reshape(128, TOK)
    norms = place3(split3(norms), iota((128, TOK), 0) % 16, 0)
    stat_rows = norms + deltas.T
    stat_columns = deltas + norms.T
    ordered_stats = dot_nt(stat_rows.astype(BF), perm).astype(BF)
    for head in range(HEADS):
        near_ref[head, 4 * TOK : CHUNK, :] = ordered_stats[head * 16 : (head + 1) * 16, :]
    far_stats = jnp.sum(
        jnp.where(iota((TOK, 128), 0) == lane // 16, stat_columns, 0.0), axis=0, keepdims=True
    )
    far_rows.append(jnp.where(iota((16, 128), 0) == 0, far_stats, 0.0))
    payload = jnp.concatenate(far_rows, axis=0).astype(BF)
    for layer in range(DEPTH):
        far_ref[layer] = payload


def far_kernel(i_ref, r_ref, s_ref, flat):
    index = i_ref[0]
    row = index // 128
    layer = (index // 8) % DEPTH
    place = index % RING
    flat[...] = r_ref[...].astype(F32).reshape(DEPTH * FAR, WIDTH)
    stats = flat[pl.ds(32, DEPTH, stride=FAR), :].astype(BF)
    spot = (iota((DEPTH, 128), 1) == place * 16 + iota((DEPTH, 128), 0)).astype(BF)
    stat_tiles = dot_tn(stats, spot)
    depth = iota((DEPTH, WIDTH), 0)
    tile_row = iota((16, WIDTH), 0)
    for head in range(HEADS):
        query, key, value, grad = [
            flat[pl.ds(tensor * 8 + head, DEPTH, stride=FAR), :] for tensor in range(4)
        ]
        extra = stat_tiles[head * 16 : (head + 1) * 16, :]
        for tensor in range(4):
            own = flat[pl.ds(layer * FAR + tensor * 8 + head, 1), :]
            extra = jnp.where(tile_row == 8 + tensor, own, extra)
        extra = extra.astype(BF)
        for target in range(ROWS):
            cut = jnp.where(row < target, DEPTH, jnp.where(row == target, layer, 0))
            earlier = depth < cut
            chunk = target * RING + head
            s_ref[chunk, 0:16, :] = jnp.where(earlier, key, query).astype(BF)
            s_ref[chunk, 16:32, :] = jnp.where(earlier, value, grad).astype(BF)
            s_ref[chunk, 32:48, :] = extra


def pair_kernel(i_ref, r_ref, p_ref):
    index = i_ref[0]
    upper = (index // 8) % 2 == 1
    offset = 32 * (index % 4)
    first = jnp.where(upper, 0, TOK)
    second = jnp.where(upper, 3 * TOK, 2 * TOK)
    for number, start in enumerate((first, second)):
        start = pl.multiple_of(start + offset, 32)
        p_ref[number * 256 : (number + 1) * 256, :] = r_ref[:, pl.ds(start, 32), :].reshape(
            256, WIDTH
        )
    p_ref[512:640, :] = r_ref[:, 4 * TOK : CHUNK, :].reshape(128, 128)


def stat_pair(tile):
    norm = tile[0:1] + tile[1:2] + tile[2:3]
    delta = tile[3:4] + tile[4:5] + tile[5:6]
    return norm, delta


def block_terms(query, key, value, grad, norm, delta, mask):
    scores = dot_nt(key, query) * SCALE
    probs = jnp.exp(scores - norm)
    if mask is not None:
        probs = jnp.where(mask, probs, 0.0)
    dprobs = dot_nt(value, grad)
    dscores = (probs * (dprobs - delta)).astype(BF)
    return probs.astype(BF), dscores


def near_kernel(r_ref, o_ref):
    half = 256
    for segment in range(2):
        base = segment * 4

        def rows(tensor, first, count):
            part = r_ref[base + first : base + first + count, tensor * TOK : (tensor + 1) * TOK, :]
            return part.reshape(count * TOK, WIDTH)

        tiles = [r_ref[base + s, 4 * TOK : CHUNK, :].astype(F32) for s in range(4)]
        key_sum = [None, None]
        value_sum = [None, None]
        for block in range(2):
            count = (block + 1) * 2
            size = count * TOK
            query = rows(0, block * 2, 2)
            grad = rows(3, block * 2, 2)
            key = rows(1, 0, count)
            value = rows(2, 0, count)
            stats = [stat_pair(tiles[block * 2 + s]) for s in range(2)]
            norm = jnp.concatenate([s[0] for s in stats], axis=1)
            delta = jnp.concatenate([s[1] for s in stats], axis=1)
            key_order = iota((size, half), 0)
            query_order = iota((size, half), 1)
            key_place = key_order // TOK * TOK + position_of(key_order % TOK)
            query_place = (
                block * half + query_order // TOK * TOK + position_of(query_order % TOK)
            )
            probs, dscores = block_terms(
                query, key, value, grad, norm, delta, key_place <= query_place
            )
            query_grad = dot_tn(dscores, key) * SCALE
            o_ref[base + block * 2 : base + block * 2 + 2, 0:TOK, :] = query_grad.reshape(
                2, TOK, WIDTH
            )
            key_part = dot(dscores, query) * SCALE
            value_part = dot(probs, grad)
            for number in range(block + 1):
                piece = slice(number * half, (number + 1) * half)
                first = number == block
                key_sum[number] = key_part[piece] if first else key_sum[number] + key_part[piece]
                value_sum[number] = (
                    value_part[piece] if first else value_sum[number] + value_part[piece]
                )
        for number in range(2):
            span = slice(base + number * 2, base + number * 2 + 2)
            o_ref[span, TOK : 2 * TOK, :] = key_sum[number].reshape(2, TOK, WIDTH)
            o_ref[span, 2 * TOK : 3 * TOK, :] = value_sum[number].reshape(2, TOK, WIDTH)


def join_kernel(i_ref, r_ref, x_ref, f_ref, n_ref, o_ref, sums, wide):
    index = i_ref[0]
    row = index // 128
    layer = (index // 8) % DEPTH
    place = index % RING
    upper = layer % 2 == 1
    offset = pl.multiple_of(32 * (index % 4), 32)
    sums[...] = n_ref[...]

    def add(tensor, part):
        span = pl.ds(pl.multiple_of(tensor * TOK + offset, 32), 32)
        sums[:, span, :] = sums[:, span, :] + part.reshape(RING, 32, WIDTH)

    def own(tensor):
        start = pl.multiple_of(tensor * TOK + offset, 32)
        return r_ref[:, pl.ds(start, 32), :].reshape(256, WIDTH)

    lane_from = iota((1024, 256), 0)
    lane_to = iota((1024, 256), 1)
    spot = (lane_from == lane_to // 32 * TOK + offset + lane_to % 32).astype(BF)
    own_tiles = jnp.concatenate([r_ref[s, 4 * TOK : CHUNK, :] for s in range(RING)], axis=1)
    own_norm, own_delta = stat_pair(dot(own_tiles, spot))
    query, key, value, grad = own(0), own(1), own(2), own(3)
    causal = iota((256, 256), 0) <= iota((256, 256), 1)
    probs, dscores = block_terms(query, key, value, grad, own_norm, own_delta, causal)
    add(0, dot_tn(dscores, key) * SCALE)
    add(1, dot(dscores, query) * SCALE)
    add(2, dot(probs, grad))

    @pl.when(upper)
    def _():
        far_key = x_ref[0:256, :]
        far_value = x_ref[256:512, :]
        _, dscores = block_terms(query, far_key, far_value, grad, own_norm, own_delta, None)
        add(0, dot_tn(dscores, far_key) * SCALE)

    @pl.when(jnp.logical_not(upper))
    def _():
        far_query = x_ref[0:256, :]
        far_grad = x_ref[256:512, :]
        far_tiles = jnp.concatenate(
            [x_ref[512 + s * 16 : 528 + s * 16, :] for s in range(RING)], axis=1
        )
        far_norm, far_delta = stat_pair(dot(far_tiles, spot))
        probs, dscores = block_terms(far_query, key, value, far_grad, far_norm, far_delta, None)
        add(1, dot(dscores, far_query) * SCALE)
        add(2, dot(probs, far_grad))

    extras = f_ref[:, 32:48, :].astype(F32)
    stat_rows = []
    for y in range(ROWS):
        stat_rows.append(jnp.sum(extras[y * RING : (y + 1) * RING], axis=0))
    norm_row, delta_row = stat_pair(jnp.concatenate(stat_rows, axis=1))
    wide[...] = f_ref[pl.ds(row * RING, RING), 32:48, :].astype(F32).reshape(128, 128)
    mine = [wide[pl.ds(8 + tensor, RING, stride=16), :] for tensor in range(4)]
    lane8 = iota((8, 512), 1)
    seat8 = iota((8, 512), 0)
    chosen = lane8 == row * 128 + seat8 * 16 + layer
    norm_column = jnp.sum(jnp.where(chosen, norm_row, 0.0), axis=1, keepdims=True)
    delta_column = jnp.sum(jnp.where(chosen, delta_row, 0.0), axis=1, keepdims=True)
    tail_lane = iota((8, 128), 1)
    tail_seat = iota((8, 128), 0)
    on_tail = tail_lane == 8 + tail_seat
    norm_tail = jnp.sum(jnp.where(on_tail, norm_column, 0.0), axis=0, keepdims=True)
    delta_tail = jnp.sum(jnp.where(on_tail, delta_column, 0.0), axis=0, keepdims=True)
    pad = jnp.zeros((112, WIDTH), F32)
    near_a = jnp.concatenate([mine[1], mine[0], pad], axis=0).astype(BF)
    near_b = jnp.concatenate([mine[2], mine[3], pad], axis=0).astype(BF)
    all_a = jnp.concatenate([f_ref[:, 0:16, :].reshape(512, WIDTH), near_a], axis=0)
    all_b = jnp.concatenate([f_ref[:, 16:32, :].reshape(512, WIDTH), near_b], axis=0)
    left = jnp.concatenate([mine[0], mine[1]], axis=0).astype(BF)
    right = jnp.concatenate([mine[3], mine[2]], axis=0).astype(BF)
    scores = dot_nt(left, all_a) * SCALE
    dprobs = dot_nt(right, all_b)
    norm_wide = jnp.concatenate([norm_row, norm_tail], axis=1)
    delta_wide = jnp.concatenate([delta_row, delta_tail], axis=1)
    norms = jnp.concatenate(
        [jnp.broadcast_to(norm_column, (8, 640)), jnp.broadcast_to(norm_wide, (8, 640))], axis=0
    )
    deltas = jnp.concatenate(
        [jnp.broadcast_to(delta_column, (8, 640)), jnp.broadcast_to(delta_wide, (8, 640))], axis=0
    )
    lane = iota((16, 640), 1)
    seat = iota((16, 640), 0)
    source = lane // 128 * DEPTH + lane % DEPTH
    here = row * DEPTH + layer
    tail = lane - 512
    low = jnp.where(lane < 512, source, jnp.where(tail < 8, here - 1 + (tail > seat), 1 << 20))
    high = jnp.where(lane < 512, source, jnp.where((tail >= 8) & (tail < 16), here + 1 - (tail < seat), -1))
    valid = ((seat < 8) & (low < here)) | ((seat >= 8) & (high > here))
    probs = jnp.where(valid, jnp.exp(jnp.where(valid, scores - norms, 0.0)), 0.0)
    dscores = (probs * (dprobs - deltas)).astype(BF)
    by_a = dot(dscores, all_a) * SCALE
    by_b = dot(probs.astype(BF), all_b)
    wide[0:16, :] = by_a
    wide[16:32, :] = by_b
    spot_row = offset + place // 4
    for s in range(RING):
        for tensor, at in ((0, s), (1, 8 + s), (2, 24 + s)):
            span = pl.ds(tensor * TOK + spot_row, 1)
            sums[s, span, :] = sums[s, span, :] + wide[at : at + 1, :]
    o_ref[...] = sums[...].astype(BF)


def post_kernel(r_ref, q_ref, k_ref, v_ref):
    back = (position_of(iota((TOK, TOK), 1)) == iota((TOK, TOK), 0)).astype(BF)
    for tensor, ref in enumerate((q_ref, k_ref, v_ref)):
        for head in range(HEADS):
            part = r_ref[head, tensor * TOK : (tensor + 1) * TOK, :]
            ref[:, head * WIDTH : (head + 1) * WIDTH] = dot(back, part).astype(BF)


def call(kernel, name, out, specs, scratch=(), flops=0, moved=0):
    return pl.pallas_call(
        kernel,
        name=name,
        out_shape=out,
        in_specs=specs,
        out_specs=jax.tree.map(lambda _: VMEM, out),
        scratch_shapes=list(scratch),
        cost_estimate=pl.CostEstimate(flops=flops, bytes_accessed=moved, transcendentals=0),
        compiler_params=pltpu.CompilerParams(vmem_limit_bytes=40 * 1024 * 1024),
    )


def shape(dims, dtype=BF):
    return jax.ShapeDtypeStruct(dims, dtype)


RING_GROUPS = [[base + i for i in range(RING)] for base in range(0, DEVICES, RING)]
DEPTH_GROUPS = [
    [y * 128 + z * 8 + i for z in range(DEPTH)] for y in range(ROWS) for i in range(RING)
]
FLAT_GROUPS = [
    [y * 128 + z * 8 + i for y in range(ROWS) for i in range(RING)] for z in range(DEPTH)
]


def exchange(array, groups):
    return lax.all_to_all(array, "seq", 0, 0, axis_index_groups=groups, tiled=True)


def body(query_rows, key_rows, value_rows, attn_out, out_grad, log_norms):
    index = lax.axis_index("seq").astype(jnp.int32).reshape(1)
    near, far = call(
        pre_kernel,
        "reorder",
        (shape((HEADS, CHUNK, WIDTH)), shape((DEPTH, FAR, WIDTH))),
        [VMEM] * 6,
        flops=2 * 128 * 128 * 4096,
        moved=3 << 20,
    )(query_rows, key_rows, value_rows, attn_out, out_grad, log_norms)
    far = exchange(far, DEPTH_GROUPS)
    near = exchange(near, RING_GROUPS)
    far = call(
        far_kernel,
        "far_middle",
        shape((ROWS * RING, FAR, WIDTH)),
        [SMEM, VMEM],
        [pltpu.VMEM((DEPTH * FAR, WIDTH), F32)],
        moved=1 << 20,
    )(index, far)
    far = exchange(far, FLAT_GROUPS)
    pair = call(pair_kernel, "pair_rows", shape((PAIR, WIDTH)), [SMEM, VMEM], moved=1 << 18)(
        index, near
    )
    pair = lax.ppermute(pair, "seq", [(i, i ^ 8) for i in range(DEVICES)])
    sums = call(
        near_kernel,
        "near_grads",
        shape((RING, OUT_CHUNK, WIDTH), F32),
        [VMEM],
        flops=2 * 10 * 128 * 512 * 384,
        moved=3 << 20,
    )(near)
    grads = call(
        join_kernel,
        "join_grads",
        shape((RING, OUT_CHUNK, WIDTH)),
        [SMEM, VMEM, VMEM, VMEM, VMEM],
        [pltpu.VMEM((RING, OUT_CHUNK, WIDTH), F32), pltpu.VMEM((128, 128), F32)],
        flops=2 * 10 * 128 * 256 * 256,
        moved=4 << 20,
    )(index, near, pair, far, sums)
    grads = exchange(grads, RING_GROUPS)
    out = shape((TOK, HEADS * WIDTH))
    return call(
        post_kernel, "restore", (out, out, out), [VMEM], flops=2 * 128 * 128 * 3072, moved=2 << 20
    )(grads)


def solution(mesh):
    return jax.shard_map(
        body,
        mesh=mesh,
        in_specs=(
            P("seq", None),
            P("seq", None),
            P("seq", None),
            P("seq", None),
            P("seq", None),
            P(None, "seq"),
        ),
        out_specs=(P("seq", None), P("seq", None), P("seq", None)),
        check_vma=False,
    )
```

time: 798 us -> 94.7 us (0.12)
  the two profiles are of different devices: /device:TPU:26 before, /device:TPU:1 now
where the time goes in v1:
time: 94.7 us; the launch traced here: 94.1 us
  blocking collectives  43.1 us (46%)
  waiting for transfers between devices  19.8 us (21%)
  starting transfers between devices  18.2 us (19%)
  Pallas kernels  6.97 us (7%)
  local copies, waits for them, and re-layouts  5.43 us (6%)
    all_to_all x2, blocking collectives, exchange(): lax.all_to_all(array, 'seq', 0, 0, axis_index_groups=groups, tiled=True)  43.1 us
    all_to_all x2, waiting for transfers between devices, exchange(): lax.all_to_all(array, 'seq', 0, 0, axis_index_groups=groups, tiled=True)  17.1 us
    all_to_all x2, starting transfers between devices, exchange(): lax.all_to_all(array, 'seq', 0, 0, axis_index_groups=groups, tiled=True)  15.2 us
    unnamed x12, local copies, waits for them, and re-layouts  5.43 us
    ppermute x1, starting transfers between devices, body(): pair = lax.ppermute(pair, 'seq', [(i, i ^ 8) for i in range(DEVICES)])  2.93 us
    ppermute x1, waiting for transfers between devices, body(): pair = lax.ppermute(pair, 'seq', [(i, i ^ 8) for i in range(DEVICES)])  2.67 us
  transfers between devices with their start and end apart: 3, of which 3 were waited for; matrix products, arithmetic and copies ran while one was open for 0% of the time, Pallas kernels for 3%

profile of v1, /device:TPU:1, one launch (start us, length us, event | category | flops | bytes accessed | tf_op | source)
XLA Modules:
  0.0 94.1 jit_solution(15729852694303110221)
XLA Ops:
  0.6 0.0 copy-start
  0.6 0.9 copy-done
  1.6 0.0 copy-start.1
  1.6 0.9 %copy-done.1 = bf16[128,1024]{1,0:T(8,128)(2,1)S(1)} copy-done((bf16[128,1024]{1,0:T(8,128)(2,1)S(1)}, bf16[128,1024]{1,0:T(8,128)(2,1)}, u32[]{:S(2)}) %copy-start.1) | copy-done | bytes 262168
  2.5 0.0 copy-start.2
  2.5 0.9 %copy-done.2 = bf16[128,1024]{1,0:T(8,128)(2,1)S(1)} copy-done((bf16[128,1024]{1,0:T(8,128)(2,1)S(1)}, bf16[128,1024]{1,0:T(8,128)(2,1)}, u32[]{:S(2)}) %copy-start.2) | copy-done | bytes 262168
  3.5 0.0 copy-start.3
  3.5 0.9 %copy-done.3 = bf16[128,1024]{1,0:T(8,128)(2,1)S(1)} copy-done((bf16[128,1024]{1,0:T(8,128)(2,1)S(1)}, bf16[128,1024]{1,0:T(8,128)(2,1)}, u32[]{:S(2)}) %copy-start.3) | copy-done | bytes 262168
  4.4 0.0 copy-start.4
  4.4 0.9 %copy-done.4 = bf16[128,1024]{1,0:T(8,128)(2,1)S(1)} copy-done((bf16[128,1024]{1,0:T(8,128)(2,1)S(1)}, bf16[128,1024]{1,0:T(8,128)(2,1)}, u32[]{:S(2)}) %copy-start.4) | copy-done | bytes 262168
  5.4 0.0 copy-start.5
  5.4 0.7 copy-done.5
  6.1 1.4 %reorder.1 = (bf16[8,528,128]{2,1,0:T(8,128)(2,1)}, bf16[16,48,128]{2,1,0:T(8,128)(2,1)S(1)}) custom-call(bf16[128,1024]{1,0:T(8,128)(2,1)S(1)} %copy-done, bf16[128,1024]{1,0:T(8,128)(2,1)S(1)} %copy-done.1, bf16[128,1024]{1,0:T(8,128)(2,1)S(1)} %copy-done.2, bf16[128,1024]{1,0:T(8,128)(2,1)S(1)} %copy-done.3, bf16[128,1024]{1,0:T(8,128)(2,1)S(1)} %copy-done.4, ...), custom_call_target="tpu_custom_call" | custom-call | flops 134217728 | bytes 3145728 | tf_op jit(solution)/shard_map/reorder/pallas_call | solution.py:356
  7.5 28.1 %all_to_all.20.r_ref = bf16[16,48,128]{2,1,0:T(8,128)(2,1)S(1)} all-to-all(bf16[16,48,128]{2,1,0:T(8,128)(2,1)S(1)} %get-tuple-element.6), channel_id=1, replica_groups={{0,8,16,24,32,40,48,56,64,72,80,88,96,104,112,120},{1,9,17,25,33,41,49,..., dimensions={0} | all-to-all | bytes 393216 | tf_op jit(solution)/shard_map/all_to_all | solution.py:351
  35.6 9.1 %all-to-all-start = ((bf16[8,528,128]{2,1,0:T(8,128)(2,1)}), bf16[8,528,128]{2,1,0:T(8,128)(2,1)S(1)}, u32[]{:S(2)}, u32[]{:S(2)}) async-start(bf16[8,528,128]{2,1,0:T(8,128)(2,1)} %get-tuple-element.5), calls=%async_computation | async-start | bytes 2162688 | tf_op jit(solution)/shard_map/all_to_all | solution.py:351
  44.7 1.0 %far_middle.1 = bf16[32,48,128]{2,1,0:T(8,128)(2,1)} custom-call(s32[1]{0:T(128)} %bitcast.i_ref, bf16[16,48,128]{2,1,0:T(8,128)(2,1)S(1)} %all_to_all.20.r_ref), custom_call_target="tpu_custom_call" | custom-call | bytes 1048576 | tf_op jit(solution)/shard_map/far_middle/pallas_call | solution.py:366
  45.7 14.5 %all-to-all-done.r_ref = bf16[8,528,128]{2,1,0:T(8,128)(2,1)S(1)} async-done(((bf16[8,528,128]{2,1,0:T(8,128)(2,1)}), bf16[8,528,128]{2,1,0:T(8,128)(2,1)S(1)}, u32[]{:S(2)}, u32[]{:S(2)}) %all-to-all-start) | async-done | bytes 1081376 | tf_op jit(solution)/shard_map/all_to_all | solution.py:351
  60.2 6.1 %all-to-all-start.2 = ((bf16[32,48,128]{2,1,0:T(8,128)(2,1)}), bf16[32,48,128]{2,1,0:T(8,128)(2,1)S(1)}, u32[]{:S(2)}, u32[]{:S(2)}) async-start(bf16[32,48,128]{2,1,0:T(8,128)(2,1)} %far_middle.1), calls=%async_computation.2 | async-start | bytes 786432 | tf_op jit(solution)/shard_map/all_to_all | solution.py:351
  66.3 2.9 %collective-permute-start = (bf16[640,128]{1,0:T(8,128)(2,1)S(1)}, bf16[640,128]{1,0:T(8,128)(2,1)S(1)}, u32[]{:S(2)}, u32[]{:S(2)}) collective-permute-start(bf16[640,128]{1,0:T(8,128)(2,1)S(1)} %pair_rows.1), channel_id=1, source_target_pairs={{0,8},{1,9},{2,10},{3,11},{4,12},{5,13},{6,14},{7,15},{8,0},{9,1},... | collective-permute-start | bytes 491528 | tf_op jit(solution)/shard_map/ppermute | solution.py:378
  69.3 1.9 %near_grads.1.n_ref = f32[8,384,128]{2,1,0:T(8,128)S(1)} custom-call(bf16[8,528,128]{2,1,0:T(8,128)(2,1)S(1)} %all-to-all-done.r_ref), custom_call_target="tpu_custom_call" | custom-call | flops 503316480 | bytes 3145728 | tf_op jit(solution)/shard_map/near_grads/pallas_call | solution.py:379
  71.1 2.7 %collective-permute-done.x_ref = bf16[640,128]{1,0:T(8,128)(2,1)S(1)} collective-permute-done((bf16[640,128]{1,0:T(8,128)(2,1)S(1)}, bf16[640,128]{1,0:T(8,128)(2,1)S(1)}, u32[]{:S(2)}, u32[]{:S(2)}) %collective-permute-start) | collective-permute-done | bytes 163872 | tf_op jit(solution)/shard_map/ppermute | solution.py:378
  73.8 2.7 %all-to-all-done.2.f_ref = bf16[32,48,128]{2,1,0:T(8,128)(2,1)S(1)} async-done(((bf16[32,48,128]{2,1,0:T(8,128)(2,1)}), bf16[32,48,128]{2,1,0:T(8,128)(2,1)S(1)}, u32[]{:S(2)}, u32[]{:S(2)}) %all-to-all-start.2) | async-done | bytes 393248 | tf_op jit(solution)/shard_map/all_to_all | solution.py:351
  76.5 1.6 %join_grads.1 = bf16[8,384,128]{2,1,0:T(8,128)(2,1)S(1)} custom-call(s32[1]{0:T(128)} %bitcast.i_ref, bf16[8,528,128]{2,1,0:T(8,128)(2,1)S(1)} %all-to-all-done.r_ref, bf16[640,128]{1,0:T(8,128)(2,1)S(1)} %collective-permute-done.x_ref, bf16[32,48,128]{2,1,0:T(8,128)(2,1)S(1)} %all-to-all-done.2.f_ref, f32[8,384,128]{2,1,0:T(8,128)S(1)} %near_grads.1.n_ref), custom_call_target="tpu_custom_call" | custom-call | flops 167772160 | bytes 4194304 | tf_op jit(solution)/shard_map/join_grads/pallas_call | solution.py:387
  78.1 15.0 %all_to_all.21.r_ref = bf16[8,384,128]{2,1,0:T(8,128)(2,1)S(1)} all-to-all(bf16[8,384,128]{2,1,0:T(8,128)(2,1)S(1)} %join_grads.1), channel_id=1, replica_groups={{0,1,2,3,4,5,6,7},{8,9,10,11,12,13,14,15},{16,17,18,19,20,21,22,23},{24..., dimensions={0} | all-to-all | bytes 1572864 | tf_op jit(solution)/shard_map/all_to_all | solution.py:351
  93.0 1.1 %restore.1 = (bf16[128,1024]{1,0:T(8,128)(2,1)}, bf16[128,1024]{1,0:T(8,128)(2,1)}, bf16[128,1024]{1,0:T(8,128)(2,1)}) custom-call(bf16[8,384,128]{2,1,0:T(8,128)(2,1)S(1)} %all_to_all.21.r_ref), custom_call_target="tpu_custom_call" | custom-call | flops 100663296 | bytes 2097152 | tf_op jit(solution)/shard_map/restore/pallas_call | solution.py:398
  (1 shorter events, 0.0 us)
Async XLA Ops:
  0.6 1.0 %copy-start = (bf16[128,1024]{1,0:T(8,128)(2,1)S(1)}, bf16[128,1024]{1,0:T(8,128)(2,1)}, u32[]{:S(2)}) copy-start(bf16[128,1024]{1,0:T(8,128)(2,1)} %q_ref.1) | copy-start | bytes 786436
  1.6 0.9 %copy-start.1 = (bf16[128,1024]{1,0:T(8,128)(2,1)S(1)}, bf16[128,1024]{1,0:T(8,128)(2,1)}, u32[]{:S(2)}) copy-start(bf16[128,1024]{1,0:T(8,128)(2,1)} %k_ref.1) | copy-start | bytes 786436
  2.5 0.9 %copy-start.2 = (bf16[128,1024]{1,0:T(8,128)(2,1)S(1)}, bf16[128,1024]{1,0:T(8,128)(2,1)}, u32[]{:S(2)}) copy-start(bf16[128,1024]{1,0:T(8,128)(2,1)} %v_ref.1) | copy-start | bytes 786436
  3.5 0.9 %copy-start.3 = (bf16[128,1024]{1,0:T(8,128)(2,1)S(1)}, bf16[128,1024]{1,0:T(8,128)(2,1)}, u32[]{:S(2)}) copy-start(bf16[128,1024]{1,0:T(8,128)(2,1)} %o_ref.1) | copy-start | bytes 786436
  4.4 0.9 %copy-start.4 = (bf16[128,1024]{1,0:T(8,128)(2,1)S(1)}, bf16[128,1024]{1,0:T(8,128)(2,1)}, u32[]{:S(2)}) copy-start(bf16[128,1024]{1,0:T(8,128)(2,1)} %g_ref.1) | copy-start | bytes 786436
  5.4 0.7 copy-start.5
  35.6 24.6 %all-to-all-start = ((bf16[8,528,128]{2,1,0:T(8,128)(2,1)}), bf16[8,528,128]{2,1,0:T(8,128)(2,1)S(1)}, u32[]{:S(2)}, u32[]{:S(2)}) async-start(bf16[8,528,128]{2,1,0:T(8,128)(2,1)} %get-tuple-element.5), calls=%async_computation | async-start | bytes 2162688 | tf_op jit(solution)/shard_map/all_to_all | solution.py:351
  60.2 16.3 %all-to-all-start.2 = ((bf16[32,48,128]{2,1,0:T(8,128)(2,1)}), bf16[32,48,128]{2,1,0:T(8,128)(2,1)S(1)}, u32[]{:S(2)}, u32[]{:S(2)}) async-start(bf16[32,48,128]{2,1,0:T(8,128)(2,1)} %far_middle.1), calls=%async_computation.2 | async-start | bytes 786432 | tf_op jit(solution)/shard_map/all_to_all | solution.py:351
  66.3 7.5 %collective-permute-start = (bf16[640,128]{1,0:T(8,128)(2,1)S(1)}, bf16[640,128]{1,0:T(8,128)(2,1)S(1)}, u32[]{:S(2)}, u32[]{:S(2)}) collective-permute-start(bf16[640,128]{1,0:T(8,128)(2,1)S(1)} %pair_rows.1), channel_id=1, source_target_pairs={{0,8},{1,9},{2,10},{3,11},{4,12},{5,13},{6,14},{7,15},{8,0},{9,1},... | collective-permute-start | bytes 491528 | tf_op jit(solution)/shard_map/ppermute | solution.py:378

commit v2 on v1

v2 whole, which is shorter than its diff:
```python
import functools

import jax
import jax.numpy as jnp
from jax import lax
from jax.experimental import pallas as pl
from jax.experimental.pallas import tpu as pltpu
from jax.sharding import PartitionSpec as P

HEADS = 8
WIDTH = 128
TOK = 128
RING = 8
DEPTH = 16
ROWS = 4
DEVICES = 512
SCALE = WIDTH**-0.5
SIDE = 32
CHUNK = 4 * SIDE + 16
OUT_CHUNK = 3 * SIDE
PAIR = 4 * 128 + 32
FAR = 48
PLANE = 2 * 128 + 16
NEAR = 2 * TOK + 16

BF = jnp.bfloat16
F32 = jnp.float32
VMEM = pl.BlockSpec(memory_space=pltpu.VMEM)
SMEM = pl.BlockSpec(memory_space=pltpu.SMEM)
ANY = pl.BlockSpec(memory_space=pl.ANY)


def iota(shape, dim):
    return lax.broadcasted_iota(jnp.int32, shape, dim)


def dot(a, b):
    return jnp.dot(a, b, preferred_element_type=F32)


def dot_nt(a, b):
    return lax.dot_general(a, b, (((1,), (1,)), ((), ())), preferred_element_type=F32)


def dot_tn(a, b):
    return lax.dot_general(a, b, (((0,), (0,)), ((), ())), preferred_element_type=F32)


def split3(x):
    high = x.astype(BF).astype(F32)
    rest = x - high
    middle = rest.astype(BF).astype(F32)
    low = (rest - middle).astype(BF).astype(F32)
    return high, middle, low


def place3(parts, slot, first):
    high, middle, low = parts
    return jnp.where(
        slot == first,
        high,
        jnp.where(slot == first + 1, middle, jnp.where(slot == first + 2, low, 0.0)),
    )


def columns_of(head):
    return slice(head * WIDTH, (head + 1) * WIDTH)


def stat_pair(tile):
    norm = tile[0:1] + tile[1:2] + tile[2:3]
    delta = tile[3:4] + tile[4:5] + tile[5:6]
    return norm, delta


def block_terms(query, key, value, grad, norm, delta, mask):
    scores = dot_nt(key, query) * SCALE
    probs = jnp.exp(scores - norm)
    if mask is not None:
        probs = jnp.where(mask, probs, 0.0)
    dprobs = dot_nt(value, grad)
    dscores = (probs * (dprobs - delta)).astype(BF)
    return probs.astype(BF), dscores


def select_kernel(i_ref, q_in, k_in, v_in, g_in, o_in, n_in, out_ref, stat_ref, q, k, v, g, o, n, sems):
    sources = (n_in, g_in, o_in, q_in, k_in, v_in)
    places = (n, g, o, q, k, v)
    copies = [
        pltpu.make_async_copy(source, place, sems.at[number])
        for number, (source, place) in enumerate(zip(sources, places))
    ]
    for copy in copies:
        copy.start()
    seat = i_ref[0] % RING
    copies[0].wait()
    copies[1].wait()
    copies[2].wait()
    lane = iota((TOK, 128), 1)
    spread = jnp.zeros((TOK, 128), F32)
    for head in range(HEADS):
        product = g[:, columns_of(head)].astype(F32) * o[:, columns_of(head)].astype(F32)
        total = jnp.sum(product, axis=-1, keepdims=True)
        spread = jnp.where(lane // 16 == head, total, spread)
    deltas = place3(split3(spread), lane % 16, 3)
    norms = jnp.broadcast_to(n[...][:, None, :], (HEADS, 16, TOK)).reshape(128, TOK)
    norms = place3(split3(norms), iota((128, TOK), 0) % 16, 0)
    stats = (norms + deltas.T).astype(BF)
    for head in range(HEADS):
        stat_ref[:, columns_of(head)] = stats[head * 16 : (head + 1) * 16, :]
    token = iota((TOK, 128), 0)
    for residue in range(4):
        spot = ((token == 4 * (lane % SIDE) + residue) & (lane // SIDE == seat % 4)).astype(BF)
        placed = dot(stats, spot).astype(BF)
        for head in (residue, residue + 4):
            out_ref[head, 4 * SIDE : CHUNK, :] = placed[head * 16 : (head + 1) * 16, :]
    order = iota((TOK, TOK), 0)
    perm = (4 * (order % SIDE) + order // SIDE == iota((TOK, TOK), 1)).astype(BF)
    for tensor, (ref, copy) in enumerate(
        ((q, copies[3]), (k, copies[4]), (v, copies[5]), (g, None))
    ):
        if copy is not None:
            copy.wait()
        ordered = dot(perm, ref[...]).astype(BF)
        for head in range(HEADS):
            start = SIDE * (head % 4)
            out_ref[head, tensor * SIDE : (tensor + 1) * SIDE, :] = ordered[
                start : start + SIDE, columns_of(head)
            ]


def payload_kernel(i_ref, q_in, k_in, v_in, g_in, s_in, core_ref, chip_ref, sems):
    index = i_ref[0]
    for number, (ref, bit) in enumerate(((core_ref, 1), (chip_ref, 2))):
        later = (index & bit) != 0

        def send(first, second, ref=ref, number=number):
            copies = [
                pltpu.make_async_copy(first, ref.at[pl.ds(0, TOK)], sems.at[number, 0]),
                pltpu.make_async_copy(second, ref.at[pl.ds(TOK, TOK)], sems.at[number, 1]),
                pltpu.make_async_copy(s_in, ref.at[pl.ds(2 * TOK, 16)], sems.at[number, 2]),
            ]
            for copy in copies:
                copy.start()
            for copy in copies:
                copy.wait()

        @pl.when(later)
        def _():
            send(q_in, g_in)

        @pl.when(jnp.logical_not(later))
        def _():
            send(k_in, v_in)


def near_kernel(i_ref, q, k, v, g, s, r1, r2, r3, after, dq, dk, dv):
    index = i_ref[0]
    core = (index & 1) == 1
    chip = (index & 2) == 2
    causal = iota((TOK, TOK), 0) <= iota((TOK, TOK), 1)
    own_stats = [stat_pair(s[:, columns_of(head)].astype(F32)) for head in range(HEADS)]
    for head in range(HEADS):
        c = columns_of(head)
        norm, delta = own_stats[head]
        probs, dscores = block_terms(q[:, c], k[:, c], v[:, c], g[:, c], norm, delta, causal)
        dq[:, c] = dot_tn(dscores, k[:, c]) * SCALE
        dk[:, c] = dot(dscores, q[:, c]) * SCALE
        dv[:, c] = dot(probs, g[:, c])

    def from_keys(refs):
        for head in range(HEADS):
            c = columns_of(head)
            norm, delta = own_stats[head]
            key = jnp.concatenate([ref[0:TOK, c] for ref in refs], axis=0)
            value = jnp.concatenate([ref[TOK : 2 * TOK, c] for ref in refs], axis=0)
            _, dscores = block_terms(q[:, c], key, value, g[:, c], norm, delta, None)
            dq[:, c] = dq[:, c] + dot_tn(dscores, key) * SCALE

    def from_queries(refs):
        for head in range(HEADS):
            c = columns_of(head)
            query = jnp.concatenate([ref[0:TOK, c] for ref in refs], axis=0)
            grad = jnp.concatenate([ref[TOK : 2 * TOK, c] for ref in refs], axis=0)
            tile = jnp.concatenate([ref[2 * TOK : NEAR, c] for ref in refs], axis=1).astype(F32)
            norm, delta = stat_pair(tile)
            probs, dscores = block_terms(query, k[:, c], v[:, c], grad, norm, delta, None)
            dk[:, c] = dk[:, c] + dot(dscores, query) * SCALE
            dv[:, c] = dv[:, c] + dot(probs, grad)

    for later, refs in ((core, (r1,)), (chip, (r2, r3))):

        @pl.when(later)
        def _(refs=refs):
            from_keys(refs)

        @pl.when(jnp.logical_not(later))
        def _(refs=refs):
            from_queries(refs)


def middle_kernel(i_ref, r_ref, far_ref, pair_ref, flat):
    index = i_ref[0]
    layer = (index // 8) % DEPTH
    place = index % RING
    upper = layer % 2 == 1
    lane = iota((16, 128), 1)
    tiles = [r_ref[s, 4 * SIDE : CHUNK, :].astype(F32) for s in range(RING)]
    stats = jnp.zeros((16, 128), F32)
    for s in range(RING):
        taken = jnp.where(lane == (s % 4) * SIDE + place // 4, tiles[s], 0.0)
        value = jnp.sum(taken, axis=1, keepdims=True)
        stats = jnp.where(lane == layer * RING + s, value, stats)
    rows = []
    for tensor in range(4):
        flat[...] = r_ref[:, tensor * SIDE : tensor * SIDE + 16, :].astype(F32).reshape(128, WIDTH)
        rows.append(flat[pl.ds(place // 4, RING, stride=16), :])
    payload = jnp.concatenate(rows + [stats], axis=0).astype(BF)
    for target in range(DEPTH):
        far_ref[target] = payload

    def fill(first, second):
        for number, tensor in enumerate((first, second)):
            pair_ref[number * 256 : (number + 1) * 256, :] = r_ref[
                :, tensor * SIDE : (tensor + 1) * SIDE, :
            ].reshape(256, WIDTH)

    @pl.when(upper)
    def _():
        fill(0, 3)

    @pl.when(jnp.logical_not(upper))
    def _():
        fill(1, 2)

    pair_ref[512:528, :] = (tiles[0] + tiles[1] + tiles[2] + tiles[3]).astype(BF)
    pair_ref[528:544, :] = (tiles[4] + tiles[5] + tiles[6] + tiles[7]).astype(BF)


def pair_kernel(i_ref, r_ref, x_ref, o_ref):
    upper = (i_ref[0] // 8) % 2 == 1

    def own(tensor):
        return r_ref[:, tensor * SIDE : (tensor + 1) * SIDE, :].reshape(256, WIDTH)

    def put(tensor, part):
        o_ref[:, tensor * SIDE : (tensor + 1) * SIDE, :] = part.reshape(RING, SIDE, WIDTH)

    def add(tensor, part):
        span = slice(tensor * SIDE, (tensor + 1) * SIDE)
        o_ref[:, span, :] = o_ref[:, span, :] + part.reshape(RING, SIDE, WIDTH)

    tiles = [r_ref[s, 4 * SIDE : CHUNK, :].astype(F32) for s in range(RING)]
    own_tile = jnp.concatenate(
        [tiles[0] + tiles[1] + tiles[2] + tiles[3], tiles[4] + tiles[5] + tiles[6] + tiles[7]],
        axis=1,
    )
    norm, delta = stat_pair(own_tile)
    query, key, value, grad = own(0), own(1), own(2), own(3)
    causal = iota((256, 256), 0) <= iota((256, 256), 1)
    probs, dscores = block_terms(query, key, value, grad, norm, delta, causal)
    put(0, dot_tn(dscores, key) * SCALE)
    put(1, dot(dscores, query) * SCALE)
    put(2, dot(probs, grad))

    @pl.when(upper)
    def _():
        far_key = x_ref[0:256, :]
        far_value = x_ref[256:512, :]
        _, dscores = block_terms(query, far_key, far_value, grad, norm, delta, None)
        add(0, dot_tn(dscores, far_key) * SCALE)

    @pl.when(jnp.logical_not(upper))
    def _():
        far_query = x_ref[0:256, :]
        far_grad = x_ref[256:512, :]
        far_tile = jnp.concatenate([x_ref[512:528, :], x_ref[528:544, :]], axis=1).astype(F32)
        far_norm, far_delta = stat_pair(far_tile)
        probs, dscores = block_terms(far_query, key, value, far_grad, far_norm, far_delta, None)
        add(1, dot(dscores, far_query) * SCALE)
        add(2, dot(probs, far_grad))


def plane_kernel(i_ref, r_ref, after_pair, o_ref):
    index = i_ref[0]
    row = index // 128
    layer = (index // 8) % DEPTH
    held = r_ref[...].astype(F32)
    query, key, value, grad = [
        held[:, tensor * 8 : (tensor + 1) * 8, :].reshape(128, WIDTH) for tensor in range(4)
    ]
    tile = jnp.sum(held[:, 32:48, :], axis=0).astype(BF)
    depth = iota((128, WIDTH), 0) // RING
    for target in range(ROWS):
        cut = jnp.where(row < target, DEPTH, jnp.where(row == target, layer, 0))
        earlier = depth < cut
        o_ref[target, 0:128, :] = jnp.where(earlier, key, query).astype(BF)
        o_ref[target, 128:256, :] = jnp.where(earlier, value, grad).astype(BF)
        o_ref[target, 256:PLANE, :] = tile


def join_kernel(i_ref, f_ref, m_ref, n_ref, after, o_ref, sums, wide):
    index = i_ref[0]
    row = index // 128
    layer = (index // 8) % DEPTH
    place = index % RING
    here = row * DEPTH + layer
    sums[...] = n_ref[...]
    mine_all = m_ref[0].astype(F32)
    mine = [mine_all[tensor * 8 : (tensor + 1) * 8] for tensor in range(4)]
    stat_rows = [f_ref[y, 256:PLANE, :].astype(F32) for y in range(ROWS)]
    norm_row, delta_row = stat_pair(jnp.concatenate(stat_rows, axis=1))
    chosen = iota((8, 512), 1) == here * RING + iota((8, 512), 0)
    norm_column = jnp.sum(jnp.where(chosen, norm_row, 0.0), axis=1, keepdims=True)
    delta_column = jnp.sum(jnp.where(chosen, delta_row, 0.0), axis=1, keepdims=True)
    on_tail = iota((8, 128), 1) == 8 + iota((8, 128), 0)
    norm_tail = jnp.sum(jnp.where(on_tail, norm_column, 0.0), axis=0, keepdims=True)
    delta_tail = jnp.sum(jnp.where(on_tail, delta_column, 0.0), axis=0, keepdims=True)
    pad = jnp.zeros((112, WIDTH), F32)
    near_a = jnp.concatenate([mine[1], mine[0], pad], axis=0).astype(BF)
    near_b = jnp.concatenate([mine[2], mine[3], pad], axis=0).astype(BF)
    all_a = jnp.concatenate([f_ref[y, 0:128, :] for y in range(ROWS)] + [near_a], axis=0)
    all_b = jnp.concatenate([f_ref[y, 128:256, :] for y in range(ROWS)] + [near_b], axis=0)
    left = jnp.concatenate([mine[0], mine[1]], axis=0).astype(BF)
    right = jnp.concatenate([mine[3], mine[2]], axis=0).astype(BF)
    scores = dot_nt(left, all_a) * SCALE
    dprobs = dot_nt(right, all_b)
    norm_wide = jnp.concatenate([norm_row, norm_tail], axis=1)
    delta_wide = jnp.concatenate([delta_row, delta_tail], axis=1)
    norms = jnp.concatenate(
        [jnp.broadcast_to(norm_column, (8, 640)), jnp.broadcast_to(norm_wide, (8, 640))], axis=0
    )
    deltas = jnp.concatenate(
        [jnp.broadcast_to(delta_column, (8, 640)), jnp.broadcast_to(delta_wide, (8, 640))], axis=0
    )
    lane = iota((16, 640), 1)
    seat = iota((16, 640), 0)
    source = lane // RING
    tail = lane - 512
    low = jnp.where(lane < 512, source, jnp.where(tail < 8, here - 1 + (tail > seat), 1 << 20))
    high = jnp.where(
        lane < 512, source, jnp.where((tail >= 8) & (tail < 16), here + 1 - (tail < seat), -1)
    )
    valid = ((seat < 8) & (low < here)) | ((seat >= 8) & (high > here))
    probs = jnp.where(valid, jnp.exp(jnp.where(valid, scores - norms, 0.0)), 0.0)
    dscores = (probs * (dprobs - deltas)).astype(BF)
    wide[0:16, :] = dot(dscores, all_a) * SCALE
    wide[16:32, :] = dot(probs.astype(BF), all_b)
    for s in range(RING):
        for tensor, at in ((0, s), (1, 8 + s), (2, 24 + s)):
            span = pl.ds(tensor * SIDE + place // 4, 1)
            sums[s, span, :] = sums[s, span, :] + wide[at : at + 1, :]
    o_ref[...] = sums[...].astype(BF)


def post_kernel(r_ref, dq, dk, dv, q_ref, k_ref, v_ref):
    for tensor, (near, ref) in enumerate(((dq, q_ref), (dk, k_ref), (dv, v_ref))):
        for head in range(HEADS):
            residue = head % 4
            back = (iota((TOK, SIDE), 0) == 4 * iota((TOK, SIDE), 1) + residue).astype(BF)
            part = dot(back, r_ref[head, tensor * SIDE : (tensor + 1) * SIDE, :])
            ref[:, columns_of(head)] = (near[:, columns_of(head)] + part).astype(BF)


def call(kernel, name, out, specs, scratch=(), flops=0, moved=0, places=None, limit=16):
    return pl.pallas_call(
        kernel,
        name=name,
        out_shape=out,
        in_specs=specs,
        out_specs=jax.tree.map(lambda _: VMEM, out) if places is None else places,
        scratch_shapes=list(scratch),
        cost_estimate=pl.CostEstimate(flops=flops, bytes_accessed=moved, transcendentals=0),
        compiler_params=pltpu.CompilerParams(vmem_limit_bytes=limit * 1024 * 1024),
    )


def shape(dims, dtype=BF):
    return jax.ShapeDtypeStruct(dims, dtype)


RING_GROUPS = [[base + i for i in range(RING)] for base in range(0, DEVICES, RING)]
DEPTH_GROUPS = [
    [y * 128 + z * 8 + i for z in range(DEPTH)] for y in range(ROWS) for i in range(RING)
]
ROW_GROUPS = [[y * 128 + i for y in range(ROWS)] for i in range(128)]


def exchange(array, groups):
    return lax.all_to_all(array, "seq", 0, 0, axis_index_groups=groups, tiled=True)


def partner(array, bit):
    return lax.ppermute(array, "seq", [(i, i ^ bit) for i in range(DEVICES)])


def body(query_rows, key_rows, value_rows, attn_out, out_grad, log_norms):
    index = lax.axis_index("seq").astype(jnp.int32).reshape(1)
    whole = (TOK, HEADS * WIDTH)
    side, stats = call(
        select_kernel,
        "select_rows",
        (shape((HEADS, CHUNK, WIDTH)), shape((16, HEADS * WIDTH))),
        [SMEM] + [ANY] * 6,
        [pltpu.VMEM(whole, BF)] * 5
        + [pltpu.VMEM((HEADS, TOK), F32), pltpu.SemaphoreType.DMA((6,))],
        flops=2 * 128 * 128 * 4096,
        moved=3 << 20,
        limit=60,
    )(index, query_rows, key_rows, value_rows, out_grad, attn_out, log_norms)
    side = exchange(side, RING_GROUPS)
    core, chip = call(
        payload_kernel,
        "near_payload",
        (shape((NEAR, HEADS * WIDTH)), shape((NEAR, HEADS * WIDTH))),
        [SMEM] + [ANY] * 5,
        [pltpu.SemaphoreType.DMA((2, 3))],
        moved=4 << 20,
        places=(ANY, ANY),
    )(index, query_rows, key_rows, value_rows, out_grad, stats)
    core = partner(core, 1)
    chip = partner(chip, 2)
    relay = partner(chip, 1)
    far, pair = call(
        middle_kernel,
        "middle_rows",
        (shape((DEPTH, FAR, WIDTH)), shape((PAIR, WIDTH))),
        [SMEM, VMEM],
        [pltpu.VMEM((128, 128), F32)],
        moved=1 << 20,
    )(index, side)
    mine = far
    far = exchange(far, DEPTH_GROUPS)
    pair = partner(pair, 8)
    sums = call(
        pair_kernel,
        "pair_grads",
        shape((RING, OUT_CHUNK, WIDTH), F32),
        [SMEM, VMEM, VMEM],
        flops=2 * 10 * 128 * 256 * 256,
        moved=1 << 20,
    )(index, side, pair)
    plane = call(
        plane_kernel,
        "plane_rows",
        shape((ROWS, PLANE, WIDTH)),
        [SMEM, VMEM, ANY],
        moved=1 << 20,
    )(index, far, sums)
    near = shape(whole, F32)
    near_grads = call(
        near_kernel,
        "near_grads",
        (near, near, near),
        [SMEM] + [VMEM] * 8 + [ANY],
        flops=2 * 128 * 128 * 128 * 8 * 17,
        moved=6 << 20,
    )(index, query_rows, key_rows, value_rows, out_grad, stats, core, chip, relay, plane)
    plane = exchange(plane, ROW_GROUPS)
    grads = call(
        join_kernel,
        "join_grads",
        shape((RING, OUT_CHUNK, WIDTH)),
        [SMEM, VMEM, VMEM, VMEM, ANY],
        [pltpu.VMEM((RING, OUT_CHUNK, WIDTH), F32), pltpu.VMEM((128, 128), F32)],
        moved=1 << 20,
    )(index, plane, mine, sums, near_grads[0])
    grads = exchange(grads, RING_GROUPS)
    out = shape(whole)
    return call(
        post_kernel,
        "add_levels",
        (out, out, out),
        [VMEM] * 4,
        flops=2 * 128 * 32 * 3072,
        moved=4 << 20,
    )(grads, *near_grads)


def solution(mesh):
    return jax.shard_map(
        body,
        mesh=mesh,
        in_specs=(
            P("seq", None),
            P("seq", None),
            P("seq", None),
            P("seq", None),
            P("seq", None),
            P(None, "seq"),
        ),
        out_specs=(P("seq", None), P("seq", None), P("seq", None)),
        check_vma=False,
    )
```

time: 94.7 us -> 74.3 us (0.78)
  blocking collectives: 43.1 us -> 11 us
  starting transfers between devices: 18.2 us -> 37 us
  waiting for transfers between devices: 19.8 us -> 7 us
  Pallas kernels: 6.97 us -> 15.4 us
  local copies, waits for them, and re-layouts: 5.43 us -> 2.43 us
    all_to_all x2 -> x1, blocking collectives: 43.1 us -> 11 us  [exchange(): lax.all_to_all(array, 'seq', 0, 0, axis_index_groups=groups, tiled=True)]
    all_to_all x2 -> x3, waiting for transfers between devices: 17.1 us -> 1.71 us  [exchange(): lax.all_to_all(array, 'seq', 0, 0, axis_index_groups=groups, tiled=True)]
    all_to_all x2 -> x3, starting transfers between devices: 15.2 us -> 25 us  [exchange(): lax.all_to_all(array, 'seq', 0, 0, axis_index_groups=groups, tiled=True)]
    ppermute x1 -> x4, starting transfers between devices: 2.93 us -> 12 us  [partner(): return lax.ppermute(array, 'seq', [(i, i ^ bit) for i in range(DEVICES)])]
    pallas_call x5 -> x7, Pallas kernels: 5.39 us -> 14.1 us  [the longest x1 6.44 us: body(): call(near_kernel, 'near_grads', (near, near, near), [SMEM] + [VMEM] * 8 +...]
    unnamed x12 -> x20, local copies, waits for them, and re-layouts: 5.43 us -> 2.43 us
    ppermute x1 -> x4, waiting for transfers between devices: 2.67 us -> 5.29 us  [partner(): return lax.ppermute(array, 'seq', [(i, i ^ bit) for i in range(DEVICES)])]
  transfers between devices with their start and end apart: 3 -> 7, of which waited for: 3 -> 2; matrix products, arithmetic and copies ran while one was open for 0% -> 0% of each run, Pallas kernels for 3% -> 13%
where the time goes in v2:
time: 74.3 us; the launch traced here: 73.7 us
  starting transfers between devices  37 us (50%)
  Pallas kernels  15.4 us (21%)
  blocking collectives  11 us (15%)
  waiting for transfers between devices  7 us (9%)
  local copies, waits for them, and re-layouts  2.43 us (3%)
  between operations  0.82 us (1%)
    all_to_all x3, starting transfers between devices, exchange(): lax.all_to_all(array, 'seq', 0, 0, axis_index_groups=groups, tiled=True)  25 us
    ppermute x4, starting transfers between devices, partner(): return lax.ppermute(array, 'seq', [(i, i ^ bit) for i in range(DEVICES)])  12 us
    all_to_all x1, blocking collectives, exchange(): lax.all_to_all(array, 'seq', 0, 0, axis_index_groups=groups, tiled=True)  11 us
    pallas_call x1, Pallas kernels, body(): call(near_kernel, 'near_grads', (near, near, near), [SMEM] + [VMEM] * 8 +...  6.44 us
    ppermute x4, waiting for transfers between devices, partner(): return lax.ppermute(array, 'seq', [(i, i ^ bit) for i in range(DEVICES)])  5.29 us
    pallas_call x1, Pallas kernels, body(): call(select_kernel, 'select_rows', (shape((HEADS, CHUNK, WIDTH)), shape((...  3.03 us
    unnamed x20, local copies, waits for them, and re-layouts  2.43 us
    all_to_all x3, waiting for transfers between devices, exchange(): lax.all_to_all(array, 'seq', 0, 0, axis_index_groups=groups, tiled=True)  1.71 us
  transfers between devices with their start and end apart: 7, of which 2 were waited for; matrix products, arithmetic and copies ran while one was open for 0% of the time, Pallas kernels for 13%

profile of v2, /device:TPU:1, one launch (start us, length us, event | category | flops | bytes accessed | tf_op | source)
XLA Modules:
  0.0 73.7 jit_solution(204543609630287667)
XLA Ops:
  0.6 0.0 copy-start.2
  0.6 0.0 copy-start.3
  0.7 3.0 %select_rows.1 = (bf16[8,144,128]{2,1,0:T(8,128)(2,1)}, bf16[16,1024]{1,0:T(8,128)(2,1)}) custom-call(s32[1]{0:T(128)} %bitcast.i_ref, bf16[128,1024]{1,0:T(8,128)(2,1)} %q.1, bf16[128,1024]{1,0:T(8,128)(2,1)} %k.1, bf16[128,1024]{1,0:T(8,128)(2,1)} %v.1, bf16[128,1024]{1,0:T(8,128)(2,1)} %g.1, bf16[128,1024]{1,0:T(8,128)(2,1)} %o_in.1, f32[8,128]{1,0:T(8,128)} %n_in.1), custom_call_target="tpu_custom_call" | custom-call | flops 134217728 | bytes 3145728 | tf_op jit(solution)/shard_map/select_rows/pallas_call | solution.py:400
  3.7 0.0 copy-start
  3.7 0.0 copy-start.1
  3.7 0.0 copy-start.8
  3.7 10.3 %all-to-all-start = ((bf16[8,144,128]{2,1,0:T(8,128)(2,1)}), bf16[8,144,128]{2,1,0:T(8,128)(2,1)S(1)}, u32[]{:S(2)}, u32[]{:S(2)}) async-start(bf16[8,144,128]{2,1,0:T(8,128)(2,1)} %get-tuple-element.12), calls=%async_computation | async-start | bytes 589824 | tf_op jit(solution)/shard_map/all_to_all | solution.py:390
  14.1 0.0 copy-done.2
  14.1 0.0 copy-done.3
  14.1 0.0 copy-done
  14.1 0.0 copy-done.1
  14.1 0.0 copy-done.8
  14.1 1.0 %near_payload.1 = (bf16[272,1024]{1,0:T(8,128)(2,1)S(1)}, bf16[272,1024]{1,0:T(8,128)(2,1)}) custom-call(s32[1]{0:T(128)} %bitcast.i_ref, bf16[128,1024]{1,0:T(8,128)(2,1)S(1)} %copy-done, bf16[128,1024]{1,0:T(8,128)(2,1)S(1)} %copy-done.1, bf16[128,1024]{1,0:T(8,128)(2,1)S(1)} %copy-done.2, bf16[128,1024]{1,0:T(8,128)(2,1)S(1)} %copy-done.3, ...), custom_call_target="tpu_custom_call" | custom-call | bytes 4194304 | tf_op jit(solution)/shard_map/near_payload/pallas_call | solution.py:412
  15.1 0.0 copy-start.9
  15.1 0.8 %copy-done.9 = bf16[272,1024]{1,0:T(8,128)(2,1)} copy-done((bf16[272,1024]{1,0:T(8,128)(2,1)}, bf16[272,1024]{1,0:T(8,128)(2,1)S(1)}, u32[]{:S(2)}) %copy-start.9) | copy-done | bytes 557080
  15.9 3.3 %collective-permute-start.2 = (bf16[272,1024]{1,0:T(8,128)(2,1)}, bf16[272,1024]{1,0:T(8,128)(2,1)S(1)}, u32[]{:S(2)}, u32[]{:S(2)}) collective-permute-start(bf16[272,1024]{1,0:T(8,128)(2,1)} %get-tuple-element.17), channel_id=1, source_target_pairs={{0,2},{1,3},{2,0},{3,1},{4,6},{5,7},{6,4},{7,5},{8,10},{9,11},{10,... | collective-permute-start | bytes 1671176 | tf_op jit(solution)/shard_map/ppermute | solution.py:394
  19.2 1.7 %all-to-all-done.r_ref = bf16[8,144,128]{2,1,0:T(8,128)(2,1)S(1)} async-done(((bf16[8,144,128]{2,1,0:T(8,128)(2,1)}), bf16[8,144,128]{2,1,0:T(8,128)(2,1)S(1)}, u32[]{:S(2)}, u32[]{:S(2)}) %all-to-all-start) | async-done | bytes 294944 | tf_op jit(solution)/shard_map/all_to_all | solution.py:390
  20.9 0.8 %middle_rows.1 = (bf16[16,48,128]{2,1,0:T(8,128)(2,1)}, bf16[544,128]{1,0:T(8,128)(2,1)S(1)}) custom-call(s32[1]{0:T(128)} %bitcast.i_ref, bf16[8,144,128]{2,1,0:T(8,128)(2,1)S(1)} %all-to-all-done.r_ref), custom_call_target="tpu_custom_call" | custom-call | bytes 1048576 | tf_op jit(solution)/shard_map/middle_rows/pallas_call | solution.py:424
  21.7 10.5 %all-to-all-start.1 = ((bf16[16,48,128]{2,1,0:T(8,128)(2,1)}), bf16[16,48,128]{2,1,0:T(8,128)(2,1)S(1)}, u32[]{:S(2)}, u32[]{:S(2)}) async-start(bf16[16,48,128]{2,1,0:T(8,128)(2,1)} %get-tuple-element.13.m_ref), calls=%async_computation.1 | async-start | bytes 393216 | tf_op jit(solution)/shard_map/all_to_all | solution.py:390
  32.2 3.3 %collective-permute-start.1 = (bf16[272,1024]{1,0:T(8,128)(2,1)}, bf16[272,1024]{1,0:T(8,128)(2,1)S(1)}, u32[]{:S(2)}, u32[]{:S(2)}) collective-permute-start(bf16[272,1024]{1,0:T(8,128)(2,1)} %copy-done.9), channel_id=1, source_target_pairs={{0,1},{1,0},{2,3},{3,2},{4,5},{5,4},{6,7},{7,6},{8,9},{9,8},{10,11... | collective-permute-start | bytes 1671176 | tf_op jit(solution)/shard_map/ppermute | solution.py:394
  35.5 0.0 collective-permute-done.2.r2
  35.5 1.9 %collective-permute-start.3 = (bf16[272,1024]{1,0:T(8,128)(2,1)S(1)}, bf16[272,1024]{1,0:T(8,128)(2,1)}, u32[]{:S(2)}, u32[]{:S(2)}) collective-permute-start(bf16[272,1024]{1,0:T(8,128)(2,1)S(1)} %collective-permute-done.2.r2), channel_id=1, source_target_pairs={{0,1},{1,0},{2,3},{3,2},{4,5},{5,4},{6,7},{7,6},{8,9},{9,8},{10,11... | collective-permute-start | bytes 1671176 | tf_op jit(solution)/shard_map/ppermute | solution.py:394
  37.4 3.5 %collective-permute-start = (bf16[544,128]{1,0:T(8,128)(2,1)S(1)}, bf16[544,128]{1,0:T(8,128)(2,1)S(1)}, u32[]{:S(2)}, u32[]{:S(2)}) collective-permute-start(bf16[544,128]{1,0:T(8,128)(2,1)S(1)} %get-tuple-element.14), channel_id=1, source_target_pairs={{0,8},{1,9},{2,10},{3,11},{4,12},{5,13},{6,14},{7,15},{8,0},{9,1},... | collective-permute-start | bytes 417800 | tf_op jit(solution)/shard_map/ppermute | solution.py:394
  41.0 5.3 %collective-permute-done.x_ref = bf16[544,128]{1,0:T(8,128)(2,1)S(1)} collective-permute-done((bf16[544,128]{1,0:T(8,128)(2,1)S(1)}, bf16[544,128]{1,0:T(8,128)(2,1)S(1)}, u32[]{:S(2)}, u32[]{:S(2)}) %collective-permute-start) | collective-permute-done | bytes 139296 | tf_op jit(solution)/shard_map/ppermute | solution.py:394
  46.3 0.9 %pair_grads.1.after_pair.n_ref = f32[8,96,128]{2,1,0:T(8,128)S(1)} custom-call(s32[1]{0:T(128)} %bitcast.i_ref, bf16[8,144,128]{2,1,0:T(8,128)(2,1)S(1)} %all-to-all-done.r_ref, bf16[544,128]{1,0:T(8,128)(2,1)S(1)} %collective-permute-done.x_ref), custom_call_target="tpu_custom_call" | custom-call | flops 167772160 | bytes 1048576 | tf_op jit(solution)/shard_map/pair_grads/pallas_call | solution.py:435
  47.2 0.0 all-to-all-done.1.r_ref
  47.2 0.8 %plane_rows.1.after = bf16[4,272,128]{2,1,0:T(8,128)(2,1)} custom-call(s32[1]{0:T(128)} %bitcast.i_ref, bf16[16,48,128]{2,1,0:T(8,128)(2,1)S(1)} %all-to-all-done.1.r_ref, f32[8,96,128]{2,1,0:T(8,128)S(1)} %pair_grads.1.after_pair.n_ref), custom_call_target="tpu_custom_call" | custom-call | bytes 1048576 | tf_op jit(solution)/shard_map/plane_rows/pallas_call | solution.py:443
  48.0 4.2 %all-to-all-start.2 = ((bf16[4,272,128]{2,1,0:T(8,128)(2,1)}), bf16[4,272,128]{2,1,0:T(8,128)(2,1)S(1)}, u32[]{:S(2)}, u32[]{:S(2)}) async-start(bf16[4,272,128]{2,1,0:T(8,128)(2,1)} %plane_rows.1.after), calls=%async_computation.2 | async-start | bytes 557056 | tf_op jit(solution)/shard_map/all_to_all | solution.py:390
  52.2 0.0 collective-permute-done.1.r1
  52.2 0.0 collective-permute-done.3.r3
  52.2 6.4 %near_grads.1 = (f32[128,1024]{1,0:T(8,128)S(1)}, f32[128,1024]{1,0:T(8,128)S(1)}, f32[128,1024]{1,0:T(8,128)S(1)}) custom-call(s32[1]{0:T(128)} %bitcast.i_ref, bf16[128,1024]{1,0:T(8,128)(2,1)S(1)} %copy-done, bf16[128,1024]{1,0:T(8,128)(2,1)S(1)} %copy-done.1, bf16[128,1024]{1,0:T(8,128)(2,1)S(1)} %copy-done.2, bf16[128,1024]{1,0:T(8,128)(2,1)S(1)} %copy-done.3, ...), custom_call_target="tpu_custom_call" | custom-call | flops 570425344 | bytes 6291456 | tf_op jit(solution)/shard_map/near_grads/pallas_call | solution.py:451
  58.6 0.0 copy-start.4
  58.6 0.8 %copy-done.4 = f32[128,1024]{1,0:T(8,128)} copy-done((f32[128,1024]{1,0:T(8,128)}, f32[128,1024]{1,0:T(8,128)S(1)}, u32[]{:S(2)}) %copy-start.4) | copy-done | bytes 524312
  59.4 0.0 copy-start.6
  59.4 0.8 %copy-done.6 = f32[128,1024]{1,0:T(8,128)} copy-done((f32[128,1024]{1,0:T(8,128)}, f32[128,1024]{1,0:T(8,128)S(1)}, u32[]{:S(2)}) %copy-start.6) | copy-done | bytes 524312
  60.2 0.0 all-to-all-done.2.f_ref
  60.2 0.0 copy-start.5
  60.2 0.0 copy-start.7
  60.2 1.4 %join_grads.1 = bf16[8,96,128]{2,1,0:T(8,128)(2,1)S(1)} custom-call(s32[1]{0:T(128)} %bitcast.i_ref, bf16[4,272,128]{2,1,0:T(8,128)(2,1)S(1)} %all-to-all-done.2.f_ref, bf16[16,48,128]{2,1,0:T(8,128)(2,1)} %get-tuple-element.13.m_ref, f32[8,96,128]{2,1,0:T(8,128)S(1)} %pair_grads.1.after_pair.n_ref, f32[128,1024]{1,0:T(8,128)S(1)} %get-tuple-element.18.after.dq), custom_call_target="tpu_custom_call" | custom-call | bytes 1048576 | tf_op jit(solution)/shard_map/join_grads/pallas_call | solution.py:460
  61.6 11.0 %all_to_all.20.r_ref = bf16[8,96,128]{2,1,0:T(8,128)(2,1)S(1)} all-to-all(bf16[8,96,128]{2,1,0:T(8,128)(2,1)S(1)} %join_grads.1), channel_id=1, replica_groups={{0,1,2,3,4,5,6,7},{8,9,10,11,12,13,14,15},{16,17,18,19,20,21,22,23},{24..., dimensions={0} | all-to-all | bytes 393216 | tf_op jit(solution)/shard_map/all_to_all | solution.py:390
  72.6 0.0 copy-done.5
  72.6 0.0 copy-done.7
  72.6 1.1 %add_levels.1 = (bf16[128,1024]{1,0:T(8,128)(2,1)}, bf16[128,1024]{1,0:T(8,128)(2,1)}, bf16[128,1024]{1,0:T(8,128)(2,1)}) custom-call(bf16[8,96,128]{2,1,0:T(8,128)(2,1)S(1)} %all_to_all.20.r_ref, f32[128,1024]{1,0:T(8,128)S(1)} %get-tuple-element.18.after.dq, f32[128,1024]{1,0:T(8,128)S(1)} %copy-done.5, f32[128,1024]{1,0:T(8,128)S(1)} %copy-done.7), custom_call_target="tpu_custom_call" | custom-call | flops 25165824 | bytes 4194304 | tf_op jit(solution)/shard_map/add_levels/pallas_call | solution.py:470
Async XLA Ops:
  0.6 13.4 %copy-start.2 = (bf16[128,1024]{1,0:T(8,128)(2,1)S(1)}, bf16[128,1024]{1,0:T(8,128)(2,1)}, u32[]{:S(2)}) copy-start(bf16[128,1024]{1,0:T(8,128)(2,1)} %v.1) | copy-start | bytes 786436
  0.6 13.4 %copy-start.3 = (bf16[128,1024]{1,0:T(8,128)(2,1)S(1)}, bf16[128,1024]{1,0:T(8,128)(2,1)}, u32[]{:S(2)}) copy-start(bf16[128,1024]{1,0:T(8,128)(2,1)} %g.1) | copy-start | bytes 786436
  3.7 10.4 %copy-start = (bf16[128,1024]{1,0:T(8,128)(2,1)S(1)}, bf16[128,1024]{1,0:T(8,128)(2,1)}, u32[]{:S(2)}) copy-start(bf16[128,1024]{1,0:T(8,128)(2,1)} %q.1) | copy-start | bytes 786436
  3.7 10.4 %copy-start.1 = (bf16[128,1024]{1,0:T(8,128)(2,1)S(1)}, bf16[128,1024]{1,0:T(8,128)(2,1)}, u32[]{:S(2)}) copy-start(bf16[128,1024]{1,0:T(8,128)(2,1)} %k.1) | copy-start | bytes 786436
  3.7 10.4 %copy-start.8 = (bf16[16,1024]{1,0:T(8,128)(2,1)S(1)}, bf16[16,1024]{1,0:T(8,128)(2,1)}, u32[]{:S(2)}) copy-start(bf16[16,1024]{1,0:T(8,128)(2,1)} %get-tuple-element.15.s_in.s) | copy-start | bytes 98308
  3.7 17.2 %all-to-all-start = ((bf16[8,144,128]{2,1,0:T(8,128)(2,1)}), bf16[8,144,128]{2,1,0:T(8,128)(2,1)S(1)}, u32[]{:S(2)}, u32[]{:S(2)}) async-start(bf16[8,144,128]{2,1,0:T(8,128)(2,1)} %get-tuple-element.12), calls=%async_computation | async-start | bytes 589824 | tf_op jit(solution)/shard_map/all_to_all | solution.py:390
  15.1 0.8 %copy-start.9 = (bf16[272,1024]{1,0:T(8,128)(2,1)}, bf16[272,1024]{1,0:T(8,128)(2,1)S(1)}, u32[]{:S(2)}) copy-start(bf16[272,1024]{1,0:T(8,128)(2,1)S(1)} %get-tuple-element.16) | copy-start | bytes 1671172
  15.9 19.6 %collective-permute-start.2 = (bf16[272,1024]{1,0:T(8,128)(2,1)}, bf16[272,1024]{1,0:T(8,128)(2,1)S(1)}, u32[]{:S(2)}, u32[]{:S(2)}) collective-permute-start(bf16[272,1024]{1,0:T(8,128)(2,1)} %get-tuple-element.17), channel_id=1, source_target_pairs={{0,2},{1,3},{2,0},{3,1},{4,6},{5,7},{6,4},{7,5},{8,10},{9,11},{10,... | collective-permute-start | bytes 1671176 | tf_op jit(solution)/shard_map/ppermute | solution.py:394
  21.7 25.5 %all-to-all-start.1 = ((bf16[16,48,128]{2,1,0:T(8,128)(2,1)}), bf16[16,48,128]{2,1,0:T(8,128)(2,1)S(1)}, u32[]{:S(2)}, u32[]{:S(2)}) async-start(bf16[16,48,128]{2,1,0:T(8,128)(2,1)} %get-tuple-element.13.m_ref), calls=%async_computation.1 | async-start | bytes 393216 | tf_op jit(solution)/shard_map/all_to_all | solution.py:390
  32.2 20.0 %collective-permute-start.1 = (bf16[272,1024]{1,0:T(8,128)(2,1)}, bf16[272,1024]{1,0:T(8,128)(2,1)S(1)}, u32[]{:S(2)}, u32[]{:S(2)}) collective-permute-start(bf16[272,1024]{1,0:T(8,128)(2,1)} %copy-done.9), channel_id=1, source_target_pairs={{0,1},{1,0},{2,3},{3,2},{4,5},{5,4},{6,7},{7,6},{8,9},{9,8},{10,11... | collective-permute-start | bytes 1671176 | tf_op jit(solution)/shard_map/ppermute | solution.py:394
  35.5 16.7 %collective-permute-start.3 = (bf16[272,1024]{1,0:T(8,128)(2,1)S(1)}, bf16[272,1024]{1,0:T(8,128)(2,1)}, u32[]{:S(2)}, u32[]{:S(2)}) collective-permute-start(bf16[272,1024]{1,0:T(8,128)(2,1)S(1)} %collective-permute-done.2.r2), channel_id=1, source_target_pairs={{0,1},{1,0},{2,3},{3,2},{4,5},{5,4},{6,7},{7,6},{8,9},{9,8},{10,11... | collective-permute-start | bytes 1671176 | tf_op jit(solution)/shard_map/ppermute | solution.py:394
  37.4 8.8 %collective-permute-start = (bf16[544,128]{1,0:T(8,128)(2,1)S(1)}, bf16[544,128]{1,0:T(8,128)(2,1)S(1)}, u32[]{:S(2)}, u32[]{:S(2)}) collective-permute-start(bf16[544,128]{1,0:T(8,128)(2,1)S(1)} %get-tuple-element.14), channel_id=1, source_target_pairs={{0,8},{1,9},{2,10},{3,11},{4,12},{5,13},{6,14},{7,15},{8,0},{9,1},... | collective-permute-start | bytes 417800 | tf_op jit(solution)/shard_map/ppermute | solution.py:394
  48.0 12.2 %all-to-all-start.2 = ((bf16[4,272,128]{2,1,0:T(8,128)(2,1)}), bf16[4,272,128]{2,1,0:T(8,128)(2,1)S(1)}, u32[]{:S(2)}, u32[]{:S(2)}) async-start(bf16[4,272,128]{2,1,0:T(8,128)(2,1)} %plane_rows.1.after), calls=%async_computation.2 | async-start | bytes 557056 | tf_op jit(solution)/shard_map/all_to_all | solution.py:390
  58.6 0.8 %copy-start.4 = (f32[128,1024]{1,0:T(8,128)}, f32[128,1024]{1,0:T(8,128)S(1)}, u32[]{:S(2)}) copy-start(f32[128,1024]{1,0:T(8,128)S(1)} %get-tuple-element.19.dk) | copy-start | bytes 1572868
  59.4 0.8 %copy-start.6 = (f32[128,1024]{1,0:T(8,128)}, f32[128,1024]{1,0:T(8,128)S(1)}, u32[]{:S(2)}) copy-start(f32[128,1024]{1,0:T(8,128)S(1)} %get-tuple-element.20.dv) | copy-start | bytes 1572868
  60.2 12.3 %copy-start.5 = (f32[128,1024]{1,0:T(8,128)S(1)}, f32[128,1024]{1,0:T(8,128)}, u32[]{:S(2)}) copy-start(f32[128,1024]{1,0:T(8,128)} %copy-done.4) | copy-start | bytes 1572868
  60.2 12.3 %copy-start.7 = (f32[128,1024]{1,0:T(8,128)S(1)}, f32[128,1024]{1,0:T(8,128)}, u32[]{:S(2)}) copy-start(f32[128,1024]{1,0:T(8,128)} %copy-done.6) | copy-start | bytes 1572868

commit v3 on v2

--- a/solution.py
+++ b/solution.py
@@ -19,7 +19,7 @@
 CHUNK = 4 * SIDE + 16
 OUT_CHUNK = 3 * SIDE
 PAIR = 4 * 128 + 32
-FAR = 48
+FAR = 40
 PLANE = 2 * 128 + 16
 NEAR = 2 * TOK + 16
 
@@ -84,18 +84,27 @@
 
 
 def select_kernel(i_ref, q_in, k_in, v_in, g_in, o_in, n_in, out_ref, stat_ref, q, k, v, g, o, n, sems):
-    sources = (n_in, g_in, o_in, q_in, k_in, v_in)
-    places = (n, g, o, q, k, v)
-    copies = [
-        pltpu.make_async_copy(source, place, sems.at[number])
-        for number, (source, place) in enumerate(zip(sources, places))
-    ]
-    for copy in copies:
-        copy.start()
+    copies = [[pltpu.make_async_copy(n_in, n, sems.at[0, 0])]]
+    for number, (source, place) in enumerate(
+        ((g_in, g), (o_in, o), (q_in, q), (k_in, k), (v_in, v))
+    ):
+        copies.append(
+            [
+                pltpu.make_async_copy(
+                    source.at[pl.ds(part * 64, 64)],
+                    place.at[pl.ds(part * 64, 64)],
+                    sems.at[number + 1, part],
+                )
+                for part in range(2)
+            ]
+        )
+    for group in copies:
+        for copy in group:
+            copy.start()
     seat = i_ref[0] % RING
-    copies[0].wait()
-    copies[1].wait()
-    copies[2].wait()
+    for group in copies[0:3]:
+        for copy in group:
+            copy.wait()
     lane = iota((TOK, 128), 1)
     spread = jnp.zeros((TOK, 128), F32)
     for head in range(HEADS):
@@ -116,10 +125,10 @@
             out_ref[head, 4 * SIDE : CHUNK, :] = placed[head * 16 : (head + 1) * 16, :]
     order = iota((TOK, TOK), 0)
     perm = (4 * (order % SIDE) + order // SIDE == iota((TOK, TOK), 1)).astype(BF)
-    for tensor, (ref, copy) in enumerate(
-        ((q, copies[3]), (k, copies[4]), (v, copies[5]), (g, None))
+    for tensor, (ref, group) in enumerate(
+        ((q, copies[3]), (k, copies[4]), (v, copies[5]), (g, ()))
     ):
-        if copy is not None:
+        for copy in group:
             copy.wait()
         ordered = dot(perm, ref[...]).astype(BF)
         for head in range(HEADS):
@@ -154,52 +163,57 @@
             send(k_in, v_in)
 
 
-def near_kernel(i_ref, q, k, v, g, s, r1, r2, r3, after, dq, dk, dv):
-    index = i_ref[0]
-    core = (index & 1) == 1
-    chip = (index & 2) == 2
-    causal = iota((TOK, TOK), 0) <= iota((TOK, TOK), 1)
-    own_stats = [stat_pair(s[:, columns_of(head)].astype(F32)) for head in range(HEADS)]
-    for head in range(HEADS):
-        c = columns_of(head)
-        norm, delta = own_stats[head]
-        probs, dscores = block_terms(q[:, c], k[:, c], v[:, c], g[:, c], norm, delta, causal)
-        dq[:, c] = dot_tn(dscores, k[:, c]) * SCALE
-        dk[:, c] = dot(dscores, q[:, c]) * SCALE
-        dv[:, c] = dot(probs, g[:, c])
-
-    def from_keys(refs):
+def near_kernel(i_ref, q, k, v, g, s, r1, r2, r3, after, out_ref):
+    place = i_ref[0] % 4
+    stat_rows = [stat_pair(s[:, columns_of(head)].astype(F32)) for head in range(HEADS)]
+    stat_rows = [row[0] for row in stat_rows] + [row[1] for row in stat_rows]
+    stat_columns = jnp.concatenate(stat_rows + [jnp.zeros((112, TOK), F32)], axis=0).T
+    blocks = (r1, r2, r3)
+
+    def part(block, number, c):
+        return block[number * TOK : (TOK, 2 * TOK, NEAR)[number], c]
+
+    def terms(earlier, later):
         for head in range(HEADS):
             c = columns_of(head)
-            norm, delta = own_stats[head]
-            key = jnp.concatenate([ref[0:TOK, c] for ref in refs], axis=0)
-            value = jnp.concatenate([ref[TOK : 2 * TOK, c] for ref in refs], axis=0)
-            _, dscores = block_terms(q[:, c], key, value, g[:, c], norm, delta, None)
-            dq[:, c] = dq[:, c] + dot_tn(dscores, key) * SCALE
-
-    def from_queries(refs):
-        for head in range(HEADS):
-            c = columns_of(head)
-            query = jnp.concatenate([ref[0:TOK, c] for ref in refs], axis=0)
-            grad = jnp.concatenate([ref[TOK : 2 * TOK, c] for ref in refs], axis=0)
-            tile = jnp.concatenate([ref[2 * TOK : NEAR, c] for ref in refs], axis=1).astype(F32)
-            norm, delta = stat_pair(tile)
-            probs, dscores = block_terms(query, k[:, c], v[:, c], grad, norm, delta, None)
-            dk[:, c] = dk[:, c] + dot(dscores, query) * SCALE
-            dv[:, c] = dv[:, c] + dot(probs, grad)
-
-    for later, refs in ((core, (r1,)), (chip, (r2, r3))):
-
-        @pl.when(later)
-        def _(refs=refs):
-            from_keys(refs)
-
-        @pl.when(jnp.logical_not(later))
-        def _(refs=refs):
-            from_queries(refs)
-
-
-def middle_kernel(i_ref, r_ref, far_ref, pair_ref, flat):
+            query, grad = q[:, c], g[:, c]
+            key = jnp.concatenate([k[:, c]] + [part(block, 0, c) for block in earlier], axis=0)
+            value = jnp.concatenate([v[:, c]] + [part(block, 1, c) for block in earlier], axis=0)
+            size = key.shape[0]
+            norm = stat_columns[:, head : head + 1]
+            delta = stat_columns[:, HEADS + head : HEADS + head + 1]
+            lane = iota((TOK, size), 1)
+            mask = (lane <= iota((TOK, size), 0)) | (lane >= TOK)
+            probs = jnp.where(mask, jnp.exp(dot_nt(query, key) * SCALE - norm), 0.0)
+            dscores = (probs * (dot_nt(grad, value) - delta)).astype(BF)
+            out_ref[0, :, c] = (dot(dscores, key) * SCALE).astype(BF)
+            key_grad = dot_tn(dscores[:, 0:TOK], query)
+            value_grad = dot_tn(probs[:, 0:TOK].astype(BF), grad)
+            if later:
+                query = jnp.concatenate([part(block, 0, c) for block in later], axis=0)
+                grad = jnp.concatenate([part(block, 1, c) for block in later], axis=0)
+                tile = jnp.concatenate([part(block, 2, c) for block in later], axis=1)
+                norm, delta = stat_pair(tile.astype(F32))
+                probs, dscores = block_terms(query, k[:, c], v[:, c], grad, norm, delta, None)
+                key_grad = key_grad + dot(dscores, query)
+                value_grad = value_grad + dot(probs, grad)
+            out_ref[1, :, c] = (key_grad * SCALE).astype(BF)
+            out_ref[2, :, c] = value_grad.astype(BF)
+
+    cases = (
+        ((), (0, 1, 2)),
+        ((0,), (1, 2)),
+        ((1, 2), (0,)),
+        ((0, 1, 2), ()),
+    )
+    for number, (earlier, later) in enumerate(cases):
+
+        @pl.when(place == number)
+        def _(earlier=earlier, later=later):
+            terms([blocks[i] for i in earlier], [blocks[i] for i in later])
+
+
+def middle_kernel(i_ref, r_ref, far_ref, mine_ref, pair_ref, flat):
     index = i_ref[0]
     layer = (index // 8) % DEPTH
     place = index % RING
@@ -215,7 +229,8 @@
     for tensor in range(4):
         flat[...] = r_ref[:, tensor * SIDE : tensor * SIDE + 16, :].astype(F32).reshape(128, WIDTH)
         rows.append(flat[pl.ds(place // 4, RING, stride=16), :])
-    payload = jnp.concatenate(rows + [stats], axis=0).astype(BF)
+    payload = jnp.concatenate(rows + [stats[0:8]], axis=0).astype(BF)
+    mine_ref[...] = payload
     for target in range(DEPTH):
         far_ref[target] = payload
 
@@ -289,7 +304,8 @@
     query, key, value, grad = [
         held[:, tensor * 8 : (tensor + 1) * 8, :].reshape(128, WIDTH) for tensor in range(4)
     ]
-    tile = jnp.sum(held[:, 32:48, :], axis=0).astype(BF)
+    tile = jnp.sum(held[:, 32:FAR, :], axis=0)
+    tile = jnp.concatenate([tile, jnp.zeros((8, 128), F32)], axis=0).astype(BF)
     depth = iota((128, WIDTH), 0) // RING
     for target in range(ROWS):
         cut = jnp.where(row < target, DEPTH, jnp.where(row == target, layer, 0))
@@ -299,14 +315,14 @@
         o_ref[target, 256:PLANE, :] = tile
 
 
-def join_kernel(i_ref, f_ref, m_ref, n_ref, after, o_ref, sums, wide):
+def join_kernel(i_ref, f_ref, m_ref, n_ref, o_ref, sums, wide):
     index = i_ref[0]
     row = index // 128
     layer = (index // 8) % DEPTH
     place = index % RING
     here = row * DEPTH + layer
     sums[...] = n_ref[...]
-    mine_all = m_ref[0].astype(F32)
+    mine_all = m_ref[...].astype(F32)
     mine = [mine_all[tensor * 8 : (tensor + 1) * 8] for tensor in range(4)]
     stat_rows = [f_ref[y, 256:PLANE, :].astype(F32) for y in range(ROWS)]
     norm_row, delta_row = stat_pair(jnp.concatenate(stat_rows, axis=1))
@@ -353,13 +369,13 @@
     o_ref[...] = sums[...].astype(BF)
 
 
-def post_kernel(r_ref, dq, dk, dv, q_ref, k_ref, v_ref):
-    for tensor, (near, ref) in enumerate(((dq, q_ref), (dk, k_ref), (dv, v_ref))):
+def post_kernel(r_ref, n_ref, q_ref, k_ref, v_ref):
+    for tensor, ref in enumerate((q_ref, k_ref, v_ref)):
         for head in range(HEADS):
             residue = head % 4
             back = (iota((TOK, SIDE), 0) == 4 * iota((TOK, SIDE), 1) + residue).astype(BF)
             part = dot(back, r_ref[head, tensor * SIDE : (tensor + 1) * SIDE, :])
-            ref[:, columns_of(head)] = (near[:, columns_of(head)] + part).astype(BF)
+            ref[:, columns_of(head)] = (n_ref[tensor, :, columns_of(head)].astype(F32) + part).astype(BF)
 
 
 def call(kernel, name, out, specs, scratch=(), flops=0, moved=0, places=None, limit=16):
@@ -403,7 +419,7 @@
         (shape((HEADS, CHUNK, WIDTH)), shape((16, HEADS * WIDTH))),
         [SMEM] + [ANY] * 6,
         [pltpu.VMEM(whole, BF)] * 5
-        + [pltpu.VMEM((HEADS, TOK), F32), pltpu.SemaphoreType.DMA((6,))],
+        + [pltpu.VMEM((HEADS, TOK), F32), pltpu.SemaphoreType.DMA((6, 2))],
         flops=2 * 128 * 128 * 4096,
         moved=3 << 20,
         limit=60,
@@ -421,15 +437,14 @@
     core = partner(core, 1)
     chip = partner(chip, 2)
     relay = partner(chip, 1)
-    far, pair = call(
+    far, mine, pair = call(
         middle_kernel,
         "middle_rows",
-        (shape((DEPTH, FAR, WIDTH)), shape((PAIR, WIDTH))),
+        (shape((DEPTH, FAR, WIDTH)), shape((FAR, WIDTH)), shape((PAIR, WIDTH))),
         [SMEM, VMEM],
         [pltpu.VMEM((128, 128), F32)],
         moved=1 << 20,
     )(index, side)
-    mine = far
     far = exchange(far, DEPTH_GROUPS)
     pair = partner(pair, 8)
     sums = call(
@@ -437,7 +452,7 @@
         "pair_grads",
         shape((RING, OUT_CHUNK, WIDTH), F32),
         [SMEM, VMEM, VMEM],
-        flops=2 * 10 * 128 * 256 * 256,
+        flops=8 * 2 * 10 * 128 * 256 * 256,
         moved=1 << 20,
     )(index, side, pair)
     plane = call(
@@ -447,34 +462,33 @@
         [SMEM, VMEM, ANY],
         moved=1 << 20,
     )(index, far, sums)
-    near = shape(whole, F32)
-    near_grads = call(
-        near_kernel,
-        "near_grads",
-        (near, near, near),
-        [SMEM] + [VMEM] * 8 + [ANY],
-        flops=2 * 128 * 128 * 128 * 8 * 17,
-        moved=6 << 20,
-    )(index, query_rows, key_rows, value_rows, out_grad, stats, core, chip, relay, plane)
     plane = exchange(plane, ROW_GROUPS)
     grads = call(
         join_kernel,
         "join_grads",
         shape((RING, OUT_CHUNK, WIDTH)),
-        [SMEM, VMEM, VMEM, VMEM, ANY],
+        [SMEM, VMEM, VMEM, VMEM],
         [pltpu.VMEM((RING, OUT_CHUNK, WIDTH), F32), pltpu.VMEM((128, 128), F32)],
         moved=1 << 20,
-    )(index, plane, mine, sums, near_grads[0])
+    )(index, plane, mine, sums)
+    near_grads = call(
+        near_kernel,
+        "near_grads",
+        shape((3, TOK, HEADS * WIDTH)),
+        [SMEM] + [VMEM] * 8 + [ANY],
+        flops=int(1 * 2 * 128 * 128 * 128 * 8 * 17),
+        moved=4 << 20,
+    )(index, query_rows, key_rows, value_rows, out_grad, stats, core, chip, relay, grads)
     grads = exchange(grads, RING_GROUPS)
     out = shape(whole)
     return call(
         post_kernel,
         "add_levels",
         (out, out, out),
-        [VMEM] * 4,
+        [VMEM] * 2,
         flops=2 * 128 * 32 * 3072,
         moved=4 << 20,
-    )(grads, *near_grads)
+    )(grads, near_grads)
 
 
 def solution(mesh):

time: 74.3 us -> 72.3 us (0.973)
  starting transfers between devices: 37 us -> 42 us
  Pallas kernels: 15.4 us -> 12.2 us
  local copies, waits for them, and re-layouts: 2.43 us -> 0.03 us
  blocking collectives: 11 us -> 9.6 us
    all_to_all x3, starting transfers between devices: 25 us -> 29.7 us  [exchange(): lax.all_to_all(array, 'seq', 0, 0, axis_index_groups=groups, tiled=True)]
    all_to_all x3, waiting for transfers between devices: 1.71 us -> 4.22 us  [exchange(): lax.all_to_all(array, 'seq', 0, 0, axis_index_groups=groups, tiled=True)]
    ppermute x4, waiting for transfers between devices: 5.29 us -> 2.8 us  [partner(): return lax.ppermute(array, 'seq', [(i, i ^ bit) for i in range(DEVICES)])]
    unnamed x20 -> x10, local copies, waits for them, and re-layouts: 2.43 us -> 0.03 us
    pallas_call x3, Pallas kernels: 8.34 us -> 6.06 us  [the longest x1 4.2 us: body(): call(near_kernel, 'near_grads', shape((3, TOK, HEADS * WIDTH)), [SMEM] +...]
    all_to_all x1, blocking collectives: 11 us -> 9.6 us  [exchange(): lax.all_to_all(array, 'seq', 0, 0, axis_index_groups=groups, tiled=True)]
  transfers between devices with their start and end apart: 7 -> 7, of which waited for: 2 -> 3; matrix products, arithmetic and copies ran while one was open for 0% -> 0% of each run, Pallas kernels for 13% -> 11%
where the time goes in v3:
time: 72.3 us; the launch traced here: 71.7 us
  starting transfers between devices  42 us (58%)
  Pallas kernels  12.2 us (17%)
  blocking collectives  9.6 us (13%)
  waiting for transfers between devices  7.01 us (10%)
  between operations  0.8 us (1%)
    all_to_all x3, starting transfers between devices, exchange(): lax.all_to_all(array, 'seq', 0, 0, axis_index_groups=groups, tiled=True)  29.7 us
    ppermute x4, starting transfers between devices, partner(): return lax.ppermute(array, 'seq', [(i, i ^ bit) for i in range(DEVICES)])  12.3 us
    all_to_all x1, blocking collectives, exchange(): lax.all_to_all(array, 'seq', 0, 0, axis_index_groups=groups, tiled=True)  9.6 us
    all_to_all x3, waiting for transfers between devices, exchange(): lax.all_to_all(array, 'seq', 0, 0, axis_index_groups=groups, tiled=True)  4.22 us
    pallas_call x1, Pallas kernels, body(): call(near_kernel, 'near_grads', shape((3, TOK, HEADS * WIDTH)), [SMEM] +...  4.2 us
    pallas_call x1, Pallas kernels, body(): call(select_kernel, 'select_rows', (shape((HEADS, CHUNK, WIDTH)), shape((...  3.14 us
    ppermute x4, waiting for transfers between devices, partner(): return lax.ppermute(array, 'seq', [(i, i ^ bit) for i in range(DEVICES)])  2.8 us
  transfers between devices with their start and end apart: 7, of which 3 were waited for; matrix products, arithmetic and copies ran while one was open for 0% of the time, Pallas kernels for 11%

profile of v3, /device:TPU:1, one launch (start us, length us, event | category | flops | bytes accessed | tf_op | source)
XLA Modules:
  0.0 71.7 jit_solution(1049302693597713869)
XLA Ops:
  0.6 0.0 copy-start.2
  0.6 0.0 copy-start.3
  0.7 3.1 %select_rows.1 = (bf16[8,144,128]{2,1,0:T(8,128)(2,1)}, bf16[16,1024]{1,0:T(8,128)(2,1)}) custom-call(s32[1]{0:T(128)} %bitcast.i_ref, bf16[128,1024]{1,0:T(8,128)(2,1)} %q.1, bf16[128,1024]{1,0:T(8,128)(2,1)} %k.1, bf16[128,1024]{1,0:T(8,128)(2,1)} %v.1, bf16[128,1024]{1,0:T(8,128)(2,1)} %g.1, bf16[128,1024]{1,0:T(8,128)(2,1)} %o_in.1, f32[8,128]{1,0:T(8,128)} %n_in.1), custom_call_target="tpu_custom_call" | custom-call | flops 134217728 | bytes 3145728 | tf_op jit(solution)/shard_map/select_rows/pallas_call | solution.py:416
  3.8 0.0 copy-start
  3.8 0.0 copy-start.1
  3.8 0.0 copy-start.4
  3.8 10.3 %all-to-all-start = ((bf16[8,144,128]{2,1,0:T(8,128)(2,1)}), bf16[8,144,128]{2,1,0:T(8,128)(2,1)S(1)}, u32[]{:S(2)}, u32[]{:S(2)}) async-start(bf16[8,144,128]{2,1,0:T(8,128)(2,1)} %get-tuple-element.10), calls=%async_computation | async-start | bytes 589824 | tf_op jit(solution)/shard_map/all_to_all | solution.py:406
  14.2 0.0 copy-done.2
  14.2 0.0 copy-done.3
  14.2 0.0 copy-done
  14.2 0.0 copy-done.1
  14.2 0.0 copy-done.4
  14.2 0.9 %near_payload.1 = (bf16[272,1024]{1,0:T(8,128)(2,1)}, bf16[272,1024]{1,0:T(8,128)(2,1)S(1)}) custom-call(s32[1]{0:T(128)} %bitcast.i_ref, bf16[128,1024]{1,0:T(8,128)(2,1)S(1)} %copy-done, bf16[128,1024]{1,0:T(8,128)(2,1)S(1)} %copy-done.1, bf16[128,1024]{1,0:T(8,128)(2,1)S(1)} %copy-done.2, bf16[128,1024]{1,0:T(8,128)(2,1)S(1)} %copy-done.3, ...), custom_call_target="tpu_custom_call" | custom-call | bytes 4194304 | tf_op jit(solution)/shard_map/near_payload/pallas_call | solution.py:428
  15.2 3.3 %collective-permute-start.2 = (bf16[272,1024]{1,0:T(8,128)(2,1)S(1)}, bf16[272,1024]{1,0:T(8,128)(2,1)S(1)}, u32[]{:S(2)}, u32[]{:S(2)}) collective-permute-start(bf16[272,1024]{1,0:T(8,128)(2,1)S(1)} %get-tuple-element.16), channel_id=1, source_target_pairs={{0,2},{1,3},{2,0},{3,1},{4,6},{5,7},{6,4},{7,5},{8,10},{9,11},{10,... | collective-permute-start | bytes 1671176 | tf_op jit(solution)/shard_map/ppermute | solution.py:410
  18.5 2.5 %all-to-all-done.r_ref = bf16[8,144,128]{2,1,0:T(8,128)(2,1)S(1)} async-done(((bf16[8,144,128]{2,1,0:T(8,128)(2,1)}), bf16[8,144,128]{2,1,0:T(8,128)(2,1)S(1)}, u32[]{:S(2)}, u32[]{:S(2)}) %all-to-all-start) | async-done | bytes 294944 | tf_op jit(solution)/shard_map/all_to_all | solution.py:406
  21.0 0.8 %middle_rows.1 = (bf16[16,40,128]{2,1,0:T(8,128)(2,1)}, bf16[40,128]{1,0:T(8,128)(2,1)S(1)}, bf16[544,128]{1,0:T(8,128)(2,1)S(1)}) custom-call(s32[1]{0:T(128)} %bitcast.i_ref, bf16[8,144,128]{2,1,0:T(8,128)(2,1)S(1)} %all-to-all-done.r_ref), custom_call_target="tpu_custom_call" | custom-call | bytes 1048576 | tf_op jit(solution)/shard_map/middle_rows/pallas_call | solution.py:440
  21.8 10.5 %all-to-all-start.1 = ((bf16[16,40,128]{2,1,0:T(8,128)(2,1)}), bf16[16,40,128]{2,1,0:T(8,128)(2,1)S(1)}, u32[]{:S(2)}, u32[]{:S(2)}) async-start(bf16[16,40,128]{2,1,0:T(8,128)(2,1)} %get-tuple-element.11), calls=%async_computation.1 | async-start | bytes 327680 | tf_op jit(solution)/shard_map/all_to_all | solution.py:406
  32.3 3.3 %collective-permute-start = (bf16[544,128]{1,0:T(8,128)(2,1)S(1)}, bf16[544,128]{1,0:T(8,128)(2,1)S(1)}, u32[]{:S(2)}, u32[]{:S(2)}) collective-permute-start(bf16[544,128]{1,0:T(8,128)(2,1)S(1)} %get-tuple-element.12), channel_id=1, source_target_pairs={{0,8},{1,9},{2,10},{3,11},{4,12},{5,13},{6,14},{7,15},{8,0},{9,1},... | collective-permute-start | bytes 417800 | tf_op jit(solution)/shard_map/ppermute | solution.py:410
  35.6 3.8 %collective-permute-start.1 = (bf16[272,1024]{1,0:T(8,128)(2,1)}, bf16[272,1024]{1,0:T(8,128)(2,1)S(1)}, u32[]{:S(2)}, u32[]{:S(2)}) collective-permute-start(bf16[272,1024]{1,0:T(8,128)(2,1)} %get-tuple-element.15), channel_id=1, source_target_pairs={{0,1},{1,0},{2,3},{3,2},{4,5},{5,4},{6,7},{7,6},{8,9},{9,8},{10,11... | collective-permute-start | bytes 1671176 | tf_op jit(solution)/shard_map/ppermute | solution.py:410
  39.4 0.0 collective-permute-done.2.r2
  39.4 1.9 %collective-permute-start.3 = (bf16[272,1024]{1,0:T(8,128)(2,1)S(1)}, bf16[272,1024]{1,0:T(8,128)(2,1)}, u32[]{:S(2)}, u32[]{:S(2)}) collective-permute-start(bf16[272,1024]{1,0:T(8,128)(2,1)S(1)} %collective-permute-done.2.r2), channel_id=1, source_target_pairs={{0,1},{1,0},{2,3},{3,2},{4,5},{5,4},{6,7},{7,6},{8,9},{9,8},{10,11... | collective-permute-start | bytes 1671176 | tf_op jit(solution)/shard_map/ppermute | solution.py:410
  41.3 2.8 %collective-permute-done.x_ref = bf16[544,128]{1,0:T(8,128)(2,1)S(1)} collective-permute-done((bf16[544,128]{1,0:T(8,128)(2,1)S(1)}, bf16[544,128]{1,0:T(8,128)(2,1)S(1)}, u32[]{:S(2)}, u32[]{:S(2)}) %collective-permute-start) | collective-permute-done | bytes 139296 | tf_op jit(solution)/shard_map/ppermute | solution.py:410
  44.1 0.9 %pair_grads.1.after_pair.n_ref = f32[8,96,128]{2,1,0:T(8,128)S(1)} custom-call(s32[1]{0:T(128)} %bitcast.i_ref, bf16[8,144,128]{2,1,0:T(8,128)(2,1)S(1)} %all-to-all-done.r_ref, bf16[544,128]{1,0:T(8,128)(2,1)S(1)} %collective-permute-done.x_ref), custom_call_target="tpu_custom_call" | custom-call | flops 1342177280 | bytes 1048576 | tf_op jit(solution)/shard_map/pair_grads/pallas_call | solution.py:450
  45.1 0.0 all-to-all-done.1.r_ref
  45.1 0.1 plane_rows.1
  45.2 9.6 %all_to_all.20.f_ref = bf16[4,272,128]{2,1,0:T(8,128)(2,1)S(1)} all-to-all(bf16[4,272,128]{2,1,0:T(8,128)(2,1)S(1)} %plane_rows.1), channel_id=1, replica_groups={{0,128,256,384},{1,129,257,385},{2,130,258,386},{3,131,259,387},{4,132,..., dimensions={0} | all-to-all | bytes 557056 | tf_op jit(solution)/shard_map/all_to_all | solution.py:406
  54.8 1.0 %join_grads.1.after = bf16[8,96,128]{2,1,0:T(8,128)(2,1)} custom-call(s32[1]{0:T(128)} %bitcast.i_ref, bf16[4,272,128]{2,1,0:T(8,128)(2,1)S(1)} %all_to_all.20.f_ref, bf16[40,128]{1,0:T(8,128)(2,1)S(1)} %get-tuple-element.13.m_ref, f32[8,96,128]{2,1,0:T(8,128)S(1)} %pair_grads.1.after_pair.n_ref), custom_call_target="tpu_custom_call" | custom-call | bytes 1048576 | tf_op jit(solution)/shard_map/join_grads/pallas_call | solution.py:466
  55.8 8.9 %all-to-all-start.3 = ((bf16[8,96,128]{2,1,0:T(8,128)(2,1)}), bf16[8,96,128]{2,1,0:T(8,128)(2,1)S(1)}, u32[]{:S(2)}, u32[]{:S(2)}) async-start(bf16[8,96,128]{2,1,0:T(8,128)(2,1)} %join_grads.1.after), calls=%async_computation.3 | async-start | bytes 393216 | tf_op jit(solution)/shard_map/all_to_all | solution.py:406
  64.7 0.0 collective-permute-done.1.r1
  64.7 0.0 collective-permute-done.3.r3
  64.7 4.2 %near_grads.1.n_ref = bf16[3,128,1024]{2,1,0:T(8,128)(2,1)S(1)} custom-call(s32[1]{0:T(128)} %bitcast.i_ref, bf16[128,1024]{1,0:T(8,128)(2,1)S(1)} %copy-done, bf16[128,1024]{1,0:T(8,128)(2,1)S(1)} %copy-done.1, bf16[128,1024]{1,0:T(8,128)(2,1)S(1)} %copy-done.2, bf16[128,1024]{1,0:T(8,128)(2,1)S(1)} %copy-done.3, bf16[16,1024]{1,0:T(8,128)(2,1)S(1)} %copy-done.4, ...), custom_call_target="tpu_custom_call" | custom-call | flops 570425344 | bytes 4194304 | tf_op jit(solution)/shard_map/near_grads/pallas_call | solution.py:474
  68.9 1.7 %all-to-all-done.3.r_ref = bf16[8,96,128]{2,1,0:T(8,128)(2,1)S(1)} async-done(((bf16[8,96,128]{2,1,0:T(8,128)(2,1)}), bf16[8,96,128]{2,1,0:T(8,128)(2,1)S(1)}, u32[]{:S(2)}, u32[]{:S(2)}) %all-to-all-start.3) | async-done | bytes 196640 | tf_op jit(solution)/shard_map/all_to_all | solution.py:406
  70.6 1.1 %add_levels.1 = (bf16[128,1024]{1,0:T(8,128)(2,1)}, bf16[128,1024]{1,0:T(8,128)(2,1)}, bf16[128,1024]{1,0:T(8,128)(2,1)}) custom-call(bf16[8,96,128]{2,1,0:T(8,128)(2,1)S(1)} %all-to-all-done.3.r_ref, bf16[3,128,1024]{2,1,0:T(8,128)(2,1)S(1)} %near_grads.1.n_ref), custom_call_target="tpu_custom_call" | custom-call | flops 25165824 | bytes 4194304 | tf_op jit(solution)/shard_map/add_levels/pallas_call | solution.py:484
Async XLA Ops:
  0.6 13.6 %copy-start.2 = (bf16[128,1024]{1,0:T(8,128)(2,1)S(1)}, bf16[128,1024]{1,0:T(8,128)(2,1)}, u32[]{:S(2)}) copy-start(bf16[128,1024]{1,0:T(8,128)(2,1)} %v.1) | copy-start | bytes 786436
  0.6 13.5 %copy-start.3 = (bf16[128,1024]{1,0:T(8,128)(2,1)S(1)}, bf16[128,1024]{1,0:T(8,128)(2,1)}, u32[]{:S(2)}) copy-start(bf16[128,1024]{1,0:T(8,128)(2,1)} %g.1) | copy-start | bytes 786436
  3.8 10.4 %copy-start = (bf16[128,1024]{1,0:T(8,128)(2,1)S(1)}, bf16[128,1024]{1,0:T(8,128)(2,1)}, u32[]{:S(2)}) copy-start(bf16[128,1024]{1,0:T(8,128)(2,1)} %q.1) | copy-start | bytes 786436
  3.8 10.4 %copy-start.1 = (bf16[128,1024]{1,0:T(8,128)(2,1)S(1)}, bf16[128,1024]{1,0:T(8,128)(2,1)}, u32[]{:S(2)}) copy-start(bf16[128,1024]{1,0:T(8,128)(2,1)} %k.1) | copy-start | bytes 786436
  3.8 10.4 %copy-start.4 = (bf16[16,1024]{1,0:T(8,128)(2,1)S(1)}, bf16[16,1024]{1,0:T(8,128)(2,1)}, u32[]{:S(2)}) copy-start(bf16[16,1024]{1,0:T(8,128)(2,1)} %get-tuple-element.14.s_in.s) | copy-start | bytes 98308
  3.8 17.2 %all-to-all-start = ((bf16[8,144,128]{2,1,0:T(8,128)(2,1)}), bf16[8,144,128]{2,1,0:T(8,128)(2,1)S(1)}, u32[]{:S(2)}, u32[]{:S(2)}) async-start(bf16[8,144,128]{2,1,0:T(8,128)(2,1)} %get-tuple-element.10), calls=%async_computation | async-start | bytes 589824 | tf_op jit(solution)/shard_map/all_to_all | solution.py:406
  15.2 24.2 %collective-permute-start.2 = (bf16[272,1024]{1,0:T(8,128)(2,1)S(1)}, bf16[272,1024]{1,0:T(8,128)(2,1)S(1)}, u32[]{:S(2)}, u32[]{:S(2)}) collective-permute-start(bf16[272,1024]{1,0:T(8,128)(2,1)S(1)} %get-tuple-element.16), channel_id=1, source_target_pairs={{0,2},{1,3},{2,0},{3,1},{4,6},{5,7},{6,4},{7,5},{8,10},{9,11},{10,... | collective-permute-start | bytes 1671176 | tf_op jit(solution)/shard_map/ppermute | solution.py:410
  21.8 23.3 %all-to-all-start.1 = ((bf16[16,40,128]{2,1,0:T(8,128)(2,1)}), bf16[16,40,128]{2,1,0:T(8,128)(2,1)S(1)}, u32[]{:S(2)}, u32[]{:S(2)}) async-start(bf16[16,40,128]{2,1,0:T(8,128)(2,1)} %get-tuple-element.11), calls=%async_computation.1 | async-start | bytes 327680 | tf_op jit(solution)/shard_map/all_to_all | solution.py:406
  32.3 11.8 %collective-permute-start = (bf16[544,128]{1,0:T(8,128)(2,1)S(1)}, bf16[544,128]{1,0:T(8,128)(2,1)S(1)}, u32[]{:S(2)}, u32[]{:S(2)}) collective-permute-start(bf16[544,128]{1,0:T(8,128)(2,1)S(1)} %get-tuple-element.12), channel_id=1, source_target_pairs={{0,8},{1,9},{2,10},{3,11},{4,12},{5,13},{6,14},{7,15},{8,0},{9,1},... | collective-permute-start | bytes 417800 | tf_op jit(solution)/shard_map/ppermute | solution.py:410
  35.6 29.1 %collective-permute-start.1 = (bf16[272,1024]{1,0:T(8,128)(2,1)}, bf16[272,1024]{1,0:T(8,128)(2,1)S(1)}, u32[]{:S(2)}, u32[]{:S(2)}) collective-permute-start(bf16[272,1024]{1,0:T(8,128)(2,1)} %get-tuple-element.15), channel_id=1, source_target_pairs={{0,1},{1,0},{2,3},{3,2},{4,5},{5,4},{6,7},{7,6},{8,9},{9,8},{10,11... | collective-permute-start | bytes 1671176 | tf_op jit(solution)/shard_map/ppermute | solution.py:410
  39.4 25.3 %collective-permute-start.3 = (bf16[272,1024]{1,0:T(8,128)(2,1)S(1)}, bf16[272,1024]{1,0:T(8,128)(2,1)}, u32[]{:S(2)}, u32[]{:S(2)}) collective-permute-start(bf16[272,1024]{1,0:T(8,128)(2,1)S(1)} %collective-permute-done.2.r2), channel_id=1, source_target_pairs={{0,1},{1,0},{2,3},{3,2},{4,5},{5,4},{6,7},{7,6},{8,9},{9,8},{10,11... | collective-permute-start | bytes 1671176 | tf_op jit(solution)/shard_map/ppermute | solution.py:410
  55.8 14.8 %all-to-all-start.3 = ((bf16[8,96,128]{2,1,0:T(8,128)(2,1)}), bf16[8,96,128]{2,1,0:T(8,128)(2,1)S(1)}, u32[]{:S(2)}, u32[]{:S(2)}) async-start(bf16[8,96,128]{2,1,0:T(8,128)(2,1)} %join_grads.1.after), calls=%async_computation.3 | async-start | bytes 393216 | tf_op jit(solution)/shard_map/all_to_all | solution.py:406

commit v4 on v3

--- a/solution.py
+++ b/solution.py
@@ -1,5 +1,3 @@
-import functools
-
 import jax
 import jax.numpy as jnp
 from jax import lax
@@ -227,7 +225,8 @@
         stats = jnp.where(lane == layer * RING + s, value, stats)
     rows = []
     for tensor in range(4):
-        flat[...] = r_ref[:, tensor * SIDE : tensor * SIDE + 16, :].astype(F32).reshape(128, WIDTH)
+        first = tensor * SIDE
+        flat[0:128] = r_ref[:, first : first + 16, :].astype(F32).reshape(128, WIDTH)
         rows.append(flat[pl.ds(place // 4, RING, stride=16), :])
     payload = jnp.concatenate(rows + [stats[0:8]], axis=0).astype(BF)
     mine_ref[...] = payload
@@ -442,7 +441,7 @@
         "middle_rows",
         (shape((DEPTH, FAR, WIDTH)), shape((FAR, WIDTH)), shape((PAIR, WIDTH))),
         [SMEM, VMEM],
-        [pltpu.VMEM((128, 128), F32)],
+        [pltpu.VMEM((144, 128), F32)],
         moved=1 << 20,
     )(index, side)
     far = exchange(far, DEPTH_GROUPS)

time: 72.3 us -> 72.3 us (level)
  no operation moved by 1% of the time
where the time goes in v4:
time: 72.3 us; the launch traced here: 71.7 us
  starting transfers between devices  42 us (58%)
  Pallas kernels  12.2 us (17%)
  blocking collectives  9.6 us (13%)
  waiting for transfers between devices  7.01 us (10%)
  between operations  0.8 us (1%)
    all_to_all x3, starting transfers between devices, exchange(): lax.all_to_all(array, 'seq', 0, 0, axis_index_groups=groups, tiled=True)  29.7 us
    ppermute x4, starting transfers between devices, partner(): return lax.ppermute(array, 'seq', [(i, i ^ bit) for i in range(DEVICES)])  12.3 us
    all_to_all x1, blocking collectives, exchange(): lax.all_to_all(array, 'seq', 0, 0, axis_index_groups=groups, tiled=True)  9.6 us
    all_to_all x3, waiting for transfers between devices, exchange(): lax.all_to_all(array, 'seq', 0, 0, axis_index_groups=groups, tiled=True)  4.22 us
    pallas_call x1, Pallas kernels, body(): call(near_kernel, 'near_grads', shape((3, TOK, HEADS * WIDTH)), [SMEM] +...  4.2 us
    pallas_call x1, Pallas kernels, body(): call(select_kernel, 'select_rows', (shape((HEADS, CHUNK, WIDTH)), shape((...  3.14 us
    ppermute x4, waiting for transfers between devices, partner(): return lax.ppermute(array, 'seq', [(i, i ^ bit) for i in range(DEVICES)])  2.8 us
  transfers between devices with their start and end apart: 7, of which 3 were waited for; matrix products, arithmetic and copies ran while one was open for 0% of the time, Pallas kernels for 11%

profile of v4, /device:TPU:1, one launch (start us, length us, event | category | flops | bytes accessed | tf_op | source)
XLA Modules:
  0.0 71.7 jit_solution(12175518290127454235)
XLA Ops:
  0.6 0.0 copy-start.2
  0.6 0.0 copy-start.3
  0.7 3.1 %select_rows.1 = (bf16[8,144,128]{2,1,0:T(8,128)(2,1)}, bf16[16,1024]{1,0:T(8,128)(2,1)}) custom-call(s32[1]{0:T(128)} %bitcast.i_ref, bf16[128,1024]{1,0:T(8,128)(2,1)} %q.1, bf16[128,1024]{1,0:T(8,128)(2,1)} %k.1, bf16[128,1024]{1,0:T(8,128)(2,1)} %v.1, bf16[128,1024]{1,0:T(8,128)(2,1)} %g.1, bf16[128,1024]{1,0:T(8,128)(2,1)} %o_in.1, f32[8,128]{1,0:T(8,128)} %n_in.1), custom_call_target="tpu_custom_call" | custom-call | flops 134217728 | bytes 3145728 | tf_op jit(solution)/shard_map/select_rows/pallas_call | solution.py:415
  3.8 0.0 copy-start
  3.8 0.0 copy-start.1
  3.8 0.0 copy-start.4
  3.8 10.3 %all-to-all-start = ((bf16[8,144,128]{2,1,0:T(8,128)(2,1)}), bf16[8,144,128]{2,1,0:T(8,128)(2,1)S(1)}, u32[]{:S(2)}, u32[]{:S(2)}) async-start(bf16[8,144,128]{2,1,0:T(8,128)(2,1)} %get-tuple-element.10), calls=%async_computation | async-start | bytes 589824 | tf_op jit(solution)/shard_map/all_to_all | solution.py:405
  14.2 0.0 copy-done.2
  14.2 0.0 copy-done.3
  14.2 0.0 copy-done
  14.2 0.0 copy-done.1
  14.2 0.0 copy-done.4
  14.2 0.9 %near_payload.1 = (bf16[272,1024]{1,0:T(8,128)(2,1)}, bf16[272,1024]{1,0:T(8,128)(2,1)S(1)}) custom-call(s32[1]{0:T(128)} %bitcast.i_ref, bf16[128,1024]{1,0:T(8,128)(2,1)S(1)} %copy-done, bf16[128,1024]{1,0:T(8,128)(2,1)S(1)} %copy-done.1, bf16[128,1024]{1,0:T(8,128)(2,1)S(1)} %copy-done.2, bf16[128,1024]{1,0:T(8,128)(2,1)S(1)} %copy-done.3, ...), custom_call_target="tpu_custom_call" | custom-call | bytes 4194304 | tf_op jit(solution)/shard_map/near_payload/pallas_call | solution.py:427
  15.2 3.3 %collective-permute-start.2 = (bf16[272,1024]{1,0:T(8,128)(2,1)S(1)}, bf16[272,1024]{1,0:T(8,128)(2,1)S(1)}, u32[]{:S(2)}, u32[]{:S(2)}) collective-permute-start(bf16[272,1024]{1,0:T(8,128)(2,1)S(1)} %get-tuple-element.16), channel_id=1, source_target_pairs={{0,2},{1,3},{2,0},{3,1},{4,6},{5,7},{6,4},{7,5},{8,10},{9,11},{10,... | collective-permute-start | bytes 1671176 | tf_op jit(solution)/shard_map/ppermute | solution.py:409
  18.5 2.5 %all-to-all-done.r_ref = bf16[8,144,128]{2,1,0:T(8,128)(2,1)S(1)} async-done(((bf16[8,144,128]{2,1,0:T(8,128)(2,1)}), bf16[8,144,128]{2,1,0:T(8,128)(2,1)S(1)}, u32[]{:S(2)}, u32[]{:S(2)}) %all-to-all-start) | async-done | bytes 294944 | tf_op jit(solution)/shard_map/all_to_all | solution.py:405
  21.0 0.8 %middle_rows.1 = (bf16[16,40,128]{2,1,0:T(8,128)(2,1)}, bf16[40,128]{1,0:T(8,128)(2,1)S(1)}, bf16[544,128]{1,0:T(8,128)(2,1)S(1)}) custom-call(s32[1]{0:T(128)} %bitcast.i_ref, bf16[8,144,128]{2,1,0:T(8,128)(2,1)S(1)} %all-to-all-done.r_ref), custom_call_target="tpu_custom_call" | custom-call | bytes 1048576 | tf_op jit(solution)/shard_map/middle_rows/pallas_call | solution.py:439
  21.8 10.5 %all-to-all-start.1 = ((bf16[16,40,128]{2,1,0:T(8,128)(2,1)}), bf16[16,40,128]{2,1,0:T(8,128)(2,1)S(1)}, u32[]{:S(2)}, u32[]{:S(2)}) async-start(bf16[16,40,128]{2,1,0:T(8,128)(2,1)} %get-tuple-element.11), calls=%async_computation.1 | async-start | bytes 327680 | tf_op jit(solution)/shard_map/all_to_all | solution.py:405
  32.3 3.3 %collective-permute-start = (bf16[544,128]{1,0:T(8,128)(2,1)S(1)}, bf16[544,128]{1,0:T(8,128)(2,1)S(1)}, u32[]{:S(2)}, u32[]{:S(2)}) collective-permute-start(bf16[544,128]{1,0:T(8,128)(2,1)S(1)} %get-tuple-element.12), channel_id=1, source_target_pairs={{0,8},{1,9},{2,10},{3,11},{4,12},{5,13},{6,14},{7,15},{8,0},{9,1},... | collective-permute-start | bytes 417800 | tf_op jit(solution)/shard_map/ppermute | solution.py:409
  35.6 3.8 %collective-permute-start.1 = (bf16[272,1024]{1,0:T(8,128)(2,1)}, bf16[272,1024]{1,0:T(8,128)(2,1)S(1)}, u32[]{:S(2)}, u32[]{:S(2)}) collective-permute-start(bf16[272,1024]{1,0:T(8,128)(2,1)} %get-tuple-element.15), channel_id=1, source_target_pairs={{0,1},{1,0},{2,3},{3,2},{4,5},{5,4},{6,7},{7,6},{8,9},{9,8},{10,11... | collective-permute-start | bytes 1671176 | tf_op jit(solution)/shard_map/ppermute | solution.py:409
  39.4 0.0 collective-permute-done.2.r2
  39.4 1.9 %collective-permute-start.3 = (bf16[272,1024]{1,0:T(8,128)(2,1)S(1)}, bf16[272,1024]{1,0:T(8,128)(2,1)}, u32[]{:S(2)}, u32[]{:S(2)}) collective-permute-start(bf16[272,1024]{1,0:T(8,128)(2,1)S(1)} %collective-permute-done.2.r2), channel_id=1, source_target_pairs={{0,1},{1,0},{2,3},{3,2},{4,5},{5,4},{6,7},{7,6},{8,9},{9,8},{10,11... | collective-permute-start | bytes 1671176 | tf_op jit(solution)/shard_map/ppermute | solution.py:409
  41.3 2.8 %collective-permute-done.x_ref = bf16[544,128]{1,0:T(8,128)(2,1)S(1)} collective-permute-done((bf16[544,128]{1,0:T(8,128)(2,1)S(1)}, bf16[544,128]{1,0:T(8,128)(2,1)S(1)}, u32[]{:S(2)}, u32[]{:S(2)}) %collective-permute-start) | collective-permute-done | bytes 139296 | tf_op jit(solution)/shard_map/ppermute | solution.py:409
  44.1 0.9 %pair_grads.1.after_pair.n_ref = f32[8,96,128]{2,1,0:T(8,128)S(1)} custom-call(s32[1]{0:T(128)} %bitcast.i_ref, bf16[8,144,128]{2,1,0:T(8,128)(2,1)S(1)} %all-to-all-done.r_ref, bf16[544,128]{1,0:T(8,128)(2,1)S(1)} %collective-permute-done.x_ref), custom_call_target="tpu_custom_call" | custom-call | flops 1342177280 | bytes 1048576 | tf_op jit(solution)/shard_map/pair_grads/pallas_call | solution.py:449
  45.1 0.0 all-to-all-done.1.r_ref
  45.1 0.1 plane_rows.1
  45.2 9.6 %all_to_all.20.f_ref = bf16[4,272,128]{2,1,0:T(8,128)(2,1)S(1)} all-to-all(bf16[4,272,128]{2,1,0:T(8,128)(2,1)S(1)} %plane_rows.1), channel_id=1, replica_groups={{0,128,256,384},{1,129,257,385},{2,130,258,386},{3,131,259,387},{4,132,..., dimensions={0} | all-to-all | bytes 557056 | tf_op jit(solution)/shard_map/all_to_all | solution.py:405
  54.8 1.0 %join_grads.1.after = bf16[8,96,128]{2,1,0:T(8,128)(2,1)} custom-call(s32[1]{0:T(128)} %bitcast.i_ref, bf16[4,272,128]{2,1,0:T(8,128)(2,1)S(1)} %all_to_all.20.f_ref, bf16[40,128]{1,0:T(8,128)(2,1)S(1)} %get-tuple-element.13.m_ref, f32[8,96,128]{2,1,0:T(8,128)S(1)} %pair_grads.1.after_pair.n_ref), custom_call_target="tpu_custom_call" | custom-call | bytes 1048576 | tf_op jit(solution)/shard_map/join_grads/pallas_call | solution.py:465
  55.8 8.9 %all-to-all-start.3 = ((bf16[8,96,128]{2,1,0:T(8,128)(2,1)}), bf16[8,96,128]{2,1,0:T(8,128)(2,1)S(1)}, u32[]{:S(2)}, u32[]{:S(2)}) async-start(bf16[8,96,128]{2,1,0:T(8,128)(2,1)} %join_grads.1.after), calls=%async_computation.3 | async-start | bytes 393216 | tf_op jit(solution)/shard_map/all_to_all | solution.py:405
  64.7 0.0 collective-permute-done.1.r1
  64.7 0.0 collective-permute-done.3.r3
  64.7 4.2 %near_grads.1.n_ref = bf16[3,128,1024]{2,1,0:T(8,128)(2,1)S(1)} custom-call(s32[1]{0:T(128)} %bitcast.i_ref, bf16[128,1024]{1,0:T(8,128)(2,1)S(1)} %copy-done, bf16[128,1024]{1,0:T(8,128)(2,1)S(1)} %copy-done.1, bf16[128,1024]{1,0:T(8,128)(2,1)S(1)} %copy-done.2, bf16[128,1024]{1,0:T(8,128)(2,1)S(1)} %copy-done.3, bf16[16,1024]{1,0:T(8,128)(2,1)S(1)} %copy-done.4, ...), custom_call_target="tpu_custom_call" | custom-call | flops 570425344 | bytes 4194304 | tf_op jit(solution)/shard_map/near_grads/pallas_call | solution.py:473
  68.9 1.7 %all-to-all-done.3.r_ref = bf16[8,96,128]{2,1,0:T(8,128)(2,1)S(1)} async-done(((bf16[8,96,128]{2,1,0:T(8,128)(2,1)}), bf16[8,96,128]{2,1,0:T(8,128)(2,1)S(1)}, u32[]{:S(2)}, u32[]{:S(2)}) %all-to-all-start.3) | async-done | bytes 196640 | tf_op jit(solution)/shard_map/all_to_all | solution.py:405
  70.6 1.1 %add_levels.1 = (bf16[128,1024]{1,0:T(8,128)(2,1)}, bf16[128,1024]{1,0:T(8,128)(2,1)}, bf16[128,1024]{1,0:T(8,128)(2,1)}) custom-call(bf16[8,96,128]{2,1,0:T(8,128)(2,1)S(1)} %all-to-all-done.3.r_ref, bf16[3,128,1024]{2,1,0:T(8,128)(2,1)S(1)} %near_grads.1.n_ref), custom_call_target="tpu_custom_call" | custom-call | flops 25165824 | bytes 4194304 | tf_op jit(solution)/shard_map/add_levels/pallas_call | solution.py:483
Async XLA Ops:
  0.6 13.6 %copy-start.2 = (bf16[128,1024]{1,0:T(8,128)(2,1)S(1)}, bf16[128,1024]{1,0:T(8,128)(2,1)}, u32[]{:S(2)}) copy-start(bf16[128,1024]{1,0:T(8,128)(2,1)} %v.1) | copy-start | bytes 786436
  0.6 13.5 %copy-start.3 = (bf16[128,1024]{1,0:T(8,128)(2,1)S(1)}, bf16[128,1024]{1,0:T(8,128)(2,1)}, u32[]{:S(2)}) copy-start(bf16[128,1024]{1,0:T(8,128)(2,1)} %g.1) | copy-start | bytes 786436
  3.8 10.4 %copy-start = (bf16[128,1024]{1,0:T(8,128)(2,1)S(1)}, bf16[128,1024]{1,0:T(8,128)(2,1)}, u32[]{:S(2)}) copy-start(bf16[128,1024]{1,0:T(8,128)(2,1)} %q.1) | copy-start | bytes 786436
  3.8 10.4 %copy-start.1 = (bf16[128,1024]{1,0:T(8,128)(2,1)S(1)}, bf16[128,1024]{1,0:T(8,128)(2,1)}, u32[]{:S(2)}) copy-start(bf16[128,1024]{1,0:T(8,128)(2,1)} %k.1) | copy-start | bytes 786436
  3.8 10.4 %copy-start.4 = (bf16[16,1024]{1,0:T(8,128)(2,1)S(1)}, bf16[16,1024]{1,0:T(8,128)(2,1)}, u32[]{:S(2)}) copy-start(bf16[16,1024]{1,0:T(8,128)(2,1)} %get-tuple-element.14.s_in.s) | copy-start | bytes 98308
  3.8 17.2 %all-to-all-start = ((bf16[8,144,128]{2,1,0:T(8,128)(2,1)}), bf16[8,144,128]{2,1,0:T(8,128)(2,1)S(1)}, u32[]{:S(2)}, u32[]{:S(2)}) async-start(bf16[8,144,128]{2,1,0:T(8,128)(2,1)} %get-tuple-element.10), calls=%async_computation | async-start | bytes 589824 | tf_op jit(solution)/shard_map/all_to_all | solution.py:405
  15.2 24.2 %collective-permute-start.2 = (bf16[272,1024]{1,0:T(8,128)(2,1)S(1)}, bf16[272,1024]{1,0:T(8,128)(2,1)S(1)}, u32[]{:S(2)}, u32[]{:S(2)}) collective-permute-start(bf16[272,1024]{1,0:T(8,128)(2,1)S(1)} %get-tuple-element.16), channel_id=1, source_target_pairs={{0,2},{1,3},{2,0},{3,1},{4,6},{5,7},{6,4},{7,5},{8,10},{9,11},{10,... | collective-permute-start | bytes 1671176 | tf_op jit(solution)/shard_map/ppermute | solution.py:409
  21.8 23.3 %all-to-all-start.1 = ((bf16[16,40,128]{2,1,0:T(8,128)(2,1)}), bf16[16,40,128]{2,1,0:T(8,128)(2,1)S(1)}, u32[]{:S(2)}, u32[]{:S(2)}) async-start(bf16[16,40,128]{2,1,0:T(8,128)(2,1)} %get-tuple-element.11), calls=%async_computation.1 | async-start | bytes 327680 | tf_op jit(solution)/shard_map/all_to_all | solution.py:405
  32.3 11.8 %collective-permute-start = (bf16[544,128]{1,0:T(8,128)(2,1)S(1)}, bf16[544,128]{1,0:T(8,128)(2,1)S(1)}, u32[]{:S(2)}, u32[]{:S(2)}) collective-permute-start(bf16[544,128]{1,0:T(8,128)(2,1)S(1)} %get-tuple-element.12), channel_id=1, source_target_pairs={{0,8},{1,9},{2,10},{3,11},{4,12},{5,13},{6,14},{7,15},{8,0},{9,1},... | collective-permute-start | bytes 417800 | tf_op jit(solution)/shard_map/ppermute | solution.py:409
  35.6 29.1 %collective-permute-start.1 = (bf16[272,1024]{1,0:T(8,128)(2,1)}, bf16[272,1024]{1,0:T(8,128)(2,1)S(1)}, u32[]{:S(2)}, u32[]{:S(2)}) collective-permute-start(bf16[272,1024]{1,0:T(8,128)(2,1)} %get-tuple-element.15), channel_id=1, source_target_pairs={{0,1},{1,0},{2,3},{3,2},{4,5},{5,4},{6,7},{7,6},{8,9},{9,8},{10,11... | collective-permute-start | bytes 1671176 | tf_op jit(solution)/shard_map/ppermute | solution.py:409
  39.4 25.3 %collective-permute-start.3 = (bf16[272,1024]{1,0:T(8,128)(2,1)S(1)}, bf16[272,1024]{1,0:T(8,128)(2,1)}, u32[]{:S(2)}, u32[]{:S(2)}) collective-permute-start(bf16[272,1024]{1,0:T(8,128)(2,1)S(1)} %collective-permute-done.2.r2), channel_id=1, source_target_pairs={{0,1},{1,0},{2,3},{3,2},{4,5},{5,4},{6,7},{7,6},{8,9},{9,8},{10,11... | collective-permute-start | bytes 1671176 | tf_op jit(solution)/shard_map/ppermute | solution.py:409
  55.8 14.8 %all-to-all-start.3 = ((bf16[8,96,128]{2,1,0:T(8,128)(2,1)}), bf16[8,96,128]{2,1,0:T(8,128)(2,1)S(1)}, u32[]{:S(2)}, u32[]{:S(2)}) async-start(bf16[8,96,128]{2,1,0:T(8,128)(2,1)} %join_grads.1.after), calls=%async_computation.3 | async-start | bytes 393216 | tf_op jit(solution)/shard_map/all_to_all | solution.py:405

commit v5 on v4

--- a/solution.py
+++ b/solution.py
@@ -251,7 +251,7 @@
     pair_ref[528:544, :] = (tiles[4] + tiles[5] + tiles[6] + tiles[7]).astype(BF)
 
 
-def pair_kernel(i_ref, r_ref, x_ref, o_ref):
+def pair_kernel(i_ref, r_ref, x_ref, after, o_ref):
     upper = (i_ref[0] // 8) % 2 == 1
 
     def own(tensor):
@@ -314,7 +314,7 @@
         o_ref[target, 256:PLANE, :] = tile
 
 
-def join_kernel(i_ref, f_ref, m_ref, n_ref, o_ref, sums, wide):
+def join_kernel(i_ref, f_ref, m_ref, n_ref, after, o_ref, sums, wide):
     index = i_ref[0]
     row = index // 128
     layer = (index // 8) % DEPTH
@@ -433,9 +433,7 @@
         moved=4 << 20,
         places=(ANY, ANY),
     )(index, query_rows, key_rows, value_rows, out_grad, stats)
-    core = partner(core, 1)
-    chip = partner(chip, 2)
-    relay = partner(chip, 1)
+    core, chip, relay = partner(core, 1), partner(chip, 2), partner(chip, 3)
     far, mine, pair = call(
         middle_kernel,
         "middle_rows",
@@ -450,10 +448,10 @@
         pair_kernel,
         "pair_grads",
         shape((RING, OUT_CHUNK, WIDTH), F32),
-        [SMEM, VMEM, VMEM],
-        flops=8 * 2 * 10 * 128 * 256 * 256,
+        [SMEM, VMEM, VMEM, ANY],
+        flops=20 * 2 * 10 * 128 * 256 * 256,
         moved=1 << 20,
-    )(index, side, pair)
+    )(index, side, pair, chip)
     plane = call(
         plane_kernel,
         "plane_rows",
@@ -461,15 +459,6 @@
         [SMEM, VMEM, ANY],
         moved=1 << 20,
     )(index, far, sums)
-    plane = exchange(plane, ROW_GROUPS)
-    grads = call(
-        join_kernel,
-        "join_grads",
-        shape((RING, OUT_CHUNK, WIDTH)),
-        [SMEM, VMEM, VMEM, VMEM],
-        [pltpu.VMEM((RING, OUT_CHUNK, WIDTH), F32), pltpu.VMEM((128, 128), F32)],
-        moved=1 << 20,
-    )(index, plane, mine, sums)
     near_grads = call(
         near_kernel,
         "near_grads",
@@ -477,7 +466,16 @@
         [SMEM] + [VMEM] * 8 + [ANY],
         flops=int(1 * 2 * 128 * 128 * 128 * 8 * 17),
         moved=4 << 20,
-    )(index, query_rows, key_rows, value_rows, out_grad, stats, core, chip, relay, grads)
+    )(index, query_rows, key_rows, value_rows, out_grad, stats, core, chip, relay, plane)
+    plane = exchange(plane, ROW_GROUPS)
+    grads = call(
+        join_kernel,
+        "join_grads",
+        shape((RING, OUT_CHUNK, WIDTH)),
+        [SMEM, VMEM, VMEM, VMEM, ANY],
+        [pltpu.VMEM((RING, OUT_CHUNK, WIDTH), F32), pltpu.VMEM((128, 128), F32)],
+        moved=1 << 20,
+    )(index, plane, mine, sums, near_grads)
     grads = exchange(grads, RING_GROUPS)
     out = shape(whole)
     return call(

time: 72.3 us -> 71.6 us (level)
  starting transfers between devices: 42 us -> 37.5 us
  waiting for transfers between devices: 7.01 us -> 10.3 us
  Pallas kernels: 12.2 us -> 13.3 us
    ppermute x4, waiting for transfers between devices: 2.8 us -> 8.45 us  [partner(): return lax.ppermute(array, 'seq', [(i, i ^ bit) for i in range(DEVICES)])]
    all_to_all x3, starting transfers between devices: 29.7 us -> 25 us  [exchange(): lax.all_to_all(array, 'seq', 0, 0, axis_index_groups=groups, tiled=True)]
    all_to_all x3, waiting for transfers between devices: 4.22 us -> 1.82 us  [exchange(): lax.all_to_all(array, 'seq', 0, 0, axis_index_groups=groups, tiled=True)]
  transfers between devices with their start and end apart: 7 -> 7, of which waited for: 3 -> 3; matrix products, arithmetic and copies ran while one was open for 0% -> 0% of each run, Pallas kernels for 11% -> 12%
where the time goes in v5:
time: 71.6 us; the launch traced here: 71 us
  starting transfers between devices  37.5 us (52%)
  Pallas kernels  13.3 us (19%)
  waiting for transfers between devices  10.3 us (14%)
  blocking collectives  9.11 us (13%)
  between operations  0.8 us (1%)
    all_to_all x3, starting transfers between devices, exchange(): lax.all_to_all(array, 'seq', 0, 0, axis_index_groups=groups, tiled=True)  25 us
    ppermute x4, starting transfers between devices, partner(): return lax.ppermute(array, 'seq', [(i, i ^ bit) for i in range(DEVICES)])  12.5 us
    all_to_all x1, blocking collectives, exchange(): lax.all_to_all(array, 'seq', 0, 0, axis_index_groups=groups, tiled=True)  9.11 us
    ppermute x4, waiting for transfers between devices, partner(): return lax.ppermute(array, 'seq', [(i, i ^ bit) for i in range(DEVICES)])  8.45 us
    pallas_call x1, Pallas kernels, body(): call(near_kernel, 'near_grads', shape((3, TOK, HEADS * WIDTH)), [SMEM] +...  4.53 us
    pallas_call x1, Pallas kernels, body(): call(select_kernel, 'select_rows', (shape((HEADS, CHUNK, WIDTH)), shape((...  3.14 us
    all_to_all x3, waiting for transfers between devices, exchange(): lax.all_to_all(array, 'seq', 0, 0, axis_index_groups=groups, tiled=True)  1.82 us
    pallas_call x1, Pallas kernels, body(): call(payload_kernel, 'near_payload', (shape((NEAR, HEADS * WIDTH)), shape...  1.66 us
  transfers between devices with their start and end apart: 7, of which 3 were waited for; matrix products, arithmetic and copies ran while one was open for 0% of the time, Pallas kernels for 12%

profile of v5, /device:TPU:1, one launch (start us, length us, event | category | flops | bytes accessed | tf_op | source)
XLA Modules:
  0.0 71.0 jit_solution(5347039855365336163)
XLA Ops:
  0.6 0.0 copy-start.2
  0.6 0.0 copy-start.3
  0.7 3.1 %select_rows.1 = (bf16[8,144,128]{2,1,0:T(8,128)(2,1)}, bf16[16,1024]{1,0:T(8,128)(2,1)}) custom-call(s32[1]{0:T(128)} %bitcast.i_ref, bf16[128,1024]{1,0:T(8,128)(2,1)} %q.1, bf16[128,1024]{1,0:T(8,128)(2,1)} %k.1, bf16[128,1024]{1,0:T(8,128)(2,1)} %v.1, bf16[128,1024]{1,0:T(8,128)(2,1)} %g.1, bf16[128,1024]{1,0:T(8,128)(2,1)} %o_in.1, f32[8,128]{1,0:T(8,128)} %n_in.1), custom_call_target="tpu_custom_call" | custom-call | flops 134217728 | bytes 3145728 | tf_op jit(solution)/shard_map/select_rows/pallas_call | solution.py:415
  3.8 0.0 copy-start
  3.8 0.0 copy-start.1
  3.8 0.0 copy-start.4
  3.8 10.3 %all-to-all-start = ((bf16[8,144,128]{2,1,0:T(8,128)(2,1)}), bf16[8,144,128]{2,1,0:T(8,128)(2,1)S(1)}, u32[]{:S(2)}, u32[]{:S(2)}) async-start(bf16[8,144,128]{2,1,0:T(8,128)(2,1)} %get-tuple-element.10), calls=%async_computation | async-start | bytes 589824 | tf_op jit(solution)/shard_map/all_to_all | solution.py:405
  14.2 0.0 copy-done.2
  14.2 0.0 copy-done.3
  14.2 0.0 copy-done
  14.2 0.0 copy-done.1
  14.2 0.0 copy-done.4
  14.2 1.7 %near_payload.1 = (bf16[272,1024]{1,0:T(8,128)(2,1)}, bf16[272,1024]{1,0:T(8,128)(2,1)}) custom-call(s32[1]{0:T(128)} %bitcast.i_ref, bf16[128,1024]{1,0:T(8,128)(2,1)S(1)} %copy-done, bf16[128,1024]{1,0:T(8,128)(2,1)S(1)} %copy-done.1, bf16[128,1024]{1,0:T(8,128)(2,1)S(1)} %copy-done.2, bf16[128,1024]{1,0:T(8,128)(2,1)S(1)} %copy-done.3, ...), custom_call_target="tpu_custom_call" | custom-call | bytes 4194304 | tf_op jit(solution)/shard_map/near_payload/pallas_call | solution.py:427
  15.9 3.3 %collective-permute-start.1 = (bf16[272,1024]{1,0:T(8,128)(2,1)}, bf16[272,1024]{1,0:T(8,128)(2,1)S(1)}, u32[]{:S(2)}, u32[]{:S(2)}) collective-permute-start(bf16[272,1024]{1,0:T(8,128)(2,1)} %get-tuple-element.14), channel_id=1, source_target_pairs={{0,2},{1,3},{2,0},{3,1},{4,6},{5,7},{6,4},{7,5},{8,10},{9,11},{10,... | collective-permute-start | bytes 1671176 | tf_op jit(solution)/shard_map/ppermute | solution.py:409
  19.2 1.8 %all-to-all-done.r_ref = bf16[8,144,128]{2,1,0:T(8,128)(2,1)S(1)} async-done(((bf16[8,144,128]{2,1,0:T(8,128)(2,1)}), bf16[8,144,128]{2,1,0:T(8,128)(2,1)S(1)}, u32[]{:S(2)}, u32[]{:S(2)}) %all-to-all-start) | async-done | bytes 294944 | tf_op jit(solution)/shard_map/all_to_all | solution.py:405
  21.0 0.8 %middle_rows.1 = (bf16[16,40,128]{2,1,0:T(8,128)(2,1)}, bf16[40,128]{1,0:T(8,128)(2,1)S(1)}, bf16[544,128]{1,0:T(8,128)(2,1)S(1)}) custom-call(s32[1]{0:T(128)} %bitcast.i_ref, bf16[8,144,128]{2,1,0:T(8,128)(2,1)S(1)} %all-to-all-done.r_ref), custom_call_target="tpu_custom_call" | custom-call | bytes 1048576 | tf_op jit(solution)/shard_map/middle_rows/pallas_call | solution.py:437
  21.8 10.5 %all-to-all-start.1 = ((bf16[16,40,128]{2,1,0:T(8,128)(2,1)}), bf16[16,40,128]{2,1,0:T(8,128)(2,1)S(1)}, u32[]{:S(2)}, u32[]{:S(2)}) async-start(bf16[16,40,128]{2,1,0:T(8,128)(2,1)} %get-tuple-element.11), calls=%async_computation.1 | async-start | bytes 327680 | tf_op jit(solution)/shard_map/all_to_all | solution.py:405
  32.3 3.3 %collective-permute-start = (bf16[544,128]{1,0:T(8,128)(2,1)S(1)}, bf16[544,128]{1,0:T(8,128)(2,1)S(1)}, u32[]{:S(2)}, u32[]{:S(2)}) collective-permute-start(bf16[544,128]{1,0:T(8,128)(2,1)S(1)} %get-tuple-element.12), channel_id=1, source_target_pairs={{0,8},{1,9},{2,10},{3,11},{4,12},{5,13},{6,14},{7,15},{8,0},{9,1},... | collective-permute-start | bytes 417800 | tf_op jit(solution)/shard_map/ppermute | solution.py:409
  35.6 3.8 %collective-permute-start.2 = (bf16[272,1024]{1,0:T(8,128)(2,1)}, bf16[272,1024]{1,0:T(8,128)(2,1)}, u32[]{:S(2)}, u32[]{:S(2)}) collective-permute-start(bf16[272,1024]{1,0:T(8,128)(2,1)} %get-tuple-element.16), channel_id=1, source_target_pairs={{0,1},{1,0},{2,3},{3,2},{4,5},{5,4},{6,7},{7,6},{8,9},{9,8},{10,11... | collective-permute-start | bytes 1671176 | tf_op jit(solution)/shard_map/ppermute | solution.py:409
  39.4 2.1 %collective-permute-start.3 = (bf16[272,1024]{1,0:T(8,128)(2,1)}, bf16[272,1024]{1,0:T(8,128)(2,1)}, u32[]{:S(2)}, u32[]{:S(2)}) collective-permute-start(bf16[272,1024]{1,0:T(8,128)(2,1)} %get-tuple-element.14), channel_id=1, source_target_pairs={{0,3},{1,2},{2,1},{3,0},{4,7},{5,6},{6,5},{7,4},{8,11},{9,10},{10,... | collective-permute-start | bytes 1671176 | tf_op jit(solution)/shard_map/ppermute | solution.py:409
  41.5 2.7 %collective-permute-done.x_ref = bf16[544,128]{1,0:T(8,128)(2,1)S(1)} collective-permute-done((bf16[544,128]{1,0:T(8,128)(2,1)S(1)}, bf16[544,128]{1,0:T(8,128)(2,1)S(1)}, u32[]{:S(2)}, u32[]{:S(2)}) %collective-permute-start) | collective-permute-done | bytes 139296 | tf_op jit(solution)/shard_map/ppermute | solution.py:409
  44.2 0.0 collective-permute-done.1.after.r2
  44.2 0.9 %pair_grads.1.after_pair.n_ref = f32[8,96,128]{2,1,0:T(8,128)S(1)} custom-call(s32[1]{0:T(128)} %bitcast.i_ref, bf16[8,144,128]{2,1,0:T(8,128)(2,1)S(1)} %all-to-all-done.r_ref, bf16[544,128]{1,0:T(8,128)(2,1)S(1)} %collective-permute-done.x_ref, bf16[272,1024]{1,0:T(8,128)(2,1)S(1)} %collective-permute-done.1.after.r2), custom_call_target="tpu_custom_call" | custom-call | flops 3355443200 | bytes 1048576 | tf_op jit(solution)/shard_map/pair_grads/pallas_call | solution.py:447
  45.2 0.0 all-to-all-done.1.r_ref
  45.2 0.8 %plane_rows.1.after = bf16[4,272,128]{2,1,0:T(8,128)(2,1)} custom-call(s32[1]{0:T(128)} %bitcast.i_ref, bf16[16,40,128]{2,1,0:T(8,128)(2,1)S(1)} %all-to-all-done.1.r_ref, f32[8,96,128]{2,1,0:T(8,128)S(1)} %pair_grads.1.after_pair.n_ref), custom_call_target="tpu_custom_call" | custom-call | bytes 1048576 | tf_op jit(solution)/shard_map/plane_rows/pallas_call | solution.py:455
  46.0 4.2 %all-to-all-start.2 = ((bf16[4,272,128]{2,1,0:T(8,128)(2,1)}), bf16[4,272,128]{2,1,0:T(8,128)(2,1)S(1)}, u32[]{:S(2)}, u32[]{:S(2)}) async-start(bf16[4,272,128]{2,1,0:T(8,128)(2,1)} %plane_rows.1.after), calls=%async_computation.2 | async-start | bytes 557056 | tf_op jit(solution)/shard_map/all_to_all | solution.py:405
  50.2 0.0 collective-permute-done.2.r1
  50.2 5.7 %collective-permute-done.3.r3 = bf16[272,1024]{1,0:T(8,128)(2,1)} collective-permute-done((bf16[272,1024]{1,0:T(8,128)(2,1)}, bf16[272,1024]{1,0:T(8,128)(2,1)}, u32[]{:S(2)}, u32[]{:S(2)}) %collective-permute-start.3) | collective-permute-done | bytes 557088 | tf_op jit(solution)/shard_map/ppermute | solution.py:409
  55.9 4.5 %near_grads.1.after.n_ref = bf16[3,128,1024]{2,1,0:T(8,128)(2,1)S(1)} custom-call(s32[1]{0:T(128)} %bitcast.i_ref, bf16[128,1024]{1,0:T(8,128)(2,1)S(1)} %copy-done, bf16[128,1024]{1,0:T(8,128)(2,1)S(1)} %copy-done.1, bf16[128,1024]{1,0:T(8,128)(2,1)S(1)} %copy-done.2, bf16[128,1024]{1,0:T(8,128)(2,1)S(1)} %copy-done.3, bf16[16,1024]{1,0:T(8,128)(2,1)S(1)} %copy-done.4, ...), custom_call_target="tpu_custom_call" | custom-call | flops 570425344 | bytes 4194304 | tf_op jit(solution)/shard_map/near_grads/pallas_call | solution.py:462
  60.4 0.0 all-to-all-done.2.f_ref
  60.4 0.4 join_grads.1
  60.8 9.1 %all_to_all.20.r_ref = bf16[8,96,128]{2,1,0:T(8,128)(2,1)S(1)} all-to-all(bf16[8,96,128]{2,1,0:T(8,128)(2,1)S(1)} %join_grads.1), channel_id=1, replica_groups={{0,1,2,3,4,5,6,7},{8,9,10,11,12,13,14,15},{16,17,18,19,20,21,22,23},{24..., dimensions={0} | all-to-all | bytes 393216 | tf_op jit(solution)/shard_map/all_to_all | solution.py:405
  69.9 1.1 %add_levels.1 = (bf16[128,1024]{1,0:T(8,128)(2,1)}, bf16[128,1024]{1,0:T(8,128)(2,1)}, bf16[128,1024]{1,0:T(8,128)(2,1)}) custom-call(bf16[8,96,128]{2,1,0:T(8,128)(2,1)S(1)} %all_to_all.20.r_ref, bf16[3,128,1024]{2,1,0:T(8,128)(2,1)S(1)} %near_grads.1.after.n_ref), custom_call_target="tpu_custom_call" | custom-call | flops 25165824 | bytes 4194304 | tf_op jit(solution)/shard_map/add_levels/pallas_call | solution.py:481
Async XLA Ops:
  0.6 13.6 %copy-start.2 = (bf16[128,1024]{1,0:T(8,128)(2,1)S(1)}, bf16[128,1024]{1,0:T(8,128)(2,1)}, u32[]{:S(2)}) copy-start(bf16[128,1024]{1,0:T(8,128)(2,1)} %v.1) | copy-start | bytes 786436
  0.6 13.5 %copy-start.3 = (bf16[128,1024]{1,0:T(8,128)(2,1)S(1)}, bf16[128,1024]{1,0:T(8,128)(2,1)}, u32[]{:S(2)}) copy-start(bf16[128,1024]{1,0:T(8,128)(2,1)} %g.1) | copy-start | bytes 786436
  3.8 10.4 %copy-start = (bf16[128,1024]{1,0:T(8,128)(2,1)S(1)}, bf16[128,1024]{1,0:T(8,128)(2,1)}, u32[]{:S(2)}) copy-start(bf16[128,1024]{1,0:T(8,128)(2,1)} %q.1) | copy-start | bytes 786436
  3.8 10.4 %copy-start.1 = (bf16[128,1024]{1,0:T(8,128)(2,1)S(1)}, bf16[128,1024]{1,0:T(8,128)(2,1)}, u32[]{:S(2)}) copy-start(bf16[128,1024]{1,0:T(8,128)(2,1)} %k.1) | copy-start | bytes 786436
  3.8 10.4 %copy-start.4 = (bf16[16,1024]{1,0:T(8,128)(2,1)S(1)}, bf16[16,1024]{1,0:T(8,128)(2,1)}, u32[]{:S(2)}) copy-start(bf16[16,1024]{1,0:T(8,128)(2,1)} %get-tuple-element.13.s_in.s) | copy-start | bytes 98308
  3.8 17.2 %all-to-all-start = ((bf16[8,144,128]{2,1,0:T(8,128)(2,1)}), bf16[8,144,128]{2,1,0:T(8,128)(2,1)S(1)}, u32[]{:S(2)}, u32[]{:S(2)}) async-start(bf16[8,144,128]{2,1,0:T(8,128)(2,1)} %get-tuple-element.10), calls=%async_computation | async-start | bytes 589824 | tf_op jit(solution)/shard_map/all_to_all | solution.py:405
  15.9 28.3 %collective-permute-start.1 = (bf16[272,1024]{1,0:T(8,128)(2,1)}, bf16[272,1024]{1,0:T(8,128)(2,1)S(1)}, u32[]{:S(2)}, u32[]{:S(2)}) collective-permute-start(bf16[272,1024]{1,0:T(8,128)(2,1)} %get-tuple-element.14), channel_id=1, source_target_pairs={{0,2},{1,3},{2,0},{3,1},{4,6},{5,7},{6,4},{7,5},{8,10},{9,11},{10,... | collective-permute-start | bytes 1671176 | tf_op jit(solution)/shard_map/ppermute | solution.py:409
  21.8 23.4 %all-to-all-start.1 = ((bf16[16,40,128]{2,1,0:T(8,128)(2,1)}), bf16[16,40,128]{2,1,0:T(8,128)(2,1)S(1)}, u32[]{:S(2)}, u32[]{:S(2)}) async-start(bf16[16,40,128]{2,1,0:T(8,128)(2,1)} %get-tuple-element.11), calls=%async_computation.1 | async-start | bytes 327680 | tf_op jit(solution)/shard_map/all_to_all | solution.py:405
  32.3 11.9 %collective-permute-start = (bf16[544,128]{1,0:T(8,128)(2,1)S(1)}, bf16[544,128]{1,0:T(8,128)(2,1)S(1)}, u32[]{:S(2)}, u32[]{:S(2)}) collective-permute-start(bf16[544,128]{1,0:T(8,128)(2,1)S(1)} %get-tuple-element.12), channel_id=1, source_target_pairs={{0,8},{1,9},{2,10},{3,11},{4,12},{5,13},{6,14},{7,15},{8,0},{9,1},... | collective-permute-start | bytes 417800 | tf_op jit(solution)/shard_map/ppermute | solution.py:409
  35.6 14.6 %collective-permute-start.2 = (bf16[272,1024]{1,0:T(8,128)(2,1)}, bf16[272,1024]{1,0:T(8,128)(2,1)}, u32[]{:S(2)}, u32[]{:S(2)}) collective-permute-start(bf16[272,1024]{1,0:T(8,128)(2,1)} %get-tuple-element.16), channel_id=1, source_target_pairs={{0,1},{1,0},{2,3},{3,2},{4,5},{5,4},{6,7},{7,6},{8,9},{9,8},{10,11... | collective-permute-start | bytes 1671176 | tf_op jit(solution)/shard_map/ppermute | solution.py:409
  39.4 16.5 %collective-permute-start.3 = (bf16[272,1024]{1,0:T(8,128)(2,1)}, bf16[272,1024]{1,0:T(8,128)(2,1)}, u32[]{:S(2)}, u32[]{:S(2)}) collective-permute-start(bf16[272,1024]{1,0:T(8,128)(2,1)} %get-tuple-element.14), channel_id=1, source_target_pairs={{0,3},{1,2},{2,1},{3,0},{4,7},{5,6},{6,5},{7,4},{8,11},{9,10},{10,... | collective-permute-start | bytes 1671176 | tf_op jit(solution)/shard_map/ppermute | solution.py:409
  46.0 14.4 %all-to-all-start.2 = ((bf16[4,272,128]{2,1,0:T(8,128)(2,1)}), bf16[4,272,128]{2,1,0:T(8,128)(2,1)S(1)}, u32[]{:S(2)}, u32[]{:S(2)}) async-start(bf16[4,272,128]{2,1,0:T(8,128)(2,1)} %plane_rows.1.after), calls=%async_computation.2 | async-start | bytes 557056 | tf_op jit(solution)/shard_map/all_to_all | solution.py:405

commit v6 on v5

--- a/solution.py
+++ b/solution.py
@@ -89,11 +89,11 @@
         copies.append(
             [
                 pltpu.make_async_copy(
-                    source.at[pl.ds(part * 64, 64)],
-                    place.at[pl.ds(part * 64, 64)],
+                    source.at[pl.ds(part * TOK, TOK)],
+                    place.at[pl.ds(part * TOK, TOK)],
                     sems.at[number + 1, part],
                 )
-                for part in range(2)
+                for part in range(1)
             ]
         )
     for group in copies:
@@ -167,6 +167,7 @@
     stat_rows = [row[0] for row in stat_rows] + [row[1] for row in stat_rows]
     stat_columns = jnp.concatenate(stat_rows + [jnp.zeros((112, TOK), F32)], axis=0).T
     blocks = (r1, r2, r3)
+    causal = iota((TOK, TOK), 1) <= iota((TOK, TOK), 0)
 
     def part(block, number, c):
         return block[number * TOK : (TOK, 2 * TOK, NEAR)[number], c]
@@ -180,13 +181,13 @@
             size = key.shape[0]
             norm = stat_columns[:, head : head + 1]
             delta = stat_columns[:, HEADS + head : HEADS + head + 1]
-            lane = iota((TOK, size), 1)
-            mask = (lane <= iota((TOK, size), 0)) | (lane >= TOK)
-            probs = jnp.where(mask, jnp.exp(dot_nt(query, key) * SCALE - norm), 0.0)
+            probs = jnp.exp(dot_nt(query, key) * SCALE - norm)
+            own = jnp.where(causal, probs[:, 0:TOK], 0.0)
+            probs = own if size == TOK else jnp.concatenate([own, probs[:, TOK:]], axis=1)
             dscores = (probs * (dot_nt(grad, value) - delta)).astype(BF)
             out_ref[0, :, c] = (dot(dscores, key) * SCALE).astype(BF)
             key_grad = dot_tn(dscores[:, 0:TOK], query)
-            value_grad = dot_tn(probs[:, 0:TOK].astype(BF), grad)
+            value_grad = dot_tn(own.astype(BF), grad)
             if later:
                 query = jnp.concatenate([part(block, 0, c) for block in later], axis=0)
                 grad = jnp.concatenate([part(block, 1, c) for block in later], axis=0)

time: 71.6 us -> 71.5 us (level)
  no operation moved by 1% of the time
where the time goes in v6:
time: 71.5 us; the launch traced here: 70.9 us
  starting transfers between devices  37.5 us (52%)
  Pallas kernels  13.2 us (18%)
  waiting for transfers between devices  10.3 us (14%)
  blocking collectives  9.11 us (13%)
  between operations  0.8 us (1%)
    all_to_all x3, starting transfers between devices, exchange(): lax.all_to_all(array, 'seq', 0, 0, axis_index_groups=groups, tiled=True)  25 us
    ppermute x4, starting transfers between devices, partner(): return lax.ppermute(array, 'seq', [(i, i ^ bit) for i in range(DEVICES)])  12.5 us
    all_to_all x1, blocking collectives, exchange(): lax.all_to_all(array, 'seq', 0, 0, axis_index_groups=groups, tiled=True)  9.11 us
    ppermute x4, waiting for transfers between devices, partner(): return lax.ppermute(array, 'seq', [(i, i ^ bit) for i in range(DEVICES)])  8.44 us
    pallas_call x1, Pallas kernels, body(): call(near_kernel, 'near_grads', shape((3, TOK, HEADS * WIDTH)), [SMEM] +...  4.54 us
    pallas_call x1, Pallas kernels, body(): call(select_kernel, 'select_rows', (shape((HEADS, CHUNK, WIDTH)), shape((...  3.08 us
    all_to_all x3, waiting for transfers between devices, exchange(): lax.all_to_all(array, 'seq', 0, 0, axis_index_groups=groups, tiled=True)  1.82 us
    pallas_call x1, Pallas kernels, body(): call(payload_kernel, 'near_payload', (shape((NEAR, HEADS * WIDTH)), shape...  1.66 us
  transfers between devices with their start and end apart: 7, of which 3 were waited for; matrix products, arithmetic and copies ran while one was open for 0% of the time, Pallas kernels for 12%

profile of v6, /device:TPU:1, one launch (start us, length us, event | category | flops | bytes accessed | tf_op | source)
XLA Modules:
  0.0 70.9 jit_solution(17431007356856641187)
XLA Ops:
  0.6 0.0 copy-start.2
  0.6 0.0 copy-start.3
  0.7 3.1 %select_rows.1 = (bf16[8,144,128]{2,1,0:T(8,128)(2,1)}, bf16[16,1024]{1,0:T(8,128)(2,1)}) custom-call(s32[1]{0:T(128)} %bitcast.i_ref, bf16[128,1024]{1,0:T(8,128)(2,1)} %q.1, bf16[128,1024]{1,0:T(8,128)(2,1)} %k.1, bf16[128,1024]{1,0:T(8,128)(2,1)} %v.1, bf16[128,1024]{1,0:T(8,128)(2,1)} %g.1, bf16[128,1024]{1,0:T(8,128)(2,1)} %o_in.1, f32[8,128]{1,0:T(8,128)} %n_in.1), custom_call_target="tpu_custom_call" | custom-call | flops 134217728 | bytes 3145728 | tf_op jit(solution)/shard_map/select_rows/pallas_call | solution.py:416
  3.7 0.0 copy-start
  3.8 0.0 copy-start.1
  3.8 0.0 copy-start.4
  3.8 10.3 %all-to-all-start = ((bf16[8,144,128]{2,1,0:T(8,128)(2,1)}), bf16[8,144,128]{2,1,0:T(8,128)(2,1)S(1)}, u32[]{:S(2)}, u32[]{:S(2)}) async-start(bf16[8,144,128]{2,1,0:T(8,128)(2,1)} %get-tuple-element.10), calls=%async_computation | async-start | bytes 589824 | tf_op jit(solution)/shard_map/all_to_all | solution.py:406
  14.1 0.0 copy-done.2
  14.1 0.0 copy-done.3
  14.1 0.0 copy-done
  14.1 0.0 copy-done.1
  14.2 0.0 copy-done.4
  14.2 1.7 %near_payload.1 = (bf16[272,1024]{1,0:T(8,128)(2,1)}, bf16[272,1024]{1,0:T(8,128)(2,1)}) custom-call(s32[1]{0:T(128)} %bitcast.i_ref, bf16[128,1024]{1,0:T(8,128)(2,1)S(1)} %copy-done, bf16[128,1024]{1,0:T(8,128)(2,1)S(1)} %copy-done.1, bf16[128,1024]{1,0:T(8,128)(2,1)S(1)} %copy-done.2, bf16[128,1024]{1,0:T(8,128)(2,1)S(1)} %copy-done.3, ...), custom_call_target="tpu_custom_call" | custom-call | bytes 4194304 | tf_op jit(solution)/shard_map/near_payload/pallas_call | solution.py:428
  15.8 3.3 %collective-permute-start.1 = (bf16[272,1024]{1,0:T(8,128)(2,1)}, bf16[272,1024]{1,0:T(8,128)(2,1)S(1)}, u32[]{:S(2)}, u32[]{:S(2)}) collective-permute-start(bf16[272,1024]{1,0:T(8,128)(2,1)} %get-tuple-element.14), channel_id=1, source_target_pairs={{0,2},{1,3},{2,0},{3,1},{4,6},{5,7},{6,4},{7,5},{8,10},{9,11},{10,... | collective-permute-start | bytes 1671176 | tf_op jit(solution)/shard_map/ppermute | solution.py:410
  19.1 1.8 %all-to-all-done.r_ref = bf16[8,144,128]{2,1,0:T(8,128)(2,1)S(1)} async-done(((bf16[8,144,128]{2,1,0:T(8,128)(2,1)}), bf16[8,144,128]{2,1,0:T(8,128)(2,1)S(1)}, u32[]{:S(2)}, u32[]{:S(2)}) %all-to-all-start) | async-done | bytes 294944 | tf_op jit(solution)/shard_map/all_to_all | solution.py:406
  21.0 0.8 %middle_rows.1 = (bf16[16,40,128]{2,1,0:T(8,128)(2,1)}, bf16[40,128]{1,0:T(8,128)(2,1)S(1)}, bf16[544,128]{1,0:T(8,128)(2,1)S(1)}) custom-call(s32[1]{0:T(128)} %bitcast.i_ref, bf16[8,144,128]{2,1,0:T(8,128)(2,1)S(1)} %all-to-all-done.r_ref), custom_call_target="tpu_custom_call" | custom-call | bytes 1048576 | tf_op jit(solution)/shard_map/middle_rows/pallas_call | solution.py:438
  21.7 10.5 %all-to-all-start.1 = ((bf16[16,40,128]{2,1,0:T(8,128)(2,1)}), bf16[16,40,128]{2,1,0:T(8,128)(2,1)S(1)}, u32[]{:S(2)}, u32[]{:S(2)}) async-start(bf16[16,40,128]{2,1,0:T(8,128)(2,1)} %get-tuple-element.11), calls=%async_computation.1 | async-start | bytes 327680 | tf_op jit(solution)/shard_map/all_to_all | solution.py:406
  32.2 3.3 %collective-permute-start = (bf16[544,128]{1,0:T(8,128)(2,1)S(1)}, bf16[544,128]{1,0:T(8,128)(2,1)S(1)}, u32[]{:S(2)}, u32[]{:S(2)}) collective-permute-start(bf16[544,128]{1,0:T(8,128)(2,1)S(1)} %get-tuple-element.12), channel_id=1, source_target_pairs={{0,8},{1,9},{2,10},{3,11},{4,12},{5,13},{6,14},{7,15},{8,0},{9,1},... | collective-permute-start | bytes 417800 | tf_op jit(solution)/shard_map/ppermute | solution.py:410
  35.5 3.8 %collective-permute-start.2 = (bf16[272,1024]{1,0:T(8,128)(2,1)}, bf16[272,1024]{1,0:T(8,128)(2,1)}, u32[]{:S(2)}, u32[]{:S(2)}) collective-permute-start(bf16[272,1024]{1,0:T(8,128)(2,1)} %get-tuple-element.16), channel_id=1, source_target_pairs={{0,1},{1,0},{2,3},{3,2},{4,5},{5,4},{6,7},{7,6},{8,9},{9,8},{10,11... | collective-permute-start | bytes 1671176 | tf_op jit(solution)/shard_map/ppermute | solution.py:410
  39.3 2.1 %collective-permute-start.3 = (bf16[272,1024]{1,0:T(8,128)(2,1)}, bf16[272,1024]{1,0:T(8,128)(2,1)}, u32[]{:S(2)}, u32[]{:S(2)}) collective-permute-start(bf16[272,1024]{1,0:T(8,128)(2,1)} %get-tuple-element.14), channel_id=1, source_target_pairs={{0,3},{1,2},{2,1},{3,0},{4,7},{5,6},{6,5},{7,4},{8,11},{9,10},{10,... | collective-permute-start | bytes 1671176 | tf_op jit(solution)/shard_map/ppermute | solution.py:410
  41.4 2.7 %collective-permute-done.x_ref = bf16[544,128]{1,0:T(8,128)(2,1)S(1)} collective-permute-done((bf16[544,128]{1,0:T(8,128)(2,1)S(1)}, bf16[544,128]{1,0:T(8,128)(2,1)S(1)}, u32[]{:S(2)}, u32[]{:S(2)}) %collective-permute-start) | collective-permute-done | bytes 139296 | tf_op jit(solution)/shard_map/ppermute | solution.py:410
  44.2 0.0 collective-permute-done.1.after.r2
  44.2 0.9 %pair_grads.1.after_pair.n_ref = f32[8,96,128]{2,1,0:T(8,128)S(1)} custom-call(s32[1]{0:T(128)} %bitcast.i_ref, bf16[8,144,128]{2,1,0:T(8,128)(2,1)S(1)} %all-to-all-done.r_ref, bf16[544,128]{1,0:T(8,128)(2,1)S(1)} %collective-permute-done.x_ref, bf16[272,1024]{1,0:T(8,128)(2,1)S(1)} %collective-permute-done.1.after.r2), custom_call_target="tpu_custom_call" | custom-call | flops 3355443200 | bytes 1048576 | tf_op jit(solution)/shard_map/pair_grads/pallas_call | solution.py:448
  45.1 0.0 all-to-all-done.1.r_ref
  45.1 0.8 %plane_rows.1.after = bf16[4,272,128]{2,1,0:T(8,128)(2,1)} custom-call(s32[1]{0:T(128)} %bitcast.i_ref, bf16[16,40,128]{2,1,0:T(8,128)(2,1)S(1)} %all-to-all-done.1.r_ref, f32[8,96,128]{2,1,0:T(8,128)S(1)} %pair_grads.1.after_pair.n_ref), custom_call_target="tpu_custom_call" | custom-call | bytes 1048576 | tf_op jit(solution)/shard_map/plane_rows/pallas_call | solution.py:456
  45.9 4.2 %all-to-all-start.2 = ((bf16[4,272,128]{2,1,0:T(8,128)(2,1)}), bf16[4,272,128]{2,1,0:T(8,128)(2,1)S(1)}, u32[]{:S(2)}, u32[]{:S(2)}) async-start(bf16[4,272,128]{2,1,0:T(8,128)(2,1)} %plane_rows.1.after), calls=%async_computation.2 | async-start | bytes 557056 | tf_op jit(solution)/shard_map/all_to_all | solution.py:406
  50.1 0.0 collective-permute-done.2.r1
  50.1 5.7 %collective-permute-done.3.r3 = bf16[272,1024]{1,0:T(8,128)(2,1)} collective-permute-done((bf16[272,1024]{1,0:T(8,128)(2,1)}, bf16[272,1024]{1,0:T(8,128)(2,1)}, u32[]{:S(2)}, u32[]{:S(2)}) %collective-permute-start.3) | collective-permute-done | bytes 557088 | tf_op jit(solution)/shard_map/ppermute | solution.py:410
  55.8 4.5 %near_grads.1.after.n_ref = bf16[3,128,1024]{2,1,0:T(8,128)(2,1)S(1)} custom-call(s32[1]{0:T(128)} %bitcast.i_ref, bf16[128,1024]{1,0:T(8,128)(2,1)S(1)} %copy-done, bf16[128,1024]{1,0:T(8,128)(2,1)S(1)} %copy-done.1, bf16[128,1024]{1,0:T(8,128)(2,1)S(1)} %copy-done.2, bf16[128,1024]{1,0:T(8,128)(2,1)S(1)} %copy-done.3, bf16[16,1024]{1,0:T(8,128)(2,1)S(1)} %copy-done.4, ...), custom_call_target="tpu_custom_call" | custom-call | flops 570425344 | bytes 4194304 | tf_op jit(solution)/shard_map/near_grads/pallas_call | solution.py:463
  60.3 0.0 all-to-all-done.2.f_ref
  60.4 0.4 join_grads.1
  60.7 9.1 %all_to_all.20.r_ref = bf16[8,96,128]{2,1,0:T(8,128)(2,1)S(1)} all-to-all(bf16[8,96,128]{2,1,0:T(8,128)(2,1)S(1)} %join_grads.1), channel_id=1, replica_groups={{0,1,2,3,4,5,6,7},{8,9,10,11,12,13,14,15},{16,17,18,19,20,21,22,23},{24..., dimensions={0} | all-to-all | bytes 393216 | tf_op jit(solution)/shard_map/all_to_all | solution.py:406
  69.8 1.1 %add_levels.1 = (bf16[128,1024]{1,0:T(8,128)(2,1)}, bf16[128,1024]{1,0:T(8,128)(2,1)}, bf16[128,1024]{1,0:T(8,128)(2,1)}) custom-call(bf16[8,96,128]{2,1,0:T(8,128)(2,1)S(1)} %all_to_all.20.r_ref, bf16[3,128,1024]{2,1,0:T(8,128)(2,1)S(1)} %near_grads.1.after.n_ref), custom_call_target="tpu_custom_call" | custom-call | flops 25165824 | bytes 4194304 | tf_op jit(solution)/shard_map/add_levels/pallas_call | solution.py:482
Async XLA Ops:
  0.6 13.5 %copy-start.2 = (bf16[128,1024]{1,0:T(8,128)(2,1)S(1)}, bf16[128,1024]{1,0:T(8,128)(2,1)}, u32[]{:S(2)}) copy-start(bf16[128,1024]{1,0:T(8,128)(2,1)} %v.1) | copy-start | bytes 786436
  0.6 13.5 %copy-start.3 = (bf16[128,1024]{1,0:T(8,128)(2,1)S(1)}, bf16[128,1024]{1,0:T(8,128)(2,1)}, u32[]{:S(2)}) copy-start(bf16[128,1024]{1,0:T(8,128)(2,1)} %g.1) | copy-start | bytes 786436
  3.7 10.4 %copy-start = (bf16[128,1024]{1,0:T(8,128)(2,1)S(1)}, bf16[128,1024]{1,0:T(8,128)(2,1)}, u32[]{:S(2)}) copy-start(bf16[128,1024]{1,0:T(8,128)(2,1)} %q.1) | copy-start | bytes 786436
  3.8 10.4 %copy-start.1 = (bf16[128,1024]{1,0:T(8,128)(2,1)S(1)}, bf16[128,1024]{1,0:T(8,128)(2,1)}, u32[]{:S(2)}) copy-start(bf16[128,1024]{1,0:T(8,128)(2,1)} %k.1) | copy-start | bytes 786436
  3.8 10.4 %copy-start.4 = (bf16[16,1024]{1,0:T(8,128)(2,1)S(1)}, bf16[16,1024]{1,0:T(8,128)(2,1)}, u32[]{:S(2)}) copy-start(bf16[16,1024]{1,0:T(8,128)(2,1)} %get-tuple-element.13.s_in.s) | copy-start | bytes 98308
  3.8 17.2 %all-to-all-start = ((bf16[8,144,128]{2,1,0:T(8,128)(2,1)}), bf16[8,144,128]{2,1,0:T(8,128)(2,1)S(1)}, u32[]{:S(2)}, u32[]{:S(2)}) async-start(bf16[8,144,128]{2,1,0:T(8,128)(2,1)} %get-tuple-element.10), calls=%async_computation | async-start | bytes 589824 | tf_op jit(solution)/shard_map/all_to_all | solution.py:406
  15.8 28.3 %collective-permute-start.1 = (bf16[272,1024]{1,0:T(8,128)(2,1)}, bf16[272,1024]{1,0:T(8,128)(2,1)S(1)}, u32[]{:S(2)}, u32[]{:S(2)}) collective-permute-start(bf16[272,1024]{1,0:T(8,128)(2,1)} %get-tuple-element.14), channel_id=1, source_target_pairs={{0,2},{1,3},{2,0},{3,1},{4,6},{5,7},{6,4},{7,5},{8,10},{9,11},{10,... | collective-permute-start | bytes 1671176 | tf_op jit(solution)/shard_map/ppermute | solution.py:410
  21.7 23.4 %all-to-all-start.1 = ((bf16[16,40,128]{2,1,0:T(8,128)(2,1)}), bf16[16,40,128]{2,1,0:T(8,128)(2,1)S(1)}, u32[]{:S(2)}, u32[]{:S(2)}) async-start(bf16[16,40,128]{2,1,0:T(8,128)(2,1)} %get-tuple-element.11), calls=%async_computation.1 | async-start | bytes 327680 | tf_op jit(solution)/shard_map/all_to_all | solution.py:406
  32.2 11.9 %collective-permute-start = (bf16[544,128]{1,0:T(8,128)(2,1)S(1)}, bf16[544,128]{1,0:T(8,128)(2,1)S(1)}, u32[]{:S(2)}, u32[]{:S(2)}) collective-permute-start(bf16[544,128]{1,0:T(8,128)(2,1)S(1)} %get-tuple-element.12), channel_id=1, source_target_pairs={{0,8},{1,9},{2,10},{3,11},{4,12},{5,13},{6,14},{7,15},{8,0},{9,1},... | collective-permute-start | bytes 417800 | tf_op jit(solution)/shard_map/ppermute | solution.py:410
  35.5 14.6 %collective-permute-start.2 = (bf16[272,1024]{1,0:T(8,128)(2,1)}, bf16[272,1024]{1,0:T(8,128)(2,1)}, u32[]{:S(2)}, u32[]{:S(2)}) collective-permute-start(bf16[272,1024]{1,0:T(8,128)(2,1)} %get-tuple-element.16), channel_id=1, source_target_pairs={{0,1},{1,0},{2,3},{3,2},{4,5},{5,4},{6,7},{7,6},{8,9},{9,8},{10,11... | collective-permute-start | bytes 1671176 | tf_op jit(solution)/shard_map/ppermute | solution.py:410
  39.3 16.5 %collective-permute-start.3 = (bf16[272,1024]{1,0:T(8,128)(2,1)}, bf16[272,1024]{1,0:T(8,128)(2,1)}, u32[]{:S(2)}, u32[]{:S(2)}) collective-permute-start(bf16[272,1024]{1,0:T(8,128)(2,1)} %get-tuple-element.14), channel_id=1, source_target_pairs={{0,3},{1,2},{2,1},{3,0},{4,7},{5,6},{6,5},{7,4},{8,11},{9,10},{10,... | collective-permute-start | bytes 1671176 | tf_op jit(solution)/shard_map/ppermute | solution.py:410
  45.9 14.4 %all-to-all-start.2 = ((bf16[4,272,128]{2,1,0:T(8,128)(2,1)}), bf16[4,272,128]{2,1,0:T(8,128)(2,1)S(1)}, u32[]{:S(2)}, u32[]{:S(2)}) async-start(bf16[4,272,128]{2,1,0:T(8,128)(2,1)} %plane_rows.1.after), calls=%async_computation.2 | async-start | bytes 557056 | tf_op jit(solution)/shard_map/all_to_all | solution.py:406

commit v7 on v5

--- a/solution.py
+++ b/solution.py
@@ -449,7 +449,7 @@
         "pair_grads",
         shape((RING, OUT_CHUNK, WIDTH), F32),
         [SMEM, VMEM, VMEM, ANY],
-        flops=20 * 2 * 10 * 128 * 256 * 256,
+        flops=8 * 2 * 10 * 128 * 256 * 256,
         moved=1 << 20,
     )(index, side, pair, chip)
     plane = call(

time: 71.6 us -> 71.1 us (level)
  waiting for transfers between devices: 10.3 us -> 7.76 us
  blocking collectives: 9.11 us -> 11.5 us
    ppermute x4, waiting for transfers between devices: 8.45 us -> 4.91 us  [partner(): return lax.ppermute(array, 'seq', [(i, i ^ bit) for i in range(DEVICES)])]
    all_to_all x1, blocking collectives: 9.11 us -> 11.5 us  [exchange(): lax.all_to_all(array, 'seq', 0, 0, axis_index_groups=groups, tiled=True)]
    all_to_all x3, waiting for transfers between devices: 1.82 us -> 2.85 us  [exchange(): lax.all_to_all(array, 'seq', 0, 0, axis_index_groups=groups, tiled=True)]
where the time goes in v7:
time: 71.1 us; the launch traced here: 70.6 us
  starting transfers between devices  37.2 us (52%)
  Pallas kernels  13.3 us (19%)
  blocking collectives  11.5 us (16%)
  waiting for transfers between devices  7.76 us (11%)
  between operations  0.8 us (1%)
    all_to_all x3, starting transfers between devices, exchange(): lax.all_to_all(array, 'seq', 0, 0, axis_index_groups=groups, tiled=True)  25 us
    ppermute x4, starting transfers between devices, partner(): return lax.ppermute(array, 'seq', [(i, i ^ bit) for i in range(DEVICES)])  12.2 us
    all_to_all x1, blocking collectives, exchange(): lax.all_to_all(array, 'seq', 0, 0, axis_index_groups=groups, tiled=True)  11.5 us
    ppermute x4, waiting for transfers between devices, partner(): return lax.ppermute(array, 'seq', [(i, i ^ bit) for i in range(DEVICES)])  4.91 us
    pallas_call x1, Pallas kernels, body(): call(near_kernel, 'near_grads', shape((3, TOK, HEADS * WIDTH)), [SMEM] +...  4.54 us
    pallas_call x1, Pallas kernels, body(): call(select_kernel, 'select_rows', (shape((HEADS, CHUNK, WIDTH)), shape((...  3.14 us
    all_to_all x3, waiting for transfers between devices, exchange(): lax.all_to_all(array, 'seq', 0, 0, axis_index_groups=groups, tiled=True)  2.85 us
    pallas_call x1, Pallas kernels, body(): call(payload_kernel, 'near_payload', (shape((NEAR, HEADS * WIDTH)), shape...  1.66 us
  transfers between devices with their start and end apart: 7, of which 3 were waited for; matrix products, arithmetic and copies ran while one was open for 0% of the time, Pallas kernels for 12%

profile of v7, /device:TPU:1, one launch (start us, length us, event | category | flops | bytes accessed | tf_op | source)
XLA Modules:
  0.0 70.6 jit_solution(4218969409257995613)
XLA Ops:
  0.6 0.0 copy-start.2
  0.6 0.0 copy-start.3
  0.7 3.1 %select_rows.1 = (bf16[8,144,128]{2,1,0:T(8,128)(2,1)}, bf16[16,1024]{1,0:T(8,128)(2,1)}) custom-call(s32[1]{0:T(128)} %bitcast.i_ref, bf16[128,1024]{1,0:T(8,128)(2,1)} %q.1, bf16[128,1024]{1,0:T(8,128)(2,1)} %k.1, bf16[128,1024]{1,0:T(8,128)(2,1)} %v.1, bf16[128,1024]{1,0:T(8,128)(2,1)} %g.1, bf16[128,1024]{1,0:T(8,128)(2,1)} %o_in.1, f32[8,128]{1,0:T(8,128)} %n_in.1), custom_call_target="tpu_custom_call" | custom-call | flops 134217728 | bytes 3145728 | tf_op jit(solution)/shard_map/select_rows/pallas_call | solution.py:415
  3.8 0.0 copy-start
  3.8 0.0 copy-start.1
  3.8 0.0 copy-start.4
  3.8 10.3 %all-to-all-start = ((bf16[8,144,128]{2,1,0:T(8,128)(2,1)}), bf16[8,144,128]{2,1,0:T(8,128)(2,1)S(1)}, u32[]{:S(2)}, u32[]{:S(2)}) async-start(bf16[8,144,128]{2,1,0:T(8,128)(2,1)} %get-tuple-element.10), calls=%async_computation | async-start | bytes 589824 | tf_op jit(solution)/shard_map/all_to_all | solution.py:405
  14.2 0.0 copy-done.2
  14.2 0.0 copy-done.3
  14.2 0.0 copy-done
  14.2 0.0 copy-done.1
  14.2 0.0 copy-done.4
  14.2 1.7 %near_payload.1 = (bf16[272,1024]{1,0:T(8,128)(2,1)}, bf16[272,1024]{1,0:T(8,128)(2,1)}) custom-call(s32[1]{0:T(128)} %bitcast.i_ref, bf16[128,1024]{1,0:T(8,128)(2,1)S(1)} %copy-done, bf16[128,1024]{1,0:T(8,128)(2,1)S(1)} %copy-done.1, bf16[128,1024]{1,0:T(8,128)(2,1)S(1)} %copy-done.2, bf16[128,1024]{1,0:T(8,128)(2,1)S(1)} %copy-done.3, ...), custom_call_target="tpu_custom_call" | custom-call | bytes 4194304 | tf_op jit(solution)/shard_map/near_payload/pallas_call | solution.py:427
  15.9 3.3 %collective-permute-start.1 = (bf16[272,1024]{1,0:T(8,128)(2,1)}, bf16[272,1024]{1,0:T(8,128)(2,1)S(1)}, u32[]{:S(2)}, u32[]{:S(2)}) collective-permute-start(bf16[272,1024]{1,0:T(8,128)(2,1)} %get-tuple-element.14), channel_id=1, source_target_pairs={{0,2},{1,3},{2,0},{3,1},{4,6},{5,7},{6,4},{7,5},{8,10},{9,11},{10,... | collective-permute-start | bytes 1671176 | tf_op jit(solution)/shard_map/ppermute | solution.py:409
  19.2 1.8 %all-to-all-done.r_ref = bf16[8,144,128]{2,1,0:T(8,128)(2,1)S(1)} async-done(((bf16[8,144,128]{2,1,0:T(8,128)(2,1)}), bf16[8,144,128]{2,1,0:T(8,128)(2,1)S(1)}, u32[]{:S(2)}, u32[]{:S(2)}) %all-to-all-start) | async-done | bytes 294944 | tf_op jit(solution)/shard_map/all_to_all | solution.py:405
  21.0 0.8 %middle_rows.1 = (bf16[16,40,128]{2,1,0:T(8,128)(2,1)}, bf16[40,128]{1,0:T(8,128)(2,1)S(1)}, bf16[544,128]{1,0:T(8,128)(2,1)S(1)}) custom-call(s32[1]{0:T(128)} %bitcast.i_ref, bf16[8,144,128]{2,1,0:T(8,128)(2,1)S(1)} %all-to-all-done.r_ref), custom_call_target="tpu_custom_call" | custom-call | bytes 1048576 | tf_op jit(solution)/shard_map/middle_rows/pallas_call | solution.py:437
  21.8 10.5 %all-to-all-start.1 = ((bf16[16,40,128]{2,1,0:T(8,128)(2,1)}), bf16[16,40,128]{2,1,0:T(8,128)(2,1)S(1)}, u32[]{:S(2)}, u32[]{:S(2)}) async-start(bf16[16,40,128]{2,1,0:T(8,128)(2,1)} %get-tuple-element.11), calls=%async_computation.1 | async-start | bytes 327680 | tf_op jit(solution)/shard_map/all_to_all | solution.py:405
  32.3 3.3 %collective-permute-start.2 = (bf16[272,1024]{1,0:T(8,128)(2,1)}, bf16[272,1024]{1,0:T(8,128)(2,1)}, u32[]{:S(2)}, u32[]{:S(2)}) collective-permute-start(bf16[272,1024]{1,0:T(8,128)(2,1)} %get-tuple-element.16), channel_id=1, source_target_pairs={{0,1},{1,0},{2,3},{3,2},{4,5},{5,4},{6,7},{7,6},{8,9},{9,8},{10,11... | collective-permute-start | bytes 1671176 | tf_op jit(solution)/shard_map/ppermute | solution.py:409
  35.6 2.1 %collective-permute-start.3 = (bf16[272,1024]{1,0:T(8,128)(2,1)}, bf16[272,1024]{1,0:T(8,128)(2,1)}, u32[]{:S(2)}, u32[]{:S(2)}) collective-permute-start(bf16[272,1024]{1,0:T(8,128)(2,1)} %get-tuple-element.14), channel_id=1, source_target_pairs={{0,3},{1,2},{2,1},{3,0},{4,7},{5,6},{6,5},{7,4},{8,11},{9,10},{10,... | collective-permute-start | bytes 1671176 | tf_op jit(solution)/shard_map/ppermute | solution.py:409
  37.7 3.5 %collective-permute-start = (bf16[544,128]{1,0:T(8,128)(2,1)S(1)}, bf16[544,128]{1,0:T(8,128)(2,1)S(1)}, u32[]{:S(2)}, u32[]{:S(2)}) collective-permute-start(bf16[544,128]{1,0:T(8,128)(2,1)S(1)} %get-tuple-element.12), channel_id=1, source_target_pairs={{0,8},{1,9},{2,10},{3,11},{4,12},{5,13},{6,14},{7,15},{8,0},{9,1},... | collective-permute-start | bytes 417800 | tf_op jit(solution)/shard_map/ppermute | solution.py:409
  41.2 4.9 %collective-permute-done.x_ref = bf16[544,128]{1,0:T(8,128)(2,1)S(1)} collective-permute-done((bf16[544,128]{1,0:T(8,128)(2,1)S(1)}, bf16[544,128]{1,0:T(8,128)(2,1)S(1)}, u32[]{:S(2)}, u32[]{:S(2)}) %collective-permute-start) | collective-permute-done | bytes 139296 | tf_op jit(solution)/shard_map/ppermute | solution.py:409
  46.1 0.0 collective-permute-done.1.after.r2
  46.1 0.9 %pair_grads.1.after_pair.n_ref = f32[8,96,128]{2,1,0:T(8,128)S(1)} custom-call(s32[1]{0:T(128)} %bitcast.i_ref, bf16[8,144,128]{2,1,0:T(8,128)(2,1)S(1)} %all-to-all-done.r_ref, bf16[544,128]{1,0:T(8,128)(2,1)S(1)} %collective-permute-done.x_ref, bf16[272,1024]{1,0:T(8,128)(2,1)S(1)} %collective-permute-done.1.after.r2), custom_call_target="tpu_custom_call" | custom-call | flops 1342177280 | bytes 1048576 | tf_op jit(solution)/shard_map/pair_grads/pallas_call | solution.py:447
  47.0 0.0 all-to-all-done.1.r_ref
  47.0 0.8 %plane_rows.1.after = bf16[4,272,128]{2,1,0:T(8,128)(2,1)} custom-call(s32[1]{0:T(128)} %bitcast.i_ref, bf16[16,40,128]{2,1,0:T(8,128)(2,1)S(1)} %all-to-all-done.1.r_ref, f32[8,96,128]{2,1,0:T(8,128)S(1)} %pair_grads.1.after_pair.n_ref), custom_call_target="tpu_custom_call" | custom-call | bytes 1048576 | tf_op jit(solution)/shard_map/plane_rows/pallas_call | solution.py:455
  47.8 4.2 %all-to-all-start.2 = ((bf16[4,272,128]{2,1,0:T(8,128)(2,1)}), bf16[4,272,128]{2,1,0:T(8,128)(2,1)S(1)}, u32[]{:S(2)}, u32[]{:S(2)}) async-start(bf16[4,272,128]{2,1,0:T(8,128)(2,1)} %plane_rows.1.after), calls=%async_computation.2 | async-start | bytes 557056 | tf_op jit(solution)/shard_map/all_to_all | solution.py:405
  52.0 0.0 collective-permute-done.2.r1
  52.0 0.0 collective-permute-done.3.r3
  52.0 4.5 %near_grads.1.after.n_ref = bf16[3,128,1024]{2,1,0:T(8,128)(2,1)S(1)} custom-call(s32[1]{0:T(128)} %bitcast.i_ref, bf16[128,1024]{1,0:T(8,128)(2,1)S(1)} %copy-done, bf16[128,1024]{1,0:T(8,128)(2,1)S(1)} %copy-done.1, bf16[128,1024]{1,0:T(8,128)(2,1)S(1)} %copy-done.2, bf16[128,1024]{1,0:T(8,128)(2,1)S(1)} %copy-done.3, bf16[16,1024]{1,0:T(8,128)(2,1)S(1)} %copy-done.4, ...), custom_call_target="tpu_custom_call" | custom-call | flops 570425344 | bytes 4194304 | tf_op jit(solution)/shard_map/near_grads/pallas_call | solution.py:462
  56.6 1.0 %all-to-all-done.2.f_ref = bf16[4,272,128]{2,1,0:T(8,128)(2,1)S(1)} async-done(((bf16[4,272,128]{2,1,0:T(8,128)(2,1)}), bf16[4,272,128]{2,1,0:T(8,128)(2,1)S(1)}, u32[]{:S(2)}, u32[]{:S(2)}) %all-to-all-start.2) | async-done | bytes 278560 | tf_op jit(solution)/shard_map/all_to_all | solution.py:405
  57.6 0.4 join_grads.1
  58.0 11.5 %all_to_all.20.r_ref = bf16[8,96,128]{2,1,0:T(8,128)(2,1)S(1)} all-to-all(bf16[8,96,128]{2,1,0:T(8,128)(2,1)S(1)} %join_grads.1), channel_id=1, replica_groups={{0,1,2,3,4,5,6,7},{8,9,10,11,12,13,14,15},{16,17,18,19,20,21,22,23},{24..., dimensions={0} | all-to-all | bytes 393216 | tf_op jit(solution)/shard_map/all_to_all | solution.py:405
  69.5 1.1 %add_levels.1 = (bf16[128,1024]{1,0:T(8,128)(2,1)}, bf16[128,1024]{1,0:T(8,128)(2,1)}, bf16[128,1024]{1,0:T(8,128)(2,1)}) custom-call(bf16[8,96,128]{2,1,0:T(8,128)(2,1)S(1)} %all_to_all.20.r_ref, bf16[3,128,1024]{2,1,0:T(8,128)(2,1)S(1)} %near_grads.1.after.n_ref), custom_call_target="tpu_custom_call" | custom-call | flops 25165824 | bytes 4194304 | tf_op jit(solution)/shard_map/add_levels/pallas_call | solution.py:481
Async XLA Ops:
  0.6 13.6 %copy-start.2 = (bf16[128,1024]{1,0:T(8,128)(2,1)S(1)}, bf16[128,1024]{1,0:T(8,128)(2,1)}, u32[]{:S(2)}) copy-start(bf16[128,1024]{1,0:T(8,128)(2,1)} %v.1) | copy-start | bytes 786436
  0.6 13.5 %copy-start.3 = (bf16[128,1024]{1,0:T(8,128)(2,1)S(1)}, bf16[128,1024]{1,0:T(8,128)(2,1)}, u32[]{:S(2)}) copy-start(bf16[128,1024]{1,0:T(8,128)(2,1)} %g.1) | copy-start | bytes 786436
  3.8 10.4 %copy-start = (bf16[128,1024]{1,0:T(8,128)(2,1)S(1)}, bf16[128,1024]{1,0:T(8,128)(2,1)}, u32[]{:S(2)}) copy-start(bf16[128,1024]{1,0:T(8,128)(2,1)} %q.1) | copy-start | bytes 786436
  3.8 10.4 %copy-start.1 = (bf16[128,1024]{1,0:T(8,128)(2,1)S(1)}, bf16[128,1024]{1,0:T(8,128)(2,1)}, u32[]{:S(2)}) copy-start(bf16[128,1024]{1,0:T(8,128)(2,1)} %k.1) | copy-start | bytes 786436
  3.8 10.4 %copy-start.4 = (bf16[16,1024]{1,0:T(8,128)(2,1)S(1)}, bf16[16,1024]{1,0:T(8,128)(2,1)}, u32[]{:S(2)}) copy-start(bf16[16,1024]{1,0:T(8,128)(2,1)} %get-tuple-element.13.s_in.s) | copy-start | bytes 98308
  3.8 17.2 %all-to-all-start = ((bf16[8,144,128]{2,1,0:T(8,128)(2,1)}), bf16[8,144,128]{2,1,0:T(8,128)(2,1)S(1)}, u32[]{:S(2)}, u32[]{:S(2)}) async-start(bf16[8,144,128]{2,1,0:T(8,128)(2,1)} %get-tuple-element.10), calls=%async_computation | async-start | bytes 589824 | tf_op jit(solution)/shard_map/all_to_all | solution.py:405
  15.9 30.2 %collective-permute-start.1 = (bf16[272,1024]{1,0:T(8,128)(2,1)}, bf16[272,1024]{1,0:T(8,128)(2,1)S(1)}, u32[]{:S(2)}, u32[]{:S(2)}) collective-permute-start(bf16[272,1024]{1,0:T(8,128)(2,1)} %get-tuple-element.14), channel_id=1, source_target_pairs={{0,2},{1,3},{2,0},{3,1},{4,6},{5,7},{6,4},{7,5},{8,10},{9,11},{10,... | collective-permute-start | bytes 1671176 | tf_op jit(solution)/shard_map/ppermute | solution.py:409
  21.8 25.2 %all-to-all-start.1 = ((bf16[16,40,128]{2,1,0:T(8,128)(2,1)}), bf16[16,40,128]{2,1,0:T(8,128)(2,1)S(1)}, u32[]{:S(2)}, u32[]{:S(2)}) async-start(bf16[16,40,128]{2,1,0:T(8,128)(2,1)} %get-tuple-element.11), calls=%async_computation.1 | async-start | bytes 327680 | tf_op jit(solution)/shard_map/all_to_all | solution.py:405
  32.3 19.7 %collective-permute-start.2 = (bf16[272,1024]{1,0:T(8,128)(2,1)}, bf16[272,1024]{1,0:T(8,128)(2,1)}, u32[]{:S(2)}, u32[]{:S(2)}) collective-permute-start(bf16[272,1024]{1,0:T(8,128)(2,1)} %get-tuple-element.16), channel_id=1, source_target_pairs={{0,1},{1,0},{2,3},{3,2},{4,5},{5,4},{6,7},{7,6},{8,9},{9,8},{10,11... | collective-permute-start | bytes 1671176 | tf_op jit(solution)/shard_map/ppermute | solution.py:409
  35.6 16.5 %collective-permute-start.3 = (bf16[272,1024]{1,0:T(8,128)(2,1)}, bf16[272,1024]{1,0:T(8,128)(2,1)}, u32[]{:S(2)}, u32[]{:S(2)}) collective-permute-start(bf16[272,1024]{1,0:T(8,128)(2,1)} %get-tuple-element.14), channel_id=1, source_target_pairs={{0,3},{1,2},{2,1},{3,0},{4,7},{5,6},{6,5},{7,4},{8,11},{9,10},{10,... | collective-permute-start | bytes 1671176 | tf_op jit(solution)/shard_map/ppermute | solution.py:409
  37.7 8.4 %collective-permute-start = (bf16[544,128]{1,0:T(8,128)(2,1)S(1)}, bf16[544,128]{1,0:T(8,128)(2,1)S(1)}, u32[]{:S(2)}, u32[]{:S(2)}) collective-permute-start(bf16[544,128]{1,0:T(8,128)(2,1)S(1)} %get-tuple-element.12), channel_id=1, source_target_pairs={{0,8},{1,9},{2,10},{3,11},{4,12},{5,13},{6,14},{7,15},{8,0},{9,1},... | collective-permute-start | bytes 417800 | tf_op jit(solution)/shard_map/ppermute | solution.py:409
  47.8 9.8 %all-to-all-start.2 = ((bf16[4,272,128]{2,1,0:T(8,128)(2,1)}), bf16[4,272,128]{2,1,0:T(8,128)(2,1)S(1)}, u32[]{:S(2)}, u32[]{:S(2)}) async-start(bf16[4,272,128]{2,1,0:T(8,128)(2,1)} %plane_rows.1.after), calls=%async_computation.2 | async-start | bytes 557056 | tf_op jit(solution)/shard_map/all_to_all | solution.py:405
